TPU v7x, 32 devices: a whole 2x2x4 slice. The times are simulated.
32 devices in a mesh: dp: 8 (over z, y), node: 4 (over x, core).
Axes of the slice: x: 2, y: 2, z: 4, core: 2. Of those that a mesh axis runs over, the one named last changes fastest.
Arguments:
- tokens_in: bfloat16 [8192, 4096], P('dp', 'node'), may hold values from -6 to 6
- out_grads: bfloat16 [8192, 4096], P('dp'), may hold values from -0.01171875 to 0.01171875
- left_old: float32 [4096, 4096], P('node', 'dp'), may hold values from -0.1 to 4.1, as said below
- right_old: float32 [4096, 4096], P('node', 'dp'), may hold values from -0.1 to 4.1, as said below
Outputs:
- left_out: float32 [4096, 4096], P('node', 'dp')
- right_out: float32 [4096, 4096], P('node', 'dp')
Inputs may be any that keep to these rules, and one draw needn't show every extreme that they name: `left_old`: symmetric. `right_old`: symmetric.
All inputs are finite; a program needn't handle non-finite values.
Results may differ from a plain program's by a relative error of at most 0.0021.
Values may be sent and summed in bfloat16 or wider, within the bound.
No kernel may reach another device: no remote copies, remote signals or barrier semaphores. Data moves between devices by JAX's collectives and lax.ppermute only.
A program may use at most 128 MiB of HBM per device.

v0:
```python
import jax
import jax.numpy as jnp
from jax import lax
from jax.sharding import PartitionSpec as P

ema_decay = 0.95


def from_root(value, axis, source):
    kept = jnp.where(lax.axis_index(axis) == source, value, 0).astype(value.dtype)
    return lax.psum(kept, axis)


def contract_first(left, right):
    return lax.dot_general(
        left, right, (((0,), (0,)), ((), ())), preferred_element_type=jnp.float32
    )


def contract_last(left, right):
    return lax.dot_general(
        left, right, (((1,), (1,)), ((), ())), preferred_element_type=jnp.float32
    )


def shards(tokens_in, out_grads, left_old, right_old):
    group_ratio = lax.axis_size("dp") // lax.axis_size("node")
    dp_index = lax.axis_index("dp")
    slab_width = left_old.shape[1]
    summed = lax.psum(contract_first(out_grads, tokens_in), "dp")
    row_panel = summed.astype(jnp.bfloat16)
    own_tile = lax.dynamic_slice_in_dim(row_panel, dp_index * slab_width, slab_width, 0)
    crossed = lax.all_to_all(row_panel, "node", split_axis=0, concat_axis=1, tiled=True)
    right_new = contract_last(crossed, lax.all_gather(own_tile, "node", axis=1, tiled=True))
    local_rows = lax.dynamic_slice_in_dim(
        row_panel, dp_index % group_ratio * slab_width, slab_width, 1
    )
    row_slab = from_root(local_rows, "node", dp_index // group_ratio)
    left_new = contract_first(row_panel, row_slab)
    left_out = ema_decay * left_old + (1.0 - ema_decay) * left_new
    right_out = ema_decay * right_old + (1.0 - ema_decay) * right_new
    return (left_out, right_out)


def solution(mesh):
    placed = (P("dp", "node"), P("dp", None), P("node", "dp"), P("node", "dp"))
    return jax.shard_map(
        shards,
        mesh=mesh,
        in_specs=placed,
        out_specs=(P("node", "dp"), P("node", "dp")),
        check_vma=False,
    )
```

profile of v0, /device:TPU:0, one launch (start us, length us, event | category | flops | bytes accessed | tf_op | source)
XLA Modules:
  0.0 879.5 jit_solution(13289272174919449863)
XLA Ops:
  7.2 0.0 copy-start
  7.2 0.0 all-reduce.3.cloned.1.call-start
  7.2 1.5 copy-done
  8.8 14.6 %fusion = f32[4096,1024]{1,0:T(8,128)} fusion(bf16[1024,4096]{1,0:T(8,128)(2,1)} %param.5, bf16[1024,1024]{1,0:T(8,128)(2,1)S(1)} %copy-done), kind=kOutput, calls=%fused_computation.4 | convolution fusion | flops 8589934592 | bytes 27262976 | tf_op jit(solution)/shard_map/dot_general | solution.py:15
  23.3 645.8 %all-reduce.4 = bf16[4096,1024]{1,0:T(8,128)(2,1)} all-reduce(f32[4096,1024]{1,0:T(8,128)} %fusion), channel_id=1, replica_groups=mesh['dp'=8,'node'=4] {'dp'}, use_global_device_ids=true, to_apply=%region_0.0 | all-reduce | flops 4194304 | bytes 25165824 | tf_op jit(solution)/shard_map/psum | solution.py:30
  669.2 5.0 dynamic-slice_select_fusion
  674.1 0.0 all-reduce.3.cloned.1.call-update
  674.2 0.0 all-gather.2.cloned.1.call-start
  674.2 2.3 constant_dynamic-slice_fusion
  676.5 0.0 all-gather.2.cloned.1.call-update
  676.5 11.5 %copy.6 = bf16[4,1024,1024]{1,2,0:T(8,128)(2,1)} copy(bf16[4,1024,1024]{2,1,0:T(8,128)(2,1)} %bitcast.10) | data formatting | bytes 16777216 | tf_op jit(solution)/shard_map/all_to_all | solution.py:33
  688.0 0.0 copy-start.2
  688.0 6.0 all-to-all-start
  694.0 117.5 %all-reduce.3.cloned.1.call-done = bf16[4096,512]{1,0:T(8,128)(2,1)} async-done(((bf16[4096,512]{1,0:T(8,128)(2,1)}), bf16[4096,512]{1,0:T(8,128)(2,1)}) %all-reduce.3.cloned.1.call-update) | async-done | bytes 4194320 | tf_op jit(solution)/shard_map/psum | solution.py:11
  811.4 0.0 copy-done.2
  811.4 10.4 %multiply_add_fusion.1 = f32[1024,512]{1,0:T(8,128)} fusion(f32[1024,512]{1,0:T(8,128)S(1)} %copy-done.2, bf16[4096,1024]{1,0:T(8,128)(2,1)} %all-reduce.4, bf16[4096,512]{1,0:T(8,128)(2,1)} %all-reduce.3.cloned.1.call-done), kind=kOutput, calls=%fused_computation.2 | convolution fusion | flops 4296540160 | bytes 16777216 | tf_op jit(solution)/shard_map/dot_general | solution.py:15
  821.9 39.5 %all-gather.2.cloned.1.call-done = bf16[512,4096]{1,0:T(8,128)(2,1)} async-done(((bf16[512,1024]{1,0:T(8,128)(2,1)}), bf16[512,4096]{1,0:T(8,128)(2,1)}) %all-gather.2.cloned.1.call-update) | async-done | bytes 4194320 | tf_op jit(solution)/shard_map/all_gather | solution.py:34
  861.4 0.0 all-to-all-done
  861.4 0.0 copy-start.1
  861.4 11.3 %multiply_add_fusion = f32[1024,512]{1,0:T(8,128)} fusion(f32[1024,512]{1,0:T(8,128)} %param.7, bf16[1024,4096]{0,1:T(8,128)(2,1)} %bitcast.2, bf16[512,4096]{1,0:T(8,128)(2,1)} %all-gather.2.cloned.1.call-done), kind=kOutput, calls=%fused_computation.1 | convolution fusion | flops 4296540160 | bytes 16777216 | tf_op jit(solution)/shard_map/dot_general | solution.py:21
  872.7 0.0 copy-done.1
Async XLA Ops:
  7.2 1.6 copy-start
  7.2 804.2 %all-reduce.3.cloned.1.call-start = ((), (), s32[]{:S(2)}) async-start(), calls=%async_computation.1 | async-start | bytes 8388608 | tf_op jit(solution)/shard_map/psum | solution.py:11
  674.2 187.2 %all-gather.2.cloned.1.call-start = ((), (), s32[]{:S(2)}) async-start(), calls=%async_computation.2 | async-start | bytes 5242880 | tf_op jit(solution)/shard_map/all_gather | solution.py:34
  688.0 123.4 %copy-start.2 = (f32[1024,512]{1,0:T(8,128)S(1)}, f32[1024,512]{1,0:T(8,128)}, u32[]{:S(2)}) copy-start(f32[1024,512]{1,0:T(8,128)} %param.6) | copy-start | bytes 6291460
  688.0 173.4 %all-to-all-start = ((bf16[4,1024,1024]{1,2,0:T(8,128)(2,1)}), bf16[4,1024,1024]{1,2,0:T(8,128)(2,1)}, u32[]{:S(2)}, u32[]{:S(2)}) async-start(bf16[4,1024,1024]{1,2,0:T(8,128)(2,1)} %copy.6), calls=%async_computation | async-start | bytes 16777216 | tf_op jit(solution)/shard_map/all_to_all | solution.py:33
  861.4 11.3 %copy-start.1 = (bf16[1024,1024]{1,0:T(8,128)(2,1)S(1)}, bf16[1024,1024]{1,0:T(8,128)(2,1)}, u32[]{:S(2)}) copy-start(bf16[1024,1024]{1,0:T(8,128)(2,1)} %param.4) | copy-start | bytes 6291460
Sparse Core Ops, SparseCore 0:
  674.3 137.0 all-reduce.2
  813.6 47.6 all-gather.1
where the time goes:
time: 880 us
  blocking collectives  646 us (73%)
  waiting for transfers between devices  157 us (18%)
  matrix products  36.3 us (4%)
  local copies, waits for them, and re-layouts  15.3 us (2%)
  between operations  14.1 us (2%)
    psum x1, blocking collectives, shards(): summed = lax.psum(contract_first(out_grads, tokens_in), 'dp')  646 us
    psum x1, waiting for transfers between devices, from_root(): return lax.psum(kept, axis)  117 us
    all_gather x1, waiting for transfers between devices, shards(): lax.all_gather(own_tile, 'node', axis=1, tiled=True)  39.5 us
    dot_general x2, matrix products, contract_first(): lax.dot_general(left, right, (((0,), (0,)), ((), ())), preferred_element_...  25 us
  transfers between devices with their start and end apart: 3, of which 2 were waited for; matrix products, arithmetic and copies ran while one was open for 3% of the time, Pallas kernels for 0%

commit v1 on v0

v1 whole, which is shorter than its diff:
```python
import jax
import jax.numpy as jnp
from jax import lax
from jax.sharding import PartitionSpec as P

ema_decay = 0.95
halves = 2
wire_gain = 2.0**20


def contract_first(left, right):
    return lax.dot_general(
        left, right, (((0,), (0,)), ((), ())), preferred_element_type=jnp.float32
    )


def contract_last(left, right):
    return lax.dot_general(
        left, right, (((1,), (1,)), ((), ())), preferred_element_type=jnp.float32
    )


def to_wire(value):
    root = jnp.sqrt(jnp.abs(value) * wire_gain)
    return jnp.where(value < 0, -root, root).astype(jnp.float16)


def from_wire(sent):
    root = sent.astype(jnp.float32)
    return root * jnp.abs(root) * (1.0 / wire_gain)


def pick(blocks, index):
    return lax.dynamic_index_in_dim(blocks, index, 0, keepdims=False)


def after(values, *done):
    return lax.optimization_barrier((values, done))[0]


def shards(tokens_in, out_grads, left_old, right_old):
    nodes = lax.axis_size("node")
    ring = lax.axis_size("dp")
    pair = ring // nodes
    depth = ring // pair
    dp_index = lax.axis_index("dp")
    node = lax.axis_index("node")
    z, y = dp_index // pair, dp_index % pair
    tokens = tokens_in.shape[0]
    rows, width = left_old.shape
    part = width // halves
    half = pair * part

    def place(z, y):
        return jnp.where(y == 0, z, ring - 1 - z)

    def member(position):
        return jnp.where(
            position < depth, position * pair, (ring - 1 - position) * pair + 1
        )

    order = [k * pair for k in range(depth)] + [k * pair + 1 for k in reversed(range(depth))]
    position = place(z, y)
    steps = ring // 2

    def rise(block):
        return lax.ppermute(
            block, "dp", [(order[k], order[(k + 1) % ring]) for k in range(ring)]
        )

    def fall(block):
        return lax.ppermute(
            block, "dp", [(order[(k + 1) % ring], order[k]) for k in range(ring)]
        )

    def swap(block):
        return lax.ppermute(block, "dp", [(d, d ^ 1) for d in range(ring)])

    def exchange(block, bit):
        return lax.ppermute(block, "node", [(n, n ^ bit) for n in range(nodes)])

    def spread(have):
        bit = nodes // 4
        while bit:
            for j in sorted(have):
                have[j | bit] = exchange(have[j], bit)
            bit //= 2
        return [have[j] for j in range(nodes)]

    tokens_split = tokens_in.reshape(tokens, pair, halves, part)
    own_tokens = [tokens_split[:, :, h].reshape(tokens, half) for h in range(halves)]

    def term(h, ahead):
        slab = member((position + ahead) % ring)
        grads = lax.dynamic_slice_in_dim(out_grads, slab * width, width, 1)
        return contract_first(own_tokens[h], grads)

    up, down = [None] * halves, [None] * halves

    def send_up(h, step):
        total = term(h, step)
        if up[h] is not None:
            total = total + from_wire(up[h])
        up[h] = rise(to_wire(total))

    def send_down(h, step):
        total = term(h, ring - step)
        if down[h] is not None:
            total = total + from_wire(down[h])
        down[h] = fall(to_wire(total))

    send_up(0, steps)
    send_down(1, steps)
    for step in range(steps - 1, 0, -1):
        send_up(1, step)
        send_down(0, step)
        send_up(0, step)
        send_down(1, step)
    own = [
        (term(h, 0) + from_wire(up[h]) + from_wire(down[h])).astype(jnp.bfloat16)
        for h in range(halves)
    ]

    sent = [{} for _ in range(halves)]

    def choose(h, panel, j, r):
        spot = (place(node ^ j, y ^ r) + ring - position) % ring
        sent[h][j, r] = pick(panel, spot)
        return sent[h][j, r]

    def gather(h, block, before, late):
        ups, downs, waiting = [block], [block], []

        def ahead():
            far = [ups[0]] if len(ups) <= steps else [jnp.concatenate([ups[-1], downs[-1]])]
            near = [block] + downs[1:steps] + far + ups[steps - 1 : 0 : -1]
            return jnp.stack(near)

        for step in range(1, steps + 1):
            top, bottom = ups[-1], downs[-1]
            if step == steps:
                top, bottom = top[: half // 2], bottom[half // 2 :]
            top, bottom = after((top, bottom), *waiting)
            waiting = []
            if step == steps:
                waiting = late(ahead(), (top, bottom))
            elif before:
                waiting = before.pop(0)((top, bottom))
            ups.append(rise(top))
            downs.append(fall(bottom))
        return ahead(), waiting

    top_bit = nodes // 2
    slab_far = [None] * halves

    def slab_job(h):
        def job(ready):
            slab_far[h] = exchange(after(own[h], ready), top_bit)
            return [slab_far[h]]

        return job

    cols = [{} for _ in range(halves)]

    def trade(h, panel, j, r):
        def job(ready):
            cols[h][j, r] = exchange(after(choose(h, panel, j, r), ready), j)
            return [cols[h][j, r]]

        return job

    far = [j for j in range(2, nodes)]
    first = far[0]

    def early(h):
        return lambda panel, ready: trade(h, panel, first, 0)(ready)

    panel_a, wait_a = gather(0, own[0], [slab_job(h) for h in range(halves)], early(0))
    slab = [spread({0: own[h], top_bit: slab_far[h]}) for h in range(halves)]

    jobs = [trade(0, panel_a, j, 0) for j in far[1:]] + [trade(0, panel_a, j, 1) for j in far]
    panel_b, wait_b = gather(1, after(own[1], panel_a, wait_a), jobs, early(1))
    ready = (panel_b, wait_b)
    for job in jobs:
        ready = job(ready)
    for j in far[1:]:
        ready = trade(1, panel_b, j, 0)(ready)
    for j in far:
        choose(1, panel_b, j, 1)
        cols[1][j, 1] = swap(cols[1][j, 0])
    for h, panel in ((0, panel_a), (1, panel_b)):
        for r in range(pair):
            cols[h][0, r] = choose(h, panel, 0, r)
            trade(h, panel, 1, r)(())

    mine = []
    for h in range(halves):
        piece = []
        for r in range(pair):
            found = jnp.stack([cols[h][j, r] for j in range(nodes)])
            found = lax.dynamic_slice(
                found, (z ^ node, y * part, 0), (1, part, width)
            )
            piece.append(found[0])
        piece = jnp.stack(piece)
        ready = exchange(after(piece, ready), top_bit)
        mine.append(spread({0: piece, top_bit: ready}))

    right_new = []
    for r in range(pair):
        total = 0.0
        for h in range(halves):
            for j in range(nodes):
                total = total + contract_first(cols[h][j, r], slab[h][j])
        right_new.append(total)
    right_new = jnp.concatenate(
        [
            jnp.where(y == 0, right_new[0], right_new[1]),
            jnp.where(y == 0, right_new[1], right_new[0]),
        ]
    )

    left_new = []
    for h in range(halves):
        line = []
        for g in range(halves):
            total = 0.0
            for j in range(nodes):
                for r in range(pair):
                    total = total + contract_last(sent[h][j, r], mine[g][j][r])
            line.append(total)
        left_new.append(jnp.concatenate(line, 1).reshape(pair, part, width))
    left_new = jnp.stack(left_new, 1).reshape(rows, width)
    left_out = ema_decay * left_old + (1.0 - ema_decay) * left_new
    right_out = ema_decay * right_old + (1.0 - ema_decay) * right_new
    return (left_out, right_out)


def solution(mesh):
    placed = (P("dp", "node"), P("dp", None), P("node", "dp"), P("node", "dp"))
    return jax.shard_map(
        shards,
        mesh=mesh,
        in_specs=placed,
        out_specs=(P("node", "dp"), P("node", "dp")),
        check_vma=False,
    )
```

time: 880 us -> 296 us (0.34)
  blocking collectives: 646 us -> 0 us
  starting transfers between devices: 6.04 us -> 46.4 us
  matrix products: 36.3 us -> 68.4 us
  waiting for transfers between devices: 157 us -> 143 us
  between operations: 14.1 us -> 1.9 us
    psum x1 -> x0, blocking collectives: 646 us -> none  [shards(): summed = lax.psum(contract_first(out_grads, tokens_in), 'dp')]
    ppermute x0 -> x54, waiting for transfers between devices: none -> 143 us  [the longest x15 50.7 us: fall(): lax.ppermute(block, 'dp', [(order[(k + 1) % ring], order[k]) for k in ran...]
    psum x1 -> x0, waiting for transfers between devices: 117 us -> none  [from_root(): return lax.psum(kept, axis)]
    ppermute x0 -> x54, starting transfers between devices: none -> 46.4 us  [the longest x15 24 us: fall(): lax.ppermute(block, 'dp', [(order[(k + 1) % ring], order[k]) for k in ran...]
    all_gather x1 -> x0, waiting for transfers between devices: 39.5 us -> none  [shards(): lax.all_gather(own_tile, 'node', axis=1, tiled=True)]
    dot_general x2 -> x32, matrix products: 25 us -> 53 us  [contract_first(): lax.dot_general(left, right, (((0,), (0,)), ((), ())), preferred_element_...]
    unnamed x6 -> x54, local copies, waits for them, and re-layouts: 1.53 us -> 14.3 us
    all_to_all x1 -> x0, local copies, waits for them, and re-layouts: 11.5 us -> none  [shards(): lax.all_to_all(row_panel, 'node', split_axis=0, concat_axis=1, tiled=True)]
  transfers between devices with their start and end apart: 3 -> 54, of which waited for: 2 -> 29; matrix products, arithmetic and copies ran while one was open for 3% -> 28% of each run, Pallas kernels for 0% -> 0%
where the time goes in v1:
time: 296 us; the launch traced here: 290 us
  waiting for transfers between devices  143 us (48%)
  matrix products  68.4 us (23%)
  starting transfers between devices  46.4 us (16%)
  local copies, waits for them, and re-layouts  19.8 us (7%)
  other arithmetic  10.4 us (4%)
    dot_general x32, matrix products, contract_first(): lax.dot_general(left, right, (((0,), (0,)), ((), ())), preferred_element_...  53 us
    ppermute x15, waiting for transfers between devices, fall(): lax.ppermute(block, 'dp', [(order[(k + 1) % ring], order[k]) for k in ran...  50.7 us
    ppermute x15, waiting for transfers between devices, rise(): lax.ppermute(block, 'dp', [(order[k], order[(k + 1) % ring]) for k in ran...  48.2 us
    ppermute x22, waiting for transfers between devices, exchange(): return lax.ppermute(block, 'node', [(n, n ^ bit) for n in range(nodes)])  35.6 us
    ppermute x15, starting transfers between devices, fall(): lax.ppermute(block, 'dp', [(order[(k + 1) % ring], order[k]) for k in ran...  24 us
    dot_general x32, matrix products, contract_last(): lax.dot_general(left, right, (((1,), (1,)), ((), ())), preferred_element_...  15.4 us
    unnamed x54, local copies, waits for them, and re-layouts  14.3 us
    ppermute x22, starting transfers between devices, exchange(): return lax.ppermute(block, 'node', [(n, n ^ bit) for n in range(nodes)])  11.7 us
  transfers between devices with their start and end apart: 54, of which 29 were waited for; matrix products, arithmetic and copies ran while one was open for 28% of the time, Pallas kernels for 0%

profile of v1, /device:TPU:0, one launch (start us, length us, event | category | flops | bytes accessed | tf_op | source)
XLA Modules:
  0.0 290.4 jit_solution(7243935824713386805)
XLA Ops:
  0.7 2.9 copy.34
  4.8 3.6 %fusion.54 = f16[512,512]{0,1:T(8,128)(2,1)} fusion(bf16[1024,512]{0,1:T(8,128)(2,1)S(1)} %bitcast.326, bf16[1024,4096]{1,0:T(8,128)(2,1)} %param.5, s32[]{:T(128)S(6)} %select_n.323), kind=kOutput, calls=%fused_computation.133 | convolution fusion | flops 538443776 | bytes 2621444 | tf_op jit(solution)/shard_map/dot_general | solution.py:12
  8.3 3.0 %collective-permute-start.15 = (f16[512,512]{0,1:T(8,128)(2,1)}, f16[512,512]{0,1:T(8,128)(2,1)}, u32[]{:S(2)}, u32[]{:S(2)}) collective-permute-start(f16[512,512]{0,1:T(8,128)(2,1)} %fusion.54), channel_id=1, source_target_pairs={{8,0},{16,8},{24,16},{28,24},{20,28},{12,20},{4,12},{0,4},{9,1},{1... | collective-permute-start | bytes 1572872 | tf_op jit(solution)/shard_map/ppermute | solution.py:72
  11.3 3.1 %fusion.43 = f16[512,512]{0,1:T(8,128)(2,1)} fusion(bf16[1024,512]{0,1:T(8,128)(2,1)S(1)} %bitcast.327, bf16[1024,4096]{1,0:T(8,128)(2,1)} %param.5, s32[]{:T(128)S(6)} %select_n.320), kind=kOutput, calls=%fused_computation.122 | convolution fusion | flops 538443776 | bytes 2621444 | tf_op jit(solution)/shard_map/dot_general | solution.py:12
  14.5 3.1 %fusion.35 = f16[512,512]{0,1:T(8,128)(2,1)} fusion(bf16[1024,512]{0,1:T(8,128)(2,1)S(1)} %bitcast.336, bf16[1024,4096]{1,0:T(8,128)(2,1)} %param.5, s32[]{:T(128)S(6)} %select_n.336), kind=kOutput, calls=%fused_computation.114 | convolution fusion | flops 538443776 | bytes 2621444 | tf_op jit(solution)/shard_map/dot_general | solution.py:12
  17.6 2.0 collective-permute-start.4
  19.5 3.1 %fusion.21 = f16[512,512]{0,1:T(8,128)(2,1)} fusion(bf16[1024,512]{0,1:T(8,128)(2,1)S(1)} %bitcast.337, bf16[1024,4096]{1,0:T(8,128)(2,1)} %param.5, s32[]{:T(128)S(6)} %select_n.323), kind=kOutput, calls=%fused_computation.100 | convolution fusion | flops 538443776 | bytes 2621444 | tf_op jit(solution)/shard_map/dot_general | solution.py:12
  22.9 2.0 convolution_bitcast_fusion.2
  24.9 3.0 %convolution_bitcast_fusion.7 = f32[512,512]{0,1:T(8,128)} fusion(bf16[1024,512]{0,1:T(8,128)(2,1)S(1)} %bitcast.338, bf16[1024,4096]{1,0:T(8,128)(2,1)} %param.5, s32[]{:T(128)S(6)} %select_n.330), kind=kOutput, calls=%fused_computation.69 | convolution fusion | flops 536870912 | bytes 3145732 | tf_op jit(solution)/shard_map/dot_general | solution.py:12
  27.9 2.0 convolution_bitcast_fusion.4
  29.9 2.3 convolution_bitcast_fusion.10
  32.2 3.3 %convolution_bitcast_fusion.1 = f32[512,512]{0,1:T(8,128)} fusion(bf16[1024,512]{0,1:T(8,128)(2,1)} %bitcast.330, bf16[1024,4096]{1,0:T(8,128)(2,1)} %param.5, s32[]{:T(128)S(6)} %select_n.333), kind=kOutput, calls=%fused_computation.63 | convolution fusion | flops 536870912 | bytes 3145732 | tf_op jit(solution)/shard_map/dot_general | solution.py:12
  35.5 2.4 convolution_bitcast_fusion.11
  37.9 2.0 convolution_bitcast_fusion.9
  39.9 2.6 fusion.57
  42.6 1.9 collective-permute-start.16
  44.5 2.6 fusion.24
  47.3 2.6 fusion.46
  50.0 2.0 collective-permute-start.13
  51.9 2.6 fusion.38
  54.8 7.2 %collective-permute-done.1 = f16[512,512]{0,1:T(8,128)(2,1)S(1)} collective-permute-done((f16[512,512]{0,1:T(8,128)(2,1)S(1)}, f16[512,512]{0,1:T(8,128)(2,1)S(1)}, u32[]{:S(2)}, u32[]{:S(2)}) %collective-permute-start.1) | collective-permute-done | bytes 524320 | tf_op jit(solution)/shard_map/ppermute | solution.py:67
  63.7 1.9 collective-permute-start.17
  65.7 3.8 %collective-permute-done.5 = f16[512,512]{0,1:T(8,128)(2,1)S(1)} collective-permute-done((f16[512,512]{0,1:T(8,128)(2,1)S(1)}, f16[512,512]{0,1:T(8,128)(2,1)S(1)}, u32[]{:S(2)}, u32[]{:S(2)}) %collective-permute-start.5) | collective-permute-done | bytes 524320 | tf_op jit(solution)/shard_map/ppermute | solution.py:72
  70.4 11.5 %collective-permute-done.2 = f16[512,512]{0,1:T(8,128)(2,1)S(1)} collective-permute-done((f16[512,512]{0,1:T(8,128)(2,1)S(1)}, f16[512,512]{0,1:T(8,128)(2,1)S(1)}, u32[]{:S(2)}, u32[]{:S(2)}) %collective-permute-start.2) | collective-permute-done | bytes 524320 | tf_op jit(solution)/shard_map/ppermute | solution.py:67
  83.7 1.7 collective-permute-start.14
  86.4 5.5 %collective-permute-done.6 = f16[512,512]{0,1:T(8,128)(2,1)S(1)} collective-permute-done((f16[512,512]{0,1:T(8,128)(2,1)S(1)}, f16[512,512]{0,1:T(8,128)(2,1)S(1)}, u32[]{:S(2)}, u32[]{:S(2)}) %collective-permute-start.6) | collective-permute-done | bytes 524320 | tf_op jit(solution)/shard_map/ppermute | solution.py:72
  91.9 5.5 %collective-permute-done.3 = f16[512,512]{0,1:T(8,128)(2,1)S(1)} collective-permute-done((f16[512,512]{0,1:T(8,128)(2,1)S(1)}, f16[512,512]{0,1:T(8,128)(2,1)S(1)}, u32[]{:S(2)}, u32[]{:S(2)}) %collective-permute-start.3) | collective-permute-done | bytes 524320 | tf_op jit(solution)/shard_map/ppermute | solution.py:67
  102.2 2.0 convolution_bitcast_fusion.5
  104.1 4.5 %collective-permute-done.14 = f16[512,512]{0,1:T(8,128)(2,1)S(1)} collective-permute-done((f16[512,512]{0,1:T(8,128)(2,1)S(1)}, f16[512,512]{0,1:T(8,128)(2,1)S(1)}, u32[]{:S(2)}, u32[]{:S(2)}) %collective-permute-start.14) | collective-permute-done | bytes 524320 | tf_op jit(solution)/shard_map/ppermute | solution.py:67
  109.1 2.6 collective-permute-done.7
  111.6 4.8 %collective-permute-done.8 = bf16[512,512]{0,1:T(8,128)(2,1)S(1)} collective-permute-done((bf16[512,512]{0,1:T(8,128)(2,1)S(1)}, bf16[512,512]{0,1:T(8,128)(2,1)S(1)}, u32[]{:S(2)}, u32[]{:S(2)}) %collective-permute-start.8) | collective-permute-done | bytes 524320 | tf_op jit(solution)/shard_map/ppermute | solution.py:67
  119.9 7.0 %collective-permute-done.10 = bf16[512,512]{0,1:T(8,128)(2,1)} collective-permute-done((bf16[512,512]{0,1:T(8,128)(2,1)S(1)}, bf16[512,512]{0,1:T(8,128)(2,1)}, u32[]{:S(2)}, u32[]{:S(2)}) %collective-permute-start.10) | collective-permute-done | bytes 524320 | tf_op jit(solution)/shard_map/ppermute | solution.py:72
  126.9 3.0 %collective-permute-done.11 = bf16[512,512]{0,1:T(8,128)(2,1)S(1)} collective-permute-done((bf16[512,512]{0,1:T(8,128)(2,1)S(1)}, bf16[512,512]{0,1:T(8,128)(2,1)S(1)}, u32[]{:S(2)}, u32[]{:S(2)}) %collective-permute-start.11) | collective-permute-done | bytes 524320 | tf_op jit(solution)/shard_map/ppermute | solution.py:67
  130.7 1.7 collective-permute-start.20
  132.4 1.9 bitcast_dynamic-update-slice_fusion.26
  134.3 1.9 bitcast_dynamic-update-slice_fusion.24
  136.2 3.2 %collective-permute-done.21 = bf16[512,512]{0,1:T(8,128)(2,1)S(1)} collective-permute-done((bf16[512,512]{0,1:T(8,128)(2,1)S(1)}, bf16[512,512]{0,1:T(8,128)(2,1)S(1)}, u32[]{:S(2)}, u32[]{:S(2)}) %collective-permute-start.21) | collective-permute-done | bytes 524320 | tf_op jit(solution)/shard_map/ppermute | solution.py:67
  143.7 2.3 copy.49
  147.2 1.8 collective-permute-done.22
  153.5 6.2 %collective-permute-done.25 = bf16[512,512]{0,1:T(8,128)(2,1)} collective-permute-done((bf16[512,512]{0,1:T(8,128)(2,1)}, bf16[512,512]{0,1:T(8,128)(2,1)}, u32[]{:S(2)}, u32[]{:S(2)}) %collective-permute-start.25) | collective-permute-done | bytes 524320 | tf_op jit(solution)/shard_map/ppermute | solution.py:80
  159.7 2.0 collective-permute-start.29
  161.7 1.7 fusion.197
  168.8 5.2 %collective-permute-done.29 = bf16[512,512]{0,1:T(8,128)(2,1)S(1)} collective-permute-done((bf16[512,512]{0,1:T(8,128)(2,1)S(1)}, bf16[512,512]{0,1:T(8,128)(2,1)S(1)}, u32[]{:S(2)}, u32[]{:S(2)}) %collective-permute-start.29) | collective-permute-done | bytes 524320 | tf_op jit(solution)/shard_map/ppermute | solution.py:72
  174.1 1.8 collective-permute-done.28
  175.9 2.1 collective-permute-done.26
  177.9 2.2 collective-permute-start.32
  182.0 9.9 %collective-permute-done.32 = bf16[512,512]{0,1:T(8,128)(2,1)S(1)} collective-permute-done((bf16[512,512]{0,1:T(8,128)(2,1)S(1)}, bf16[512,512]{0,1:T(8,128)(2,1)S(1)}, u32[]{:S(2)}, u32[]{:S(2)}) %collective-permute-start.32) | collective-permute-done | bytes 524320 | tf_op jit(solution)/shard_map/ppermute | solution.py:72
  191.9 2.0 collective-permute-done.31
  193.8 1.8 collective-permute-start.35
  196.4 10.4 %collective-permute-done.35 = bf16[512,512]{0,1:T(8,128)(2,1)S(1)} collective-permute-done((bf16[512,512]{0,1:T(8,128)(2,1)S(1)}, bf16[512,512]{0,1:T(8,128)(2,1)S(1)}, u32[]{:S(2)}, u32[]{:S(2)}) %collective-permute-start.35) | collective-permute-done | bytes 524320 | tf_op jit(solution)/shard_map/ppermute | solution.py:72
  208.2 1.9 collective-permute-done.33
  210.0 1.8 collective-permute-start.38
  213.4 4.9 %collective-permute-done.38 = bf16[256,512]{0,1:T(8,128)(2,1)S(1)} collective-permute-done((bf16[256,512]{0,1:T(8,128)(2,1)S(1)}, bf16[256,512]{0,1:T(8,128)(2,1)S(1)}, u32[]{:S(2)}, u32[]{:S(2)}) %collective-permute-start.38) | collective-permute-done | bytes 262176 | tf_op jit(solution)/shard_map/ppermute | solution.py:72
  218.4 1.9 collective-permute-done.37
  224.6 9.2 %collective-permute-done.39 = bf16[512,512]{0,1:T(8,128)(2,1)S(1)} collective-permute-done((bf16[512,512]{0,1:T(8,128)(2,1)S(1)}, bf16[512,512]{0,1:T(8,128)(2,1)S(1)}, u32[]{:S(2)}, u32[]{:S(2)}) %collective-permute-start.39) | collective-permute-done | bytes 524320 | tf_op jit(solution)/shard_map/ppermute | solution.py:80
  234.1 1.8 collective-permute-start.45
  236.3 10.5 %collective-permute-done.40 = bf16[512,512]{0,1:T(8,128)(2,1)S(1)} collective-permute-done((bf16[512,512]{0,1:T(8,128)(2,1)S(1)}, bf16[512,512]{0,1:T(8,128)(2,1)S(1)}, u32[]{:S(2)}, u32[]{:S(2)}) %collective-permute-start.40) | collective-permute-done | bytes 524320 | tf_op jit(solution)/shard_map/ppermute | solution.py:80
  246.8 1.7 collective-permute-start.46
  250.9 8.8 %collective-permute-done.46 = bf16[512,512]{0,1:T(8,128)(2,1)S(1)} collective-permute-done((bf16[512,512]{0,1:T(8,128)(2,1)S(1)}, bf16[512,512]{0,1:T(8,128)(2,1)S(1)}, u32[]{:S(2)}, u32[]{:S(2)}) %collective-permute-start.46) | collective-permute-done | bytes 524320 | tf_op jit(solution)/shard_map/ppermute | solution.py:77
  260.7 2.2 collective-permute-done.41
  262.9 1.7 collective-permute-start.48
  270.6 1.8 fusion
  272.4 3.7 %collective-permute-done.48 = bf16[2,256,512]{1,2,0:T(8,128)(2,1)S(1)} collective-permute-done((bf16[2,256,512]{1,2,0:T(8,128)(2,1)S(1)}, bf16[2,256,512]{1,2,0:T(8,128)(2,1)S(1)}, u32[]{:S(2)}, u32[]{:S(2)}) %collective-permute-start.48) | collective-permute-done | bytes 524320 | tf_op jit(solution)/shard_map/ppermute | solution.py:80
  288.4 1.8 bitcast_add_fusion
  (196 shorter events, 63.9 us)
Async XLA Ops:
  4.8 23.1 %copy-start.14 = (bf16[1024,2,1,256]{0,3,2,1:T(8,128)(2,1)}, bf16[1024,2,1,256]{0,3,2,1:T(8,128)(2,1)S(1)}, u32[]{:S(2)}) copy-start(bf16[1024,2,1,256]{0,3,2,1:T(8,128)(2,1)S(1)} %get-tuple-element.73) | copy-start | bytes 3145732
  4.8 9.7 %copy-start.16 = (bf16[1024,2,1,256]{0,3,2,1:T(8,128)(2,1)S(1)}, bf16[1024,2,1,256]{0,3,2,1:T(8,128)(2,1)}, u32[]{:S(2)}) copy-start(bf16[1024,2,1,256]{0,3,2,1:T(8,128)(2,1)} %get-tuple-element.72) | copy-start | bytes 3145732
  8.3 31.6 %collective-permute-start.15 = (f16[512,512]{0,1:T(8,128)(2,1)}, f16[512,512]{0,1:T(8,128)(2,1)}, u32[]{:S(2)}, u32[]{:S(2)}) collective-permute-start(f16[512,512]{0,1:T(8,128)(2,1)} %fusion.54), channel_id=1, source_target_pairs={{8,0},{16,8},{24,16},{28,24},{20,28},{12,20},{4,12},{0,4},{9,1},{1... | collective-permute-start | bytes 1572872 | tf_op jit(solution)/shard_map/ppermute | solution.py:72
  14.4 32.9 %collective-permute-start.12 = (f16[512,512]{0,1:T(8,128)(2,1)}, f16[512,512]{0,1:T(8,128)(2,1)}, u32[]{:S(2)}, u32[]{:S(2)}) collective-permute-start(f16[512,512]{0,1:T(8,128)(2,1)} %fusion.43), channel_id=1, source_target_pairs={{0,8},{8,16},{16,24},{24,28},{28,20},{20,12},{12,4},{4,0},{1,9},{9... | collective-permute-start | bytes 1572872 | tf_op jit(solution)/shard_map/ppermute | solution.py:67
  17.6 34.4 %collective-permute-start.4 = (f16[512,512]{0,1:T(8,128)(2,1)}, f16[512,512]{0,1:T(8,128)(2,1)}, u32[]{:S(2)}, u32[]{:S(2)}) collective-permute-start(f16[512,512]{0,1:T(8,128)(2,1)} %fusion.35), channel_id=1, source_target_pairs={{8,0},{16,8},{24,16},{28,24},{20,28},{12,20},{4,12},{0,4},{9,1},{1... | collective-permute-start | bytes 1572872 | tf_op jit(solution)/shard_map/ppermute | solution.py:72
  22.6 21.9 %collective-permute-start = (f16[512,512]{0,1:T(8,128)(2,1)}, f16[512,512]{0,1:T(8,128)(2,1)}, u32[]{:S(2)}, u32[]{:S(2)}) collective-permute-start(f16[512,512]{0,1:T(8,128)(2,1)} %fusion.21), channel_id=1, source_target_pairs={{0,8},{8,16},{16,24},{24,28},{28,20},{20,12},{12,4},{4,0},{1,9},{9... | collective-permute-start | bytes 1572872 | tf_op jit(solution)/shard_map/ppermute | solution.py:67
  35.5 4.5 %copy-start.15 = (bf16[1024,2,1,256]{0,3,2,1:T(8,128)(2,1)S(1)}, bf16[1024,2,1,256]{0,3,2,1:T(8,128)(2,1)}, u32[]{:S(2)}) copy-start(bf16[1024,2,1,256]{0,3,2,1:T(8,128)(2,1)} %copy-done.14) | copy-start | bytes 3145732
  42.6 20.5 %collective-permute-start.16 = (f16[512,512]{0,1:T(8,128)(2,1)S(1)}, f16[512,512]{0,1:T(8,128)(2,1)S(1)}, u32[]{:S(2)}, u32[]{:S(2)}) collective-permute-start(f16[512,512]{0,1:T(8,128)(2,1)S(1)} %fusion.57), channel_id=1, source_target_pairs={{8,0},{16,8},{24,16},{28,24},{20,28},{12,20},{4,12},{0,4},{9,1},{1... | collective-permute-start | bytes 1572872 | tf_op jit(solution)/shard_map/ppermute | solution.py:72
  47.1 14.9 %collective-permute-start.1 = (f16[512,512]{0,1:T(8,128)(2,1)S(1)}, f16[512,512]{0,1:T(8,128)(2,1)S(1)}, u32[]{:S(2)}, u32[]{:S(2)}) collective-permute-start(f16[512,512]{0,1:T(8,128)(2,1)S(1)} %fusion.24), channel_id=1, source_target_pairs={{0,8},{8,16},{16,24},{24,28},{28,20},{20,12},{12,4},{4,0},{1,9},{9... | collective-permute-start | bytes 1572872 | tf_op jit(solution)/shard_map/ppermute | solution.py:67
  50.0 13.1 %copy-start.13 = (f32[512,512]{0,1:T(8,128)S(1)}, f32[512,512]{0,1:T(8,128)}, u32[]{:S(2)}) copy-start(f32[512,512]{0,1:T(8,128)} %convolution_bitcast_fusion.1) | copy-start | bytes 3145732
  50.0 19.5 %copy-start.12 = (f32[512,512]{0,1:T(8,128)S(1)}, f32[512,512]{0,1:T(8,128)}, u32[]{:S(2)}) copy-start(f32[512,512]{0,1:T(8,128)} %convolution_bitcast_fusion.7) | copy-start | bytes 3145732
  50.0 33.1 %collective-permute-start.13 = (f16[512,512]{0,1:T(8,128)(2,1)S(1)}, f16[512,512]{0,1:T(8,128)(2,1)S(1)}, u32[]{:S(2)}, u32[]{:S(2)}) collective-permute-start(f16[512,512]{0,1:T(8,128)(2,1)S(1)} %fusion.46), channel_id=1, source_target_pairs={{0,8},{8,16},{16,24},{24,28},{28,20},{20,12},{12,4},{4,0},{1,9},{9... | collective-permute-start | bytes 1572872 | tf_op jit(solution)/shard_map/ppermute | solution.py:67
  54.6 14.9 %collective-permute-start.5 = (f16[512,512]{0,1:T(8,128)(2,1)S(1)}, f16[512,512]{0,1:T(8,128)(2,1)S(1)}, u32[]{:S(2)}, u32[]{:S(2)}) collective-permute-start(f16[512,512]{0,1:T(8,128)(2,1)S(1)} %fusion.38), channel_id=1, source_target_pairs={{8,0},{16,8},{24,16},{28,24},{20,28},{12,20},{4,12},{0,4},{9,1},{1... | collective-permute-start | bytes 1572872 | tf_op jit(solution)/shard_map/ppermute | solution.py:72
  62.7 19.2 %collective-permute-start.2 = (f16[512,512]{0,1:T(8,128)(2,1)S(1)}, f16[512,512]{0,1:T(8,128)(2,1)S(1)}, u32[]{:S(2)}, u32[]{:S(2)}) collective-permute-start(f16[512,512]{0,1:T(8,128)(2,1)S(1)} %fusion.27), channel_id=1, source_target_pairs={{0,8},{8,16},{16,24},{24,28},{28,20},{20,12},{12,4},{4,0},{1,9},{9... | collective-permute-start | bytes 1572872 | tf_op jit(solution)/shard_map/ppermute | solution.py:67
  63.7 21.6 %collective-permute-start.17 = (f16[512,512]{0,1:T(8,128)(2,1)S(1)}, f16[512,512]{0,1:T(8,128)(2,1)S(1)}, u32[]{:S(2)}, u32[]{:S(2)}) collective-permute-start(f16[512,512]{0,1:T(8,128)(2,1)S(1)} %fusion.60), channel_id=1, source_target_pairs={{8,0},{16,8},{24,16},{28,24},{20,28},{12,20},{4,12},{0,4},{9,1},{1... | collective-permute-start | bytes 1572872 | tf_op jit(solution)/shard_map/ppermute | solution.py:72
  70.1 21.8 %collective-permute-start.6 = (f16[512,512]{0,1:T(8,128)(2,1)S(1)}, f16[512,512]{0,1:T(8,128)(2,1)S(1)}, u32[]{:S(2)}, u32[]{:S(2)}) collective-permute-start(f16[512,512]{0,1:T(8,128)(2,1)S(1)} %fusion.41), channel_id=1, source_target_pairs={{8,0},{16,8},{24,16},{28,24},{20,28},{12,20},{4,12},{0,4},{9,1},{1... | collective-permute-start | bytes 1572872 | tf_op jit(solution)/shard_map/ppermute | solution.py:72
  82.5 14.9 %collective-permute-start.3 = (f16[512,512]{0,1:T(8,128)(2,1)S(1)}, f16[512,512]{0,1:T(8,128)(2,1)S(1)}, u32[]{:S(2)}, u32[]{:S(2)}) collective-permute-start(f16[512,512]{0,1:T(8,128)(2,1)S(1)} %fusion.30), channel_id=1, source_target_pairs={{0,8},{8,16},{16,24},{24,28},{28,20},{20,12},{12,4},{4,0},{1,9},{9... | collective-permute-start | bytes 1572872 | tf_op jit(solution)/shard_map/ppermute | solution.py:67
  83.7 25.0 %collective-permute-start.14 = (f16[512,512]{0,1:T(8,128)(2,1)S(1)}, f16[512,512]{0,1:T(8,128)(2,1)S(1)}, u32[]{:S(2)}, u32[]{:S(2)}) collective-permute-start(f16[512,512]{0,1:T(8,128)(2,1)S(1)} %fusion.49), channel_id=1, source_target_pairs={{0,8},{8,16},{16,24},{24,28},{28,20},{20,12},{12,4},{4,0},{1,9},{9... | collective-permute-start | bytes 1572872 | tf_op jit(solution)/shard_map/ppermute | solution.py:67
  86.0 22.7 %collective-permute-start.18 = (f16[512,512]{0,1:T(8,128)(2,1)S(1)}, f16[512,512]{0,1:T(8,128)(2,1)S(1)}, u32[]{:S(2)}, u32[]{:S(2)}) collective-permute-start(f16[512,512]{0,1:T(8,128)(2,1)S(1)} %fusion.63), channel_id=1, source_target_pairs={{8,0},{16,8},{24,16},{28,24},{20,28},{12,20},{4,12},{0,4},{9,1},{1... | collective-permute-start | bytes 1572872 | tf_op jit(solution)/shard_map/ppermute | solution.py:72
  98.6 13.0 %collective-permute-start.7 = (bf16[512,512]{0,1:T(8,128)(2,1)S(1)}, bf16[512,512]{0,1:T(8,128)(2,1)S(1)}, u32[]{:S(2)}, u32[]{:S(2)}) collective-permute-start(bf16[512,512]{0,1:T(8,128)(2,1)S(1)} %get-tuple-element.31), channel_id=1, source_target_pairs={{8,0},{16,8},{24,16},{28,24},{20,28},{12,20},{4,12},{0,4},{9,1},{1... | collective-permute-start | bytes 1572872 | tf_op jit(solution)/shard_map/ppermute | solution.py:72
  100.2 16.2 %collective-permute-start.8 = (bf16[512,512]{0,1:T(8,128)(2,1)S(1)}, bf16[512,512]{0,1:T(8,128)(2,1)S(1)}, u32[]{:S(2)}, u32[]{:S(2)}) collective-permute-start(bf16[512,512]{0,1:T(8,128)(2,1)S(1)} %get-tuple-element.31), channel_id=1, source_target_pairs={{0,8},{8,16},{16,24},{24,28},{28,20},{20,12},{12,4},{4,0},{1,9},{9... | collective-permute-start | bytes 1572872 | tf_op jit(solution)/shard_map/ppermute | solution.py:67
  100.7 15.7 %collective-permute-start.9 = (bf16[512,512]{0,1:T(8,128)(2,1)S(1)}, bf16[512,512]{0,1:T(8,128)(2,1)S(1)}, u32[]{:S(2)}, u32[]{:S(2)}) collective-permute-start(bf16[512,512]{0,1:T(8,128)(2,1)S(1)} %get-tuple-element.31), channel_id=1, source_target_pairs={{0,2},{1,3},{2,0},{3,1},{4,6},{5,7},{6,4},{7,5},{8,10},{9,11},{10,... | collective-permute-start | bytes 1572872 | tf_op jit(solution)/shard_map/ppermute | solution.py:80
  111.6 18.4 %copy-start.18 = (bf16[512,512]{0,1:T(8,128)(2,1)}, bf16[512,512]{0,1:T(8,128)(2,1)S(1)}, u32[]{:S(2)}) copy-start(bf16[512,512]{0,1:T(8,128)(2,1)S(1)} %collective-permute-done.7) | copy-start | bytes 1572868
  116.4 13.5 %copy-start.8 = (bf16[512,512]{0,1:T(8,128)(2,1)}, bf16[512,512]{0,1:T(8,128)(2,1)S(1)}, u32[]{:S(2)}) copy-start(bf16[512,512]{0,1:T(8,128)(2,1)S(1)} %collective-permute-done.9) | copy-start | bytes 1572868
  116.4 10.5 %collective-permute-start.10 = (bf16[512,512]{0,1:T(8,128)(2,1)S(1)}, bf16[512,512]{0,1:T(8,128)(2,1)}, u32[]{:S(2)}, u32[]{:S(2)}) collective-permute-start(bf16[512,512]{0,1:T(8,128)(2,1)S(1)} %collective-permute-done.7), channel_id=1, source_target_pairs={{8,0},{16,8},{24,16},{28,24},{20,28},{12,20},{4,12},{0,4},{9,1},{1... | collective-permute-start | bytes 1572872 | tf_op jit(solution)/shard_map/ppermute | solution.py:72
  118.0 11.9 %collective-permute-start.11 = (bf16[512,512]{0,1:T(8,128)(2,1)S(1)}, bf16[512,512]{0,1:T(8,128)(2,1)S(1)}, u32[]{:S(2)}, u32[]{:S(2)}) collective-permute-start(bf16[512,512]{0,1:T(8,128)(2,1)S(1)} %collective-permute-done.8), channel_id=1, source_target_pairs={{0,8},{8,16},{16,24},{24,28},{28,20},{20,12},{12,4},{4,0},{1,9},{9... | collective-permute-start | bytes 1572872 | tf_op jit(solution)/shard_map/ppermute | solution.py:67
  118.4 11.5 %collective-permute-start.19 = (bf16[512,512]{0,1:T(8,128)(2,1)S(1)}, bf16[512,512]{0,1:T(8,128)(2,1)S(1)}, u32[]{:S(2)}, u32[]{:S(2)}) collective-permute-start(bf16[512,512]{0,1:T(8,128)(2,1)S(1)} %fusion.53), channel_id=1, source_target_pairs={{0,2},{1,3},{2,0},{3,1},{4,6},{5,7},{6,4},{7,5},{8,10},{9,11},{10,... | collective-permute-start | bytes 1572872 | tf_op jit(solution)/shard_map/ppermute | solution.py:80
  129.9 9.4 %collective-permute-start.21 = (bf16[512,512]{0,1:T(8,128)(2,1)S(1)}, bf16[512,512]{0,1:T(8,128)(2,1)S(1)}, u32[]{:S(2)}, u32[]{:S(2)}) collective-permute-start(bf16[512,512]{0,1:T(8,128)(2,1)S(1)} %collective-permute-done.11), channel_id=1, source_target_pairs={{0,8},{8,16},{16,24},{24,28},{28,20},{20,12},{12,4},{4,0},{1,9},{9... | collective-permute-start | bytes 1572872 | tf_op jit(solution)/shard_map/ppermute | solution.py:67
  130.7 10.1 %collective-permute-start.20 = (bf16[512,512]{0,1:T(8,128)(2,1)}, bf16[512,512]{0,1:T(8,128)(2,1)S(1)}, u32[]{:S(2)}, u32[]{:S(2)}) collective-permute-start(bf16[512,512]{0,1:T(8,128)(2,1)} %collective-permute-done.10), channel_id=1, source_target_pairs={{8,0},{16,8},{24,16},{28,24},{20,28},{12,20},{4,12},{0,4},{9,1},{1... | collective-permute-start | bytes 1572872 | tf_op jit(solution)/shard_map/ppermute | solution.py:72
  132.4 27.3 %collective-permute-start.50 = (bf16[512,512]{0,1:T(8,128)(2,1)S(1)}, bf16[512,512]{0,1:T(8,128)(2,1)}, u32[]{:S(2)}, u32[]{:S(2)}) collective-permute-start(bf16[512,512]{0,1:T(8,128)(2,1)S(1)} %get-tuple-element.31), channel_id=1, source_target_pairs={{0,1},{1,0},{2,3},{3,2},{4,5},{5,4},{6,7},{7,6},{8,9},{9,8},{10,11... | collective-permute-start | bytes 1572872 | tf_op jit(solution)/shard_map/ppermute | solution.py:80
  140.8 6.4 %collective-permute-start.23 = (bf16[256,512]{0,1:T(8,128)(2,1)S(1)}, bf16[256,512]{0,1:T(8,128)(2,1)S(1)}, u32[]{:S(2)}, u32[]{:S(2)}) collective-permute-start(bf16[256,512]{0,1:T(8,128)(2,1)S(1)} %slice.87), channel_id=1, source_target_pairs={{8,0},{16,8},{24,16},{28,24},{20,28},{12,20},{4,12},{0,4},{9,1},{1... | collective-permute-start | bytes 786440 | tf_op jit(solution)/shard_map/ppermute | solution.py:72
  142.4 6.6 %collective-permute-start.22 = (bf16[256,512]{0,1:T(8,128)(2,1)S(1)}, bf16[256,512]{0,1:T(8,128)(2,1)S(1)}, u32[]{:S(2)}, u32[]{:S(2)}) collective-permute-start(bf16[256,512]{0,1:T(8,128)(2,1)S(1)} %slice.86), channel_id=1, source_target_pairs={{0,8},{8,16},{16,24},{24,28},{28,20},{20,12},{12,4},{4,0},{1,9},{9... | collective-permute-start | bytes 786440 | tf_op jit(solution)/shard_map/ppermute | solution.py:67
  150.2 9.5 %collective-permute-start.25 = (bf16[512,512]{0,1:T(8,128)(2,1)}, bf16[512,512]{0,1:T(8,128)(2,1)}, u32[]{:S(2)}, u32[]{:S(2)}) collective-permute-start(bf16[512,512]{0,1:T(8,128)(2,1)} %dynamic-slice_bitcast_fusion.8), channel_id=1, source_target_pairs={{0,2},{1,3},{2,0},{3,1},{4,6},{5,7},{6,4},{7,5},{8,10},{9,11},{10,... | collective-permute-start | bytes 1572872 | tf_op jit(solution)/shard_map/ppermute | solution.py:80
  153.0 8.7 %collective-permute-start.27 = (bf16[512,512]{0,1:T(8,128)(2,1)S(1)}, bf16[512,512]{0,1:T(8,128)(2,1)}, u32[]{:S(2)}, u32[]{:S(2)}) collective-permute-start(bf16[512,512]{0,1:T(8,128)(2,1)S(1)} %get-tuple-element.61), channel_id=1, source_target_pairs={{0,1},{1,0},{2,3},{3,2},{4,5},{5,4},{6,7},{7,6},{8,9},{9,8},{10,11... | collective-permute-start | bytes 1572872 | tf_op jit(solution)/shard_map/ppermute | solution.py:80
  153.0 10.9 %copy-start.2 = (bf16[512,512]{0,1:T(8,128)(2,1)S(1)}, bf16[512,512]{0,1:T(8,128)(2,1)}, u32[]{:S(2)}) copy-start(bf16[512,512]{0,1:T(8,128)(2,1)} %get-tuple-element.43) | copy-start | bytes 1572868
  153.0 81.1 %collective-permute-start.52 = (bf16[512,512]{0,1:T(8,128)(2,1)S(1)}, bf16[512,512]{0,1:T(8,128)(2,1)S(1)}, u32[]{:S(2)}, u32[]{:S(2)}) collective-permute-start(bf16[512,512]{0,1:T(8,128)(2,1)S(1)} %fusion.53), channel_id=1, source_target_pairs={{0,1},{1,0},{2,3},{3,2},{4,5},{5,4},{6,7},{7,6},{8,9},{9,8},{10,11... | collective-permute-start | bytes 1572872 | tf_op jit(solution)/shard_map/ppermute | solution.py:80
  153.5 68.4 %collective-permute-start.51 = (bf16[512,512]{0,1:T(8,128)(2,1)}, bf16[512,512]{0,1:T(8,128)(2,1)S(1)}, u32[]{:S(2)}, u32[]{:S(2)}) collective-permute-start(bf16[512,512]{0,1:T(8,128)(2,1)} %copy-done.8), channel_id=1, source_target_pairs={{0,1},{1,0},{2,3},{3,2},{4,5},{5,4},{6,7},{7,6},{8,9},{9,8},{10,11... | collective-permute-start | bytes 1572872 | tf_op jit(solution)/shard_map/ppermute | solution.py:80
  159.7 4.2 %collective-permute-start.24 = (bf16[512,512]{0,1:T(8,128)(2,1)}, bf16[512,512]{0,1:T(8,128)(2,1)S(1)}, u32[]{:S(2)}, u32[]{:S(2)}) collective-permute-start(bf16[512,512]{0,1:T(8,128)(2,1)} %get-tuple-element.64), channel_id=1, source_target_pairs={{0,1},{1,0},{2,3},{3,2},{4,5},{5,4},{6,7},{7,6},{8,9},{9,8},{10,11... | collective-permute-start | bytes 1572872 | tf_op jit(solution)/shard_map/ppermute | solution.py:80
  159.7 14.3 %collective-permute-start.29 = (bf16[512,512]{0,1:T(8,128)(2,1)S(1)}, bf16[512,512]{0,1:T(8,128)(2,1)S(1)}, u32[]{:S(2)}, u32[]{:S(2)}) collective-permute-start(bf16[512,512]{0,1:T(8,128)(2,1)S(1)} %fusion.53), channel_id=1, source_target_pairs={{8,0},{16,8},{24,16},{28,24},{20,28},{12,20},{4,12},{0,4},{9,1},{1... | collective-permute-start | bytes 1572872 | tf_op jit(solution)/shard_map/ppermute | solution.py:72
  161.7 14.1 %collective-permute-start.28 = (bf16[512,512]{0,1:T(8,128)(2,1)S(1)}, bf16[512,512]{0,1:T(8,128)(2,1)S(1)}, u32[]{:S(2)}, u32[]{:S(2)}) collective-permute-start(bf16[512,512]{0,1:T(8,128)(2,1)S(1)} %fusion.53), channel_id=1, source_target_pairs={{0,8},{8,16},{16,24},{24,28},{28,20},{20,12},{12,4},{4,0},{1,9},{9... | collective-permute-start | bytes 1572872 | tf_op jit(solution)/shard_map/ppermute | solution.py:67
  163.9 16.2 %copy-start.1 = (bf16[512,512]{0,1:T(8,128)(2,1)S(1)}, bf16[512,512]{0,1:T(8,128)(2,1)}, u32[]{:S(2)}) copy-start(bf16[512,512]{0,1:T(8,128)(2,1)} %get-tuple-element.46) | copy-start | bytes 1572868
  163.9 14.0 %collective-permute-start.26 = (bf16[512,512]{0,1:T(8,128)(2,1)S(1)}, bf16[512,512]{0,1:T(8,128)(2,1)S(1)}, u32[]{:S(2)}, u32[]{:S(2)}) collective-permute-start(bf16[512,512]{0,1:T(8,128)(2,1)S(1)} %copy-done.2), channel_id=1, source_target_pairs={{0,3},{1,2},{2,1},{3,0},{4,7},{5,6},{6,5},{7,4},{8,11},{9,10},{10,... | collective-permute-start | bytes 1572872 | tf_op jit(solution)/shard_map/ppermute | solution.py:80
  177.9 14.0 %collective-permute-start.32 = (bf16[512,512]{0,1:T(8,128)(2,1)S(1)}, bf16[512,512]{0,1:T(8,128)(2,1)S(1)}, u32[]{:S(2)}, u32[]{:S(2)}) collective-permute-start(bf16[512,512]{0,1:T(8,128)(2,1)S(1)} %collective-permute-done.29), channel_id=1, source_target_pairs={{8,0},{16,8},{24,16},{28,24},{20,28},{12,20},{4,12},{0,4},{9,1},{1... | collective-permute-start | bytes 1572872 | tf_op jit(solution)/shard_map/ppermute | solution.py:72
  180.1 13.8 %collective-permute-start.31 = (bf16[512,512]{0,1:T(8,128)(2,1)S(1)}, bf16[512,512]{0,1:T(8,128)(2,1)S(1)}, u32[]{:S(2)}, u32[]{:S(2)}) collective-permute-start(bf16[512,512]{0,1:T(8,128)(2,1)S(1)} %collective-permute-done.28), channel_id=1, source_target_pairs={{0,8},{8,16},{16,24},{24,28},{28,20},{20,12},{12,4},{4,0},{1,9},{9... | collective-permute-start | bytes 1572872 | tf_op jit(solution)/shard_map/ppermute | solution.py:67
  180.1 26.7 %copy-start.11 = (bf16[512,512]{0,1:T(8,128)(2,1)S(1)}, bf16[512,512]{0,1:T(8,128)(2,1)}, u32[]{:S(2)}) copy-start(bf16[512,512]{0,1:T(8,128)(2,1)} %copy-done.10) | copy-start | bytes 1572868
  180.1 13.8 %collective-permute-start.30 = (bf16[512,512]{0,1:T(8,128)(2,1)S(1)}, bf16[512,512]{0,1:T(8,128)(2,1)S(1)}, u32[]{:S(2)}, u32[]{:S(2)}) collective-permute-start(bf16[512,512]{0,1:T(8,128)(2,1)S(1)} %copy-done.1), channel_id=1, source_target_pairs={{0,2},{1,3},{2,0},{3,1},{4,6},{5,7},{6,4},{7,5},{8,10},{9,11},{10,... | collective-permute-start | bytes 1572872 | tf_op jit(solution)/shard_map/ppermute | solution.py:80
  193.8 12.9 %collective-permute-start.35 = (bf16[512,512]{0,1:T(8,128)(2,1)S(1)}, bf16[512,512]{0,1:T(8,128)(2,1)S(1)}, u32[]{:S(2)}, u32[]{:S(2)}) collective-permute-start(bf16[512,512]{0,1:T(8,128)(2,1)S(1)} %collective-permute-done.32), channel_id=1, source_target_pairs={{8,0},{16,8},{24,16},{28,24},{20,28},{12,20},{4,12},{0,4},{9,1},{1... | collective-permute-start | bytes 1572872 | tf_op jit(solution)/shard_map/ppermute | solution.py:72
  195.6 12.4 %collective-permute-start.36 = (bf16[512,512]{0,1:T(8,128)(2,1)S(1)}, bf16[512,512]{0,1:T(8,128)(2,1)S(1)}, u32[]{:S(2)}, u32[]{:S(2)}) collective-permute-start(bf16[512,512]{0,1:T(8,128)(2,1)S(1)} %collective-permute-done.31), channel_id=1, source_target_pairs={{0,8},{8,16},{16,24},{24,28},{28,20},{20,12},{12,4},{4,0},{1,9},{9... | collective-permute-start | bytes 1572872 | tf_op jit(solution)/shard_map/ppermute | solution.py:67
  195.9 14.2 %collective-permute-start.33 = (bf16[512,512]{0,1:T(8,128)(2,1)S(1)}, bf16[512,512]{0,1:T(8,128)(2,1)S(1)}, u32[]{:S(2)}, u32[]{:S(2)}) collective-permute-start(bf16[512,512]{0,1:T(8,128)(2,1)S(1)} %get-tuple-element.49), channel_id=1, source_target_pairs={{0,3},{1,2},{2,1},{3,0},{4,7},{5,6},{6,5},{7,4},{8,11},{9,10},{10,... | collective-permute-start | bytes 1572872 | tf_op jit(solution)/shard_map/ppermute | solution.py:80
  206.7 60.7 %collective-permute-start.53 = (bf16[512,512]{0,1:T(8,128)(2,1)S(1)}, bf16[512,512]{0,1:T(8,128)(2,1)S(1)}, u32[]{:S(2)}, u32[]{:S(2)}) collective-permute-start(bf16[512,512]{0,1:T(8,128)(2,1)S(1)} %copy-done.11), channel_id=1, source_target_pairs={{0,1},{1,0},{2,3},{3,2},{4,5},{5,4},{6,7},{7,6},{8,9},{9,8},{10,11... | collective-permute-start | bytes 1572872 | tf_op jit(solution)/shard_map/ppermute | solution.py:80
  210.0 8.3 %collective-permute-start.38 = (bf16[256,512]{0,1:T(8,128)(2,1)S(1)}, bf16[256,512]{0,1:T(8,128)(2,1)S(1)}, u32[]{:S(2)}, u32[]{:S(2)}) collective-permute-start(bf16[256,512]{0,1:T(8,128)(2,1)S(1)} %slice.91), channel_id=1, source_target_pairs={{8,0},{16,8},{24,16},{28,24},{20,28},{12,20},{4,12},{0,4},{9,1},{1... | collective-permute-start | bytes 786440 | tf_op jit(solution)/shard_map/ppermute | solution.py:72
  211.9 8.4 %collective-permute-start.37 = (bf16[256,512]{0,1:T(8,128)(2,1)S(1)}, bf16[256,512]{0,1:T(8,128)(2,1)S(1)}, u32[]{:S(2)}, u32[]{:S(2)}) collective-permute-start(bf16[256,512]{0,1:T(8,128)(2,1)S(1)} %slice.90), channel_id=1, source_target_pairs={{0,8},{8,16},{16,24},{24,28},{28,20},{20,12},{12,4},{4,0},{1,9},{9... | collective-permute-start | bytes 786440 | tf_op jit(solution)/shard_map/ppermute | solution.py:67
  218.4 5.3 %collective-permute-start.34 = (bf16[2,256,512]{1,2,0:T(8,128)(2,1)S(1)}, bf16[2,256,512]{1,2,0:T(8,128)(2,1)S(1)}, u32[]{:S(2)}, u32[]{:S(2)}) collective-permute-start(bf16[2,256,512]{1,2,0:T(8,128)(2,1)S(1)} %pad_maximum_fusion.2), channel_id=1, source_target_pairs={{0,1},{1,0},{2,3},{3,2},{4,5},{5,4},{6,7},{7,6},{8,9},{9,8},{10,11... | collective-permute-start | bytes 1572872 | tf_op jit(solution)/shard_map/ppermute | solution.py:80
  220.9 12.9 %collective-permute-start.39 = (bf16[512,512]{0,1:T(8,128)(2,1)S(1)}, bf16[512,512]{0,1:T(8,128)(2,1)S(1)}, u32[]{:S(2)}, u32[]{:S(2)}) collective-permute-start(bf16[512,512]{0,1:T(8,128)(2,1)S(1)} %dynamic-slice_bitcast_fusion.2), channel_id=1, source_target_pairs={{0,2},{1,3},{2,0},{3,1},{4,6},{5,7},{6,4},{7,5},{8,10},{9,11},{10,... | collective-permute-start | bytes 1572872 | tf_op jit(solution)/shard_map/ppermute | solution.py:80
  221.9 13.9 %collective-permute-start.44 = (bf16[512,512]{0,1:T(8,128)(2,1)S(1)}, bf16[512,512]{0,1:T(8,128)(2,1)S(1)}, u32[]{:S(2)}, u32[]{:S(2)}) collective-permute-start(bf16[512,512]{0,1:T(8,128)(2,1)S(1)} %get-tuple-element.66), channel_id=1, source_target_pairs={{0,1},{1,0},{2,3},{3,2},{4,5},{5,4},{6,7},{7,6},{8,9},{9,8},{10,11... | collective-permute-start | bytes 1572872 | tf_op jit(solution)/shard_map/ppermute | solution.py:80
  223.7 25.3 %collective-permute-start.43 = (bf16[512,512]{0,1:T(8,128)(2,1)S(1)}, bf16[512,512]{0,1:T(8,128)(2,1)S(1)}, u32[]{:S(2)}, u32[]{:S(2)}) collective-permute-start(bf16[512,512]{0,1:T(8,128)(2,1)S(1)} %get-tuple-element.68), channel_id=1, source_target_pairs={{0,1},{1,0},{2,3},{3,2},{4,5},{5,4},{6,7},{7,6},{8,9},{9,8},{10,11... | collective-permute-start | bytes 1572872 | tf_op jit(solution)/shard_map/ppermute | solution.py:80
  233.7 13.1 %collective-permute-start.40 = (bf16[512,512]{0,1:T(8,128)(2,1)S(1)}, bf16[512,512]{0,1:T(8,128)(2,1)S(1)}, u32[]{:S(2)}, u32[]{:S(2)}) collective-permute-start(bf16[512,512]{0,1:T(8,128)(2,1)S(1)} %get-tuple-element.53), channel_id=1, source_target_pairs={{0,3},{1,2},{2,1},{3,0},{4,7},{5,6},{6,5},{7,4},{8,11},{9,10},{10,... | collective-permute-start | bytes 1572872 | tf_op jit(solution)/shard_map/ppermute | solution.py:80
  234.1 16.8 %collective-permute-start.45 = (bf16[512,512]{0,1:T(8,128)(2,1)S(1)}, bf16[512,512]{0,1:T(8,128)(2,1)S(1)}, u32[]{:S(2)}, u32[]{:S(2)}) collective-permute-start(bf16[512,512]{0,1:T(8,128)(2,1)S(1)} %collective-permute-done.39), channel_id=1, source_target_pairs={{0,4},{4,0},{8,12},{12,8},{16,20},{20,16},{24,28},{28,24},{1,5},{5... | collective-permute-start | bytes 1572872 | tf_op jit(solution)/shard_map/ppermute | solution.py:77
  246.8 12.9 %collective-permute-start.46 = (bf16[512,512]{0,1:T(8,128)(2,1)S(1)}, bf16[512,512]{0,1:T(8,128)(2,1)S(1)}, u32[]{:S(2)}, u32[]{:S(2)}) collective-permute-start(bf16[512,512]{0,1:T(8,128)(2,1)S(1)} %collective-permute-done.40), channel_id=1, source_target_pairs={{0,4},{4,0},{8,12},{12,8},{16,20},{20,16},{24,28},{28,24},{1,5},{5... | collective-permute-start | bytes 1572872 | tf_op jit(solution)/shard_map/ppermute | solution.py:77
  249.5 13.5 %collective-permute-start.41 = (bf16[2,256,512]{1,2,0:T(8,128)(2,1)S(1)}, bf16[2,256,512]{1,2,0:T(8,128)(2,1)S(1)}, u32[]{:S(2)}, u32[]{:S(2)}) collective-permute-start(bf16[2,256,512]{1,2,0:T(8,128)(2,1)S(1)} %pad_maximum_fusion.2), channel_id=1, source_target_pairs={{0,2},{1,3},{2,0},{3,1},{4,6},{5,7},{6,4},{7,5},{8,10},{9,11},{10,... | collective-permute-start | bytes 1572872 | tf_op jit(solution)/shard_map/ppermute | solution.py:80
  259.9 19.3 %collective-permute-start.47 = (bf16[2,256,512]{1,2,0:T(8,128)(2,1)S(1)}, bf16[2,256,512]{1,2,0:T(8,128)(2,1)S(1)}, u32[]{:S(2)}, u32[]{:S(2)}) collective-permute-start(bf16[2,256,512]{1,2,0:T(8,128)(2,1)S(1)} %pad_maximum_fusion.3), channel_id=1, source_target_pairs={{0,1},{1,0},{2,3},{3,2},{4,5},{5,4},{6,7},{7,6},{8,9},{9,8},{10,11... | collective-permute-start | bytes 1572872 | tf_op jit(solution)/shard_map/ppermute | solution.py:80
  262.9 13.2 %collective-permute-start.48 = (bf16[2,256,512]{1,2,0:T(8,128)(2,1)S(1)}, bf16[2,256,512]{1,2,0:T(8,128)(2,1)S(1)}, u32[]{:S(2)}, u32[]{:S(2)}) collective-permute-start(bf16[2,256,512]{1,2,0:T(8,128)(2,1)S(1)} %pad_maximum_fusion.3), channel_id=1, source_target_pairs={{0,2},{1,3},{2,0},{3,1},{4,6},{5,7},{6,4},{7,5},{8,10},{9,11},{10,... | collective-permute-start | bytes 1572872 | tf_op jit(solution)/shard_map/ppermute | solution.py:80
  264.6 12.5 %collective-permute-start.42 = (bf16[2,256,512]{1,2,0:T(8,128)(2,1)S(1)}, bf16[2,256,512]{1,2,0:T(8,128)(2,1)S(1)}, u32[]{:S(2)}, u32[]{:S(2)}) collective-permute-start(bf16[2,256,512]{1,2,0:T(8,128)(2,1)S(1)} %collective-permute-done.41), channel_id=1, source_target_pairs={{0,1},{1,0},{2,3},{3,2},{4,5},{5,4},{6,7},{7,6},{8,9},{9,8},{10,11... | collective-permute-start | bytes 1572872 | tf_op jit(solution)/shard_map/ppermute | solution.py:80
  276.1 6.4 %collective-permute-start.49 = (bf16[2,256,512]{1,2,0:T(8,128)(2,1)S(1)}, bf16[2,256,512]{1,2,0:T(8,128)(2,1)S(1)}, u32[]{:S(2)}, u32[]{:S(2)}) collective-permute-start(bf16[2,256,512]{1,2,0:T(8,128)(2,1)S(1)} %collective-permute-done.48), channel_id=1, source_target_pairs={{0,1},{1,0},{2,3},{3,2},{4,5},{5,4},{6,7},{7,6},{8,9},{9,8},{10,11... | collective-permute-start | bytes 1572872 | tf_op jit(solution)/shard_map/ppermute | solution.py:80
  (9 other events, 19.2 us)

commit v2 on v0

v2 whole, which is shorter than its diff:
```python
import functools

import jax
import jax.numpy as jnp
from jax import lax
from jax.experimental import pallas as pl
from jax.experimental.pallas import tpu as pltpu
from jax.sharding import PartitionSpec as P

ema_decay = 0.95
halves = 2
wire_gain = 2.0**20
kernel_vmem = 32 * 2**20
large_vmem = 56 * 2**20


def to_wire(value):
    scaled = value * wire_gain
    square = scaled * scaled
    return (scaled * jnp.abs(scaled) * square).astype(jnp.bfloat16)


def from_wire(sent):
    power = sent.astype(jnp.float32)
    root = lax.rsqrt(lax.rsqrt(jnp.abs(power))) * (1.0 / wire_gain)
    return jnp.where(power < 0, -root, root)


def after(values, *done):
    return lax.optimization_barrier((values, done))[0]


def sum_body(counts, parts, turned, slabs, tokens, first, second, *rest):
    arrived, outs = rest[: sum(counts)], rest[sum(counts) :]
    contracted = 1 if turned else 0
    for k, grads in enumerate((first, second)):
        total = lax.dot_general(
            tokens[...],
            grads[...],
            (((contracted,), (0,)), ((), ())),
            preferred_element_type=jnp.float32,
        )
        across = outs[k].shape[1]
        if total.shape[1] != across:
            total = total[:, parts[k] * across : (parts[k] + 1) * across]
        for ref in arrived[sum(counts[:k]) : sum(counts[: k + 1])]:
            total = total + from_wire(ref[...])
        outs[k][...] = to_wire(total) if outs[k].dtype == jnp.bfloat16 else total


def sum_round(slabs, tokens, turned, grads, half, picks, arrived, kind=jnp.bfloat16):
    rows, depth = tokens.shape if turned else tokens.shape[::-1]
    high = rows // 2 if rows % 512 == 0 else rows
    wide = half if half % 128 == 0 else half * halves
    per_slab = half * halves // wide
    parts = [part for _, part in picks]

    def grad_block(ahead, part):
        return pl.BlockSpec(
            (depth, wide), lambda i, s: (0, s[ahead] * per_slab + part % per_slab)
        )

    if turned:
        token_block = pl.BlockSpec((high, depth), lambda i, s: (i, 0))
    else:
        token_block = pl.BlockSpec((depth, high), lambda i, s: (0, i))
    block = pl.BlockSpec((high, half), lambda i, s: (i, 0))
    counts = tuple(len(a) for a in arrived)
    flat = [a for group in arrived for a in group]
    return pl.pallas_call(
        functools.partial(sum_body, counts, parts, turned),
        out_shape=[jax.ShapeDtypeStruct((rows, half), kind)] * 2,
        grid_spec=pltpu.PrefetchScalarGridSpec(
            num_scalar_prefetch=1,
            grid=(rows // high,),
            in_specs=[token_block] + [grad_block(*pick) for pick in picks] + [block] * len(flat),
            out_specs=[block] * 2,
        ),
        compiler_params=pltpu.CompilerParams(vmem_limit_bytes=kernel_vmem if turned else large_vmem),
        cost_estimate=pl.CostEstimate(
            flops=4 * half * depth * rows,
            bytes_accessed=2 * depth * rows + 4 * depth * half + 4 * half * rows * 2,
            transcendentals=0,
        ),
    )(slabs, tokens, grads, grads, *flat)


def block_spec(block, shape, where):
    array, index = block
    if index is None:
        return pl.BlockSpec(shape, where)
    return pl.BlockSpec((None, *shape), lambda *args: (index, *where(*args)))


def alone(block):
    array, index = block
    return array if index is None else array[index]


def pick_body(cases, count, spots, *refs):
    sources, out, sems = refs[:cases], refs[cases], refs[-1]
    for k in range(count):
        for c in range(cases):

            @pl.when(spots[k] == c)
            def _():
                pltpu.make_async_copy(sources[c], out.at[k], sems.at[k]).start()

    for k in range(count):
        pltpu.make_async_copy(sources[0], out.at[k], sems.at[k]).wait()


def pick_blocks(spots, cases):
    count = spots.shape[0]
    shape = (count, *cases[0].shape)
    return pl.pallas_call(
        functools.partial(pick_body, len(cases), count),
        out_shape=jax.ShapeDtypeStruct(shape, cases[0].dtype),
        grid_spec=pltpu.PrefetchScalarGridSpec(
            num_scalar_prefetch=1,
            grid=(1,),
            in_specs=[pl.BlockSpec(memory_space=pl.ANY)] * len(cases),
            out_specs=pl.BlockSpec(shape, lambda i, s: (0, 0, 0)),
            scratch_shapes=[pltpu.SemaphoreType.DMA((count,))],
        ),
        compiler_params=pltpu.CompilerParams(vmem_limit_bytes=kernel_vmem),
        cost_estimate=pl.CostEstimate(
            flops=0, bytes_accessed=4 * count * cases[0].size, transcendentals=0
        ),
    )(spots, *cases)


def rows_body(views, pair, high, spots, *refs):
    sources, out, sems = refs[: len(views)], refs[-2], refs[-1]
    start = pl.multiple_of(spots[1] * high, high)

    def rows(k, first):
        if views[k] is None:
            return sources[k].at[pl.ds(first, high)]
        return sources[k].at[views[k], pl.ds(first, high)]

    for r in range(pair):
        for c in range(len(views) // pair):

            @pl.when(spots[0] == c)
            def _():
                copied = rows(c * pair + r, start)
                pltpu.make_async_copy(copied, out.at[r], sems.at[r]).start()

    for r in range(pair):
        pltpu.make_async_copy(rows(r, 0), out.at[r], sems.at[r]).wait()


def pick_rows(spots, cases, pair, high):
    across, kind = cases[0][0].shape[-1], cases[0][0].dtype
    shape = (pair, high, across)
    return pl.pallas_call(
        functools.partial(rows_body, [view for _, view in cases], pair, high),
        out_shape=jax.ShapeDtypeStruct(shape, kind),
        grid_spec=pltpu.PrefetchScalarGridSpec(
            num_scalar_prefetch=1,
            grid=(1,),
            in_specs=[pl.BlockSpec(memory_space=pl.ANY)] * len(cases),
            out_specs=pl.BlockSpec(shape, lambda i, s: (0, 0, 0)),
            scratch_shapes=[pltpu.SemaphoreType.DMA((pair,))],
        ),
        compiler_params=pltpu.CompilerParams(vmem_limit_bytes=kernel_vmem),
        cost_estimate=pl.CostEstimate(
            flops=0, bytes_accessed=4 * pair * high * across, transcendentals=0
        ),
    )(spots, *[array for array, _ in cases])


def left_body(count, pair, final, *refs):
    blocks, theirs = refs[: count * pair], refs[count * pair : count * pair + count]
    rest = refs[count * pair + count :]
    total = rest[0][...] if len(rest) > 1 else 0.0
    for j in range(count):
        for r in range(pair):
            total = total + lax.dot_general(
                blocks[j * pair + r][...],
                theirs[j][r],
                (((1,), (1,)), ((), ())),
                preferred_element_type=jnp.float32,
            )
    if final:
        total = ema_decay * rest[1][...] + (1.0 - ema_decay) * total
    rest[-1][...] = total


def left_sum(blocks, theirs, earlier, final=False):
    rows, across = blocks[0][0].shape[-2:]
    width = theirs[0].shape[1]
    high = rows // 2 if rows % 512 == 0 else rows
    pair = len(blocks) // len(theirs)
    out = pl.BlockSpec((high, width), lambda i: (i, 0))
    return pl.pallas_call(
        functools.partial(left_body, len(theirs), pair, final),
        out_shape=jax.ShapeDtypeStruct((rows, width), jnp.float32),
        grid=(rows // high,),
        in_specs=[block_spec(b, (high, across), lambda i: (i, 0)) for b in blocks]
        + [pl.BlockSpec(theirs[0].shape, lambda i: (0, 0, 0))] * len(theirs)
        + [out] * len(earlier),
        out_specs=out,
        compiler_params=pltpu.CompilerParams(vmem_limit_bytes=large_vmem),
        cost_estimate=pl.CostEstimate(
            flops=2 * len(blocks) * across * rows * width,
            bytes_accessed=2 * len(blocks) * across * (rows + width) + 8 * rows * width,
            transcendentals=0,
        ),
    )(*[b for b, _ in blocks], *theirs, *earlier)


def turn_body(count, *refs):
    for k in range(count):
        refs[count + k][...] = refs[k][...].T


def turn_blocks(blocks):
    rows, across = blocks[0].shape
    high = min(rows, 256)
    return pl.pallas_call(
        functools.partial(turn_body, len(blocks)),
        out_shape=[jax.ShapeDtypeStruct((across, rows), blocks[0].dtype)] * len(blocks),
        grid=(rows // high,),
        in_specs=[pl.BlockSpec((high, across), lambda i: (i, 0))] * len(blocks),
        out_specs=[pl.BlockSpec((across, high), lambda i: (0, i))] * len(blocks),
        compiler_params=pltpu.CompilerParams(vmem_limit_bytes=large_vmem),
        cost_estimate=pl.CostEstimate(
            flops=0, bytes_accessed=4 * len(blocks) * rows * across, transcendentals=0
        ),
    )(*blocks)


def right_body(count, pair, *refs):
    slabs, blocks = refs[: count * halves], refs[count * halves : -2]
    out, total = refs[-2:]
    step = pl.program_id(0)

    @pl.when(step == 0)
    def _():
        total[...] = jnp.zeros_like(total)

    high = slabs[0].shape[0]
    for r in range(pair):
        for g in range(halves):
            part = 0.0
            for j in range(count):
                part = part + jnp.dot(
                    slabs[j * halves + g][...],
                    blocks[j * pair + r][...],
                    preferred_element_type=jnp.float32,
                )
            total[r, g * high : (g + 1) * high] += part

    @pl.when(step == pl.num_programs(0) - 1)
    def _():
        for r in range(pair):
            out[r] = total[r].T


def right_sum(slabs, blocks, pair):
    half, rows = slabs[0].shape
    count = len(blocks) // pair
    deep = rows // 2 if rows % 512 == 0 else rows
    return pl.pallas_call(
        functools.partial(right_body, count, pair),
        out_shape=jax.ShapeDtypeStruct((pair, half, half * halves), jnp.float32),
        grid=(rows // deep,),
        in_specs=[pl.BlockSpec((half, deep), lambda i: (0, i))] * len(slabs)
        + [block_spec(b, (deep, half), lambda i: (i, 0)) for b in blocks],
        out_specs=pl.BlockSpec((pair, half, half * halves), lambda i: (0, 0, 0)),
        scratch_shapes=[pltpu.VMEM((pair, half * halves, half), jnp.float32)],
        compiler_params=pltpu.CompilerParams(vmem_limit_bytes=large_vmem),
        cost_estimate=pl.CostEstimate(
            flops=2 * len(blocks) * half * rows * half * halves,
            bytes_accessed=2 * (len(blocks) + len(slabs)) * half * rows,
            transcendentals=0,
        ),
    )(*slabs, *[b for b, _ in blocks])


def shards(tokens_in, out_grads, left_old, right_old):
    nodes = lax.axis_size("node")
    ring = lax.axis_size("dp")
    pair = ring // nodes
    depth = ring // pair
    dp_index = lax.axis_index("dp")
    node = lax.axis_index("node")
    z, y = dp_index // pair, dp_index % pair
    width = left_old.shape[1]
    half = width // halves
    steps = ring // 2
    top_bit = nodes // 2

    def place(z, y):
        return jnp.where(y == 0, z, ring - 1 - z)

    order = [k * pair for k in range(depth)] + [k * pair + 1 for k in reversed(range(depth))]
    position = place(z, y)
    places = (position + jnp.arange(ring, dtype=jnp.int32)) % ring
    slabs = jnp.where(places < depth, places * pair, (ring - 1 - places) * pair + 1)

    def rise(block):
        return lax.ppermute(
            block, "dp", [(order[k], order[(k + 1) % ring]) for k in range(ring)]
        )

    def fall(block):
        return lax.ppermute(
            block, "dp", [(order[(k + 1) % ring], order[k]) for k in range(ring)]
        )

    def swap(block):
        return lax.ppermute(block, "dp", [(d, d ^ 1) for d in range(ring)])

    def exchange(bit):
        pairs = [(n, n ^ bit) for n in range(nodes)]
        return lambda block: lax.ppermute(block, "node", pairs)

    turned = tokens_in.T
    up, down = [None] * halves, [None] * halves
    previous = ()

    def send(h, up_step, down_step):
        nonlocal previous
        arrived = [[a[g]] if a[g] is not None else [] for a, g in ((up, h), (down, 1 - h))]
        picks = [(up_step, h), (ring - down_step, 1 - h)]
        turn = after(slabs, previous)
        tokens, flipped = (turned, True) if any(arrived) else (tokens_in, False)
        previous = sum_round(turn, tokens, flipped, out_grads, half, picks, arrived)
        up[h], down[1 - h] = rise(previous[0]), fall(previous[1])

    send(0, steps, steps)
    for step in range(steps - 1, 0, -1):
        send(1, step, step)
        send(0, step, step)
    turn = after(slabs, previous)
    last = sum_round(
        turn, turned, True, out_grads, half, [(0, 0), (0, 1)], [[], []], jnp.float32
    )
    own = [
        (last[h] + from_wire(up[h]) + from_wire(down[h])).astype(jnp.bfloat16)
        for h in range(halves)
    ]

    ups, downs = [[block] for block in own], [[block] for block in own]
    sent = [{} for _ in range(halves)]
    cols = [{} for _ in range(halves)]
    slab = [{0: (block, None)} for block in own]
    mine = [{} for _ in range(halves)]
    ended = ()
    near = []

    def choose(h, r, js, *done):
        bands = node ^ jnp.array(js, jnp.int32)
        spots = (place(bands, y ^ r) + ring - position) % ring
        middle = (ups, downs)[h][h][steps] if r else own[h]
        cases = downs[h][:steps] + [middle] + ups[h][steps - 1 : 0 : -1]
        picked = pick_blocks(after(spots, *done), cases)
        for k, j in enumerate(js):
            sent[h][j, r] = (picked, k)
            if j == 0:
                cols[h][0, r] = (picked, k)
            if j == 1:
                near.append((sent[h], (1, r), cols[h], (1, r), 1))
        return picked

    def slot(*jobs):
        nonlocal ended
        jobs = list(jobs)
        ready = [k for k, job in enumerate(near) if job[1] in job[0]][:3]
        taken = [near[k] for k in ready]
        near[:] = [job for k, job in enumerate(near) if k not in ready]
        for source, key, store, place_in, bit in taken:
            jobs.append((exchange(bit), alone(source[key]), keep(store, place_in)))
        ended = tuple(job[0](after(job[1], ended)) for job in jobs)
        for job, result in zip(jobs, ended):
            job[2](result)

    def keep(store, key):
        return lambda result: store.__setitem__(key, (result, None))

    def spread(store):
        have, bit = [0, top_bit], nodes // 4
        while bit:
            for j in sorted(have):
                near.append((store, j, store, j | bit, bit))
                have.append(j | bit)
            bit //= 2

    passing = [{} for _ in range(halves)]

    def pass_on(h, j, r):
        near.append((passing[h], (j, r), cols[h], (j, r), 1))

    def trade(h, r, js):
        def store(result):
            for k, j in enumerate(js):
                (passing if j & 1 else cols)[h][j, r] = (result, k)
                if j & 1:
                    pass_on(h, j, r)

        return (exchange(js[0] & ~1), choose(h, r, js), store)

    everyone = range(nodes)
    far = list(range(2, nodes))
    queue = [(r, [j, j + 1]) for r in range(pair) for j in far[::2]]
    jobs = {h + 1: (exchange(top_bit), own[h], keep(slab[h], top_bit)) for h in range(halves)}
    for h in range(halves):
        spread(slab[h])
    rounds = ring - 1
    holding = None
    for k in range(1, rounds + 1):
        h_up, h_down = int(k > steps), int(k >= steps)
        beside = [jobs[k]] if k in jobs else []
        ring_jobs = [
            (rise, ups[h_up][-1], ups[h_up].append),
            (fall, downs[h_down][-1], downs[h_down].append),
        ]
        if k >= steps and (k - steps) % 2 == 0 and queue:
            job = trade(0, *queue.pop(0))
            holding = (job[0](after(job[1], ended)), job[2])
        slot(*ring_jobs, *beside)
        if holding and (k - steps) % 2:
            holding[1](holding[0])
            ended = ended + (holding[0],)
            holding = None
        if k == steps + 1:
            for r in range(pair):
                choose(0, r, [0, 1], ended)
    if holding:
        holding[1](holding[0])
        ended = ended + (holding[0],)
    while queue:
        slot(trade(0, *queue.pop(0)))
    swaps = []

    def swap_job(j):
        store = passing if j & 1 else cols
        if j & 1:
            pass_on(1, j, 1)
        return (swap, alone(store[1][j, 0]), keep(store[1], (j, 1)))

    turned_slab = None
    for j in reversed(far):
        slot(trade(1, 0, [j]), *swaps)
        if turned_slab is None:
            choose(1, 0, [0, 1], ended[:0], sent[1][j, 0][0])
            choose(1, 1, [0, 1], sent[1][1, 0][0])
            whole_slab = [alone(slab[g][j]) for j in everyone for g in range(halves)]
            turned_slab = turn_blocks(after(whole_slab, sent[1][1, 1][0]))
        swaps = [swap_job(j)]
    choose(1, 1, far, ended)

    def own_rows(h):
        cases = [cols[h][j, r] for j in range(nodes) for r in range(pair)]
        piece = pick_rows(jnp.stack([z ^ node, y]), cases, pair, width)
        mine[h][0] = (piece, None)
        spread(mine[h])
        return (exchange(top_bit), piece, keep(mine[h], top_bit))

    def left_part(h, js, earlier, final=False):
        blocks = [sent[h][j, r] for j in js for r in range(pair)]
        return left_sum(blocks, [mine[h][j][0] for j in js], earlier, final)

    def complete(h):
        return all((j, r) in cols[h] for j in range(nodes) for r in range(pair))

    def right_part(h):
        return right_sum(
            turned_slab, [cols[h][j, r] for j in everyone for r in range(pair)], pair
        )

    while not complete(0):
        slot()
    right_new = [right_part(0)]
    job = own_rows(0)
    slot(job, *swaps)
    ended = ended + (right_new[0],)
    while not complete(1):
        slot()
    job = own_rows(1)
    slot(job)
    right_new.append(right_part(1))
    ended = ended + (right_new[1],)
    while not all(j in mine[0] for j in everyone):
        slot()
    total = left_part(0, everyone, [])
    ended = ended + (total,)
    while near:
        slot()
    total = left_part(1, everyone[:top_bit], [total])
    left_out = left_part(1, everyone[top_bit:], [total, left_old], True)

    right_new = jnp.stack(right_new, 1)
    right_new = jnp.where(y == 0, right_new, right_new[::-1]).reshape(right_old.shape)
    right_out = ema_decay * right_old + (1.0 - ema_decay) * right_new
    return (left_out, right_out)


def solution(mesh):
    placed = (P("dp", "node"), P("dp", None), P("node", "dp"), P("node", "dp"))
    return jax.shard_map(
        shards,
        mesh=mesh,
        in_specs=placed,
        out_specs=(P("node", "dp"), P("node", "dp")),
        check_vma=False,
    )
```

time: 880 us -> 280 us (0.32)
  blocking collectives: 646 us -> 0 us
  Pallas kernels: 0 us -> 72.4 us
  starting transfers between devices: 6.04 us -> 48.7 us
  waiting for transfers between devices: 157 us -> 116 us
  matrix products: 36.3 us -> 0 us
  local copies, waits for them, and re-layouts: 15.3 us -> 34.7 us
  between operations: 14.1 us -> 1.43 us
    psum x1 -> x0, blocking collectives: 646 us -> none  [shards(): summed = lax.psum(contract_first(out_grads, tokens_in), 'dp')]
    psum x1 -> x0, waiting for transfers between devices: 117 us -> none  [from_root(): return lax.psum(kept, axis)]
    ppermute x0 -> x54, waiting for transfers between devices: none -> 116 us  [the longest x14 61.4 us: rise(): lax.ppermute(block, 'dp', [(order[k], order[(k + 1) % ring]) for k in ran...]
    pallas_call x0 -> x25, Pallas kernels: none -> 72.4 us  [the longest x8 26.4 us: sum_round(): pl.pallas_call(functools.partial(sum_body, counts, parts, turned), out_sh...]
    ppermute x0 -> x54, starting transfers between devices: none -> 48.7 us  [the longest x14 20.9 us: rise(): lax.ppermute(block, 'dp', [(order[k], order[(k + 1) % ring]) for k in ran...]
    all_gather x1 -> x0, waiting for transfers between devices: 39.5 us -> none  [shards(): lax.all_gather(own_tile, 'node', axis=1, tiled=True)]
    dot_general x3 -> x0, matrix products: 36.3 us -> none  [the longest x2 25 us: contract_first(): lax.dot_general(left, right, (((0,), (0,)), ((), ())), preferred_element_...]
    unnamed x6 -> x121, local copies, waits for them, and re-layouts: 1.53 us -> 30.8 us
  transfers between devices with their start and end apart: 3 -> 54, of which waited for: 2 -> 32; matrix products, arithmetic and copies ran while one was open for 3% -> 4% of each run, Pallas kernels for 0% -> 23%
where the time goes in v2:
time: 280 us; the launch traced here: 279 us
  waiting for transfers between devices  116 us (41%)
  Pallas kernels  72.4 us (26%)
  starting transfers between devices  48.7 us (17%)
  local copies, waits for them, and re-layouts  34.7 us (12%)
  other arithmetic  5.54 us (2%)
    ppermute x14, waiting for transfers between devices, rise(): lax.ppermute(block, 'dp', [(order[k], order[(k + 1) % ring]) for k in ran...  61.4 us
    ppermute x14, waiting for transfers between devices, fall(): lax.ppermute(block, 'dp', [(order[(k + 1) % ring], order[k]) for k in ran...  31.1 us
    unnamed x121, local copies, waits for them, and re-layouts  30.8 us
    pallas_call x8, Pallas kernels, sum_round(): pl.pallas_call(functools.partial(sum_body, counts, parts, turned), out_sh...  26.4 us
    ppermute x14, starting transfers between devices, rise(): lax.ppermute(block, 'dp', [(order[k], order[(k + 1) % ring]) for k in ran...  20.9 us
    ppermute x24, waiting for transfers between devices, exchange(): return lambda block: lax.ppermute(block, 'node', pairs)  20.6 us
    pallas_call x3, Pallas kernels, left_sum(): pl.pallas_call(functools.partial(left_body, len(theirs), pair, final), ou...  15.5 us
    ppermute x24, starting transfers between devices, exchange(): return lambda block: lax.ppermute(block, 'node', pairs)  13.4 us
  transfers between devices with their start and end apart: 54, of which 32 were waited for; matrix products, arithmetic and copies ran while one was open for 4% of the time, Pallas kernels for 23%

profile of v2, /device:TPU:0, one launch (start us, length us, event | category | flops | bytes accessed | tf_op | source)
XLA Modules:
  0.0 278.8 jit_solution(7644253140374201168)
XLA Ops:
  1.2 4.7 %shard_map.140 = (bf16[1024,256]{1,0:T(8,128)(2,1)}, bf16[1024,256]{1,0:T(8,128)(2,1)}) custom-call(s32[8]{0:T(128)} %compare_select_fusion.10.slabs, bf16[1024,1024]{1,0:T(8,128)(2,1)} %tokens.3, bf16[1024,4096]{1,0:T(8,128)(2,1)} %second.15, bf16[1024,4096]{1,0:T(8,128)(2,1)} %second.15), custom_call_target="tpu_custom_call" | custom-call | flops 1073741824 | bytes 5242880 | tf_op jit(solution)/shard_map/pallas_call | solution.py:70
  5.9 3.0 %collective-permute-start = (bf16[1024,256]{1,0:T(8,128)(2,1)}, bf16[1024,256]{1,0:T(8,128)(2,1)}, u32[]{:S(2)}, u32[]{:S(2)}) collective-permute-start(bf16[1024,256]{1,0:T(8,128)(2,1)} %get-tuple-element.78), channel_id=1, source_target_pairs={{0,8},{8,16},{16,24},{24,28},{28,20},{20,12},{12,4},{4,0},{1,9},{9... | collective-permute-start | bytes 1572872 | tf_op jit(solution)/shard_map/ppermute | solution.py:305
  8.9 4.6 %shard_map.141 = (bf16[1024,256]{1,0:T(8,128)(2,1)}, bf16[1024,256]{1,0:T(8,128)(2,1)}) custom-call(s32[8]{0:T(128)} %compare_select_fusion.10.slabs, bf16[1024,1024]{1,0:T(8,128)(2,1)} %tokens.3, bf16[1024,4096]{1,0:T(8,128)(2,1)} %second.15, bf16[1024,4096]{1,0:T(8,128)(2,1)} %second.15), custom_call_target="tpu_custom_call" | custom-call | flops 1073741824 | bytes 5242880 | tf_op jit(solution)/shard_map/pallas_call | solution.py:70
  13.6 2.0 collective-permute-start.2
  15.6 2.9 %copy.16 = bf16[1024,1024]{0,1:T(8,128)(2,1)S(1)} copy(bf16[1024,1024]{1,0:T(8,128)(2,1)} %tokens.3) | data formatting | bytes 4194304 | tf_op args[0]
  18.5 3.5 %collective-permute-done.rest_0_ = bf16[1024,256]{1,0:T(8,128)(2,1)} collective-permute-done((bf16[1024,256]{1,0:T(8,128)(2,1)}, bf16[1024,256]{1,0:T(8,128)(2,1)}, u32[]{:S(2)}, u32[]{:S(2)}) %collective-permute-start) | collective-permute-done | bytes 524320 | tf_op jit(solution)/shard_map/ppermute | solution.py:305
  22.0 2.2 collective-permute-done.1.rest_1_
  24.1 3.4 %copy-done = bf16[1024,4096]{1,0:T(8,128)(2,1)S(1)} copy-done((bf16[1024,4096]{1,0:T(8,128)(2,1)S(1)}, bf16[1024,4096]{1,0:T(8,128)(2,1)}, u32[]{:S(2)}) %copy-start) | copy-done | bytes 8388632
  27.5 3.7 %shard_map.142 = (bf16[1024,256]{1,0:T(8,128)(2,1)S(1)}, bf16[1024,256]{1,0:T(8,128)(2,1)S(1)}) custom-call(s32[8]{0:T(128)S(1)} %copy-done.48, bf16[1024,1024]{1,0:T(8,128)(2,1)S(1)} %bitcast.25, bf16[1024,4096]{1,0:T(8,128)(2,1)S(1)} %copy-done, bf16[1024,4096]{1,0:T(8,128)(2,1)S(1)} %copy-done, bf16[1024,256]{1,0:T(8,128)(2,1)} %collective-permute-done.rest_0_, ...), custom_call_target="tpu_custom_call" | custom-call | flops 1073741824 | bytes 5242880 | tf_op jit(solution)/shard_map/pallas_call | solution.py:70
  31.2 1.6 collective-permute-start.4
  33.3 1.9 collective-permute-done.3.rest_1_
  35.2 2.8 %shard_map.143 = (bf16[1024,256]{1,0:T(8,128)(2,1)S(1)}, bf16[1024,256]{1,0:T(8,128)(2,1)S(1)}) custom-call(s32[8]{0:T(128)S(1)} %copy-done.48, bf16[1024,1024]{1,0:T(8,128)(2,1)S(1)} %bitcast.26, bf16[1024,4096]{1,0:T(8,128)(2,1)S(1)} %copy-done, bf16[1024,4096]{1,0:T(8,128)(2,1)S(1)} %copy-done, bf16[1024,256]{1,0:T(8,128)(2,1)S(1)} %collective-permute-done.2.rest_0_, ...), custom_call_target="tpu_custom_call" | custom-call | flops 1073741824 | bytes 5242880 | tf_op jit(solution)/shard_map/pallas_call | solution.py:70
  38.0 1.6 collective-permute-start.6
  40.0 6.1 %collective-permute-done.4.rest_0_ = bf16[1024,256]{1,0:T(8,128)(2,1)S(1)} collective-permute-done((bf16[1024,256]{1,0:T(8,128)(2,1)S(1)}, bf16[1024,256]{1,0:T(8,128)(2,1)S(1)}, u32[]{:S(2)}, u32[]{:S(2)}) %collective-permute-start.4) | collective-permute-done | bytes 524320 | tf_op jit(solution)/shard_map/ppermute | solution.py:305
  46.1 1.6 collective-permute-done.5.rest_1_
  47.7 2.8 %shard_map.144 = (bf16[1024,256]{1,0:T(8,128)(2,1)S(1)}, bf16[1024,256]{1,0:T(8,128)(2,1)S(1)}) custom-call(s32[8]{0:T(128)S(1)} %copy-done.48, bf16[1024,1024]{1,0:T(8,128)(2,1)S(1)} %bitcast.27, bf16[1024,4096]{1,0:T(8,128)(2,1)S(1)} %copy-done, bf16[1024,4096]{1,0:T(8,128)(2,1)S(1)} %copy-done, bf16[1024,256]{1,0:T(8,128)(2,1)S(1)} %collective-permute-done.4.rest_0_, ...), custom_call_target="tpu_custom_call" | custom-call | flops 1073741824 | bytes 5242880 | tf_op jit(solution)/shard_map/pallas_call | solution.py:70
  50.5 1.6 collective-permute-start.8
  52.6 4.8 %collective-permute-done.6.rest_0_ = bf16[1024,256]{1,0:T(8,128)(2,1)S(1)} collective-permute-done((bf16[1024,256]{1,0:T(8,128)(2,1)S(1)}, bf16[1024,256]{1,0:T(8,128)(2,1)S(1)}, u32[]{:S(2)}, u32[]{:S(2)}) %collective-permute-start.6) | collective-permute-done | bytes 524320 | tf_op jit(solution)/shard_map/ppermute | solution.py:305
  57.3 1.6 collective-permute-done.7.rest_1_
  58.9 2.8 %shard_map.145 = (bf16[1024,256]{1,0:T(8,128)(2,1)S(1)}, bf16[1024,256]{1,0:T(8,128)(2,1)S(1)}) custom-call(s32[8]{0:T(128)S(1)} %copy-done.48, bf16[1024,1024]{1,0:T(8,128)(2,1)S(1)} %bitcast.28, bf16[1024,4096]{1,0:T(8,128)(2,1)S(1)} %copy-done, bf16[1024,4096]{1,0:T(8,128)(2,1)S(1)} %copy-done, bf16[1024,256]{1,0:T(8,128)(2,1)S(1)} %collective-permute-done.6.rest_0_, ...), custom_call_target="tpu_custom_call" | custom-call | flops 1073741824 | bytes 5242880 | tf_op jit(solution)/shard_map/pallas_call | solution.py:70
  62.2 3.7 %collective-permute-done.8.rest_0_ = bf16[1024,256]{1,0:T(8,128)(2,1)S(1)} collective-permute-done((bf16[1024,256]{1,0:T(8,128)(2,1)S(1)}, bf16[1024,256]{1,0:T(8,128)(2,1)S(1)}, u32[]{:S(2)}, u32[]{:S(2)}) %collective-permute-start.8) | collective-permute-done | bytes 524320 | tf_op jit(solution)/shard_map/ppermute | solution.py:305
  66.0 4.2 %collective-permute-done.9.rest_1_ = bf16[1024,256]{1,0:T(8,128)(2,1)S(1)} collective-permute-done((bf16[1024,256]{1,0:T(8,128)(2,1)S(1)}, bf16[1024,256]{1,0:T(8,128)(2,1)S(1)}, u32[]{:S(2)}, u32[]{:S(2)}) %collective-permute-start.9) | collective-permute-done | bytes 524320 | tf_op jit(solution)/shard_map/ppermute | solution.py:310
  70.2 2.8 %shard_map.146 = (bf16[1024,256]{1,0:T(8,128)(2,1)S(1)}, bf16[1024,256]{1,0:T(8,128)(2,1)S(1)}) custom-call(s32[8]{0:T(128)S(1)} %copy-done.48, bf16[1024,1024]{1,0:T(8,128)(2,1)S(1)} %bitcast.29, bf16[1024,4096]{1,0:T(8,128)(2,1)S(1)} %copy-done, bf16[1024,4096]{1,0:T(8,128)(2,1)S(1)} %copy-done, bf16[1024,256]{1,0:T(8,128)(2,1)S(1)} %collective-permute-done.8.rest_0_, ...), custom_call_target="tpu_custom_call" | custom-call | flops 1073741824 | bytes 5242880 | tf_op jit(solution)/shard_map/pallas_call | solution.py:70
  73.0 1.6 collective-permute-start.12
  74.6 1.5 collective-permute-start.10
  76.6 2.2 shard_map.147
  78.8 2.6 collective-permute-done.13
  81.4 5.8 %collective-permute-done.12 = bf16[1024,256]{1,0:T(8,128)(2,1)S(1)} collective-permute-done((bf16[1024,256]{1,0:T(8,128)(2,1)S(1)}, bf16[1024,256]{1,0:T(8,128)(2,1)S(1)}, u32[]{:S(2)}, u32[]{:S(2)}) %collective-permute-start.12) | collective-permute-done | bytes 524320 | tf_op jit(solution)/shard_map/ppermute | solution.py:305
  88.0 1.6 collective-permute-start.16
  90.7 2.2 collective-permute-done.10
  92.8 1.8 collective-permute-start.14
  95.5 6.9 %collective-permute-done.16.refs_4_ = bf16[1024,256]{1,0:T(8,128)(2,1)S(1)} collective-permute-done((bf16[1024,256]{1,0:T(8,128)(2,1)S(1)}, bf16[1024,256]{1,0:T(8,128)(2,1)S(1)}, u32[]{:S(2)}, u32[]{:S(2)}) %collective-permute-start.16) | collective-permute-done | bytes 524320 | tf_op jit(solution)/shard_map/ppermute | solution.py:319
  107.6 9.1 %collective-permute-done.19.refs_6_ = bf16[1024,256]{1,0:T(8,128)(2,1)S(1)} collective-permute-done((bf16[1024,256]{1,0:T(8,128)(2,1)S(1)}, bf16[1024,256]{1,0:T(8,128)(2,1)S(1)}, u32[]{:S(2)}, u32[]{:S(2)}) %collective-permute-start.19) | collective-permute-done | bytes 524320 | tf_op jit(solution)/shard_map/ppermute | solution.py:305
  118.4 1.6 collective-permute-start.23
  120.5 9.3 %collective-permute-done.23.refs_5_ = bf16[1024,256]{1,0:T(8,128)(2,1)} collective-permute-done((bf16[1024,256]{1,0:T(8,128)(2,1)S(1)}, bf16[1024,256]{1,0:T(8,128)(2,1)}, u32[]{:S(2)}, u32[]{:S(2)}) %collective-permute-start.23) | collective-permute-done | bytes 524320 | tf_op jit(solution)/shard_map/ppermute | solution.py:305
  131.0 1.7 shard_map.148.refs_4_.refs_6_
  134.9 9.5 %collective-permute-done.26.refs_1_ = bf16[1024,256]{1,0:T(8,128)(2,1)S(1)} collective-permute-done((bf16[1024,256]{1,0:T(8,128)(2,1)S(1)}, bf16[1024,256]{1,0:T(8,128)(2,1)S(1)}, u32[]{:S(2)}, u32[]{:S(2)}) %collective-permute-start.26) | collective-permute-done | bytes 524320 | tf_op jit(solution)/shard_map/ppermute | solution.py:310
  145.8 1.6 collective-permute-start.29
  147.5 6.4 %collective-permute-done.30.refs_4_.refs_12_ = bf16[2,1024,256]{2,1,0:T(8,128)(2,1)S(1)} collective-permute-done((bf16[2,1024,256]{2,1,0:T(8,128)(2,1)S(1)}, bf16[2,1024,256]{2,1,0:T(8,128)(2,1)S(1)}, u32[]{:S(2)}, u32[]{:S(2)}) %collective-permute-start.30) | collective-permute-done | bytes 1048608 | tf_op jit(solution)/shard_map/ppermute | solution.py:319
  162.4 3.1 %collective-permute-start.31 = (bf16[1024,256]{1,0:T(8,128)(2,1)S(1)}, bf16[1024,256]{1,0:T(8,128)(2,1)S(1)}, u32[]{:S(2)}, u32[]{:S(2)}) collective-permute-start(bf16[1024,256]{1,0:T(8,128)(2,1)S(1)} %collective-permute-done.28.refs_2_), channel_id=1, source_target_pairs={{8,0},{16,8},{24,16},{28,24},{20,28},{12,20},{4,12},{0,4},{9,1},{1... | collective-permute-start | bytes 1572872 | tf_op jit(solution)/shard_map/ppermute | solution.py:310
  166.6 2.6 shard_map.153.refs_5_.refs_7_
  170.0 1.7 collective-permute-start.38
  173.3 4.0 %collective-permute-done.31.refs_3_ = bf16[1024,256]{1,0:T(8,128)(2,1)S(1)} collective-permute-done((bf16[1024,256]{1,0:T(8,128)(2,1)S(1)}, bf16[1024,256]{1,0:T(8,128)(2,1)S(1)}, u32[]{:S(2)}, u32[]{:S(2)}) %collective-permute-start.31) | collective-permute-done | bytes 524320 | tf_op jit(solution)/shard_map/ppermute | solution.py:310
  177.4 3.3 %collective-permute-done.32.refs_6_ = bf16[1024,256]{1,0:T(8,128)(2,1)} collective-permute-done((bf16[1024,256]{1,0:T(8,128)(2,1)S(1)}, bf16[1024,256]{1,0:T(8,128)(2,1)}, u32[]{:S(2)}, u32[]{:S(2)}) %collective-permute-start.32) | collective-permute-done | bytes 524320 | tf_op jit(solution)/shard_map/ppermute | solution.py:305
  180.7 2.0 collective-permute-start.37
  182.7 11.4 %collective-permute-done.36.refs_5_ = bf16[1024,256]{1,0:T(8,128)(2,1)S(1)} collective-permute-done((bf16[1024,256]{1,0:T(8,128)(2,1)}, bf16[1024,256]{1,0:T(8,128)(2,1)S(1)}, u32[]{:S(2)}, u32[]{:S(2)}) %collective-permute-start.36) | collective-permute-done | bytes 524320 | tf_op jit(solution)/shard_map/ppermute | solution.py:305
  195.5 1.9 slice_bitcast_fusion.2
  205.1 1.7 shard_map.155.refs_1_.refs_9_.refs_3_
  208.6 3.5 %collective-permute-done.39 = bf16[1,1024,256]{2,1,0:T(8,128)(2,1)} collective-permute-done((bf16[1,1024,256]{2,1,0:T(8,128)(2,1)}, bf16[1,1024,256]{2,1,0:T(8,128)(2,1)}, u32[]{:S(2)}, u32[]{:S(2)}) %collective-permute-start.39) | collective-permute-done | bytes 524320 | tf_op jit(solution)/shard_map/ppermute | solution.py:319
  213.9 1.9 collective-permute-start.42
  223.3 2.5 collective-permute-done.41.refs_4_.refs_12_
  225.9 2.8 %collective-permute-done.42 = bf16[1024,256]{1,0:T(8,128)(2,1)} collective-permute-done((bf16[1024,256]{1,0:T(8,128)(2,1)}, bf16[1024,256]{1,0:T(8,128)(2,1)}, u32[]{:S(2)}, u32[]{:S(2)}) %collective-permute-start.42) | collective-permute-done | bytes 524320 | tf_op jit(solution)/shard_map/ppermute | solution.py:315
  228.7 1.7 collective-permute-start.46
  230.9 1.7 collective-permute-start.48
  232.7 5.0 %shard_map.159 = (bf16[256,1024]{1,0:T(8,128)(2,1)}, bf16[256,1024]{1,0:T(8,128)(2,1)}, bf16[256,1024]{1,0:T(8,128)(2,1)}, bf16[256,1024]{1,0:T(8,128)(2,1)}, bf...) custom-call(bf16[1024,256]{1,0:T(8,128)(2,1)} %copy-done.3, ...), custom_call_target="tpu_custom_call" | custom-call | bytes 8388608 | tf_op jit(solution)/shard_map/pallas_call | solution.py:222
  237.8 6.3 %shard_map.160 = f32[2,256,512]{2,1,0:T(8,128)} custom-call(bf16[256,1024]{1,0:T(8,128)(2,1)} %get-tuple-element.143.refs_0_, bf16[256,1024]{1,0:T(8,128)(2,1)} %get-tuple-element.144.refs_1_, bf16[256,1024]{1,0:T(8,128)(2,1)} %get-tuple-element.145.refs_2_, bf16[256,1024]{1,0:T(8,128)(2,1)} %get-tuple-element.146.refs_3_, ...), custom_call_target="tpu_custom_call" | custom-call | flops 2147483648 | bytes 8388608 | tf_op jit(solution)/shard_map/pallas_call | solution.py:266
  245.1 1.7 shard_map.156.refs_1_.refs_3_
  249.0 1.6 collective-permute-start.50
  250.5 6.1 %shard_map.161 = f32[2,256,512]{2,1,0:T(8,128)} custom-call(bf16[256,1024]{1,0:T(8,128)(2,1)} %get-tuple-element.143.refs_0_, bf16[256,1024]{1,0:T(8,128)(2,1)} %get-tuple-element.144.refs_1_, bf16[256,1024]{1,0:T(8,128)(2,1)} %get-tuple-element.145.refs_2_, bf16[256,1024]{1,0:T(8,128)(2,1)} %get-tuple-element.146.refs_3_, ...), custom_call_target="tpu_custom_call" | custom-call | flops 2147483648 | bytes 8388608 | tf_op jit(solution)/shard_map/pallas_call | solution.py:266
  258.0 6.0 %shard_map.162.refs_6_ = f32[1024,512]{1,0:T(8,128)} custom-call(bf16[2,1024,256]{2,1,0:T(8,128)(2,1)} %copy-done.6, bf16[2,1024,256]{2,1,0:T(8,128)(2,1)} %copy-done.8, bf16[2,1024,256]{2,1,0:T(8,128)(2,1)} %copy-done.6, bf16[2,1024,256]{2,1,0:T(8,128)(2,1)} %copy-done.8, bf16[2,1024,256]{2,1,0:T(8,128)(2,1)} %copy-done.24, ...), custom_call_target="tpu_custom_call" | custom-call | flops 2147483648 | bytes 10485760 | tf_op jit(solution)/shard_map/pallas_call | solution.py:197
  265.2 1.4 copy-done.50
  266.6 1.8 bitcast_add_fusion
  268.4 4.6 %shard_map.163.refs_6_ = f32[1024,512]{1,0:T(8,128)} custom-call(bf16[2,1024,256]{2,1,0:T(8,128)(2,1)} %copy-done.4, bf16[2,1024,256]{2,1,0:T(8,128)(2,1)} %copy-done.5, bf16[2,1024,256]{2,1,0:T(8,128)(2,1)} %copy-done.4, bf16[2,1024,256]{2,1,0:T(8,128)(2,1)} %copy-done.5, bf16[2,512,256]{2,1,0:T(8,128)(2,1)} %copy-done.40, bf16[2,512,256]{2,1,0:T(8,128)(2,1)} %copy-done.53, ...), custom_call_target="tpu_custom_call" | custom-call | flops 1073741824 | bytes 7340032 | tf_op jit(solution)/shard_map/pallas_call | solution.py:197
  273.9 4.9 %shard_map.164 = f32[1024,512]{1,0:T(8,128)} custom-call(bf16[1,1024,256]{2,1,0:T(8,128)(2,1)} %shard_map.151.refs_0_, bf16[2,1024,256]{2,1,0:T(8,128)(2,1)} %copy-done.25, bf16[1,1024,256]{2,1,0:T(8,128)(2,1)} %shard_map.152.refs_2_, bf16[2,1024,256]{2,1,0:T(8,128)(2,1)} %copy-done.25, bf16[2,512,256]{2,1,0:T(8,128)(2,1)} %copy-done.52, ...), custom_call_target="tpu_custom_call" | custom-call | flops 1073741824 | bytes 7340032 | tf_op jit(solution)/shard_map/pallas_call | solution.py:197
  (206 shorter events, 56.6 us)
Async XLA Ops:
  5.9 16.0 %collective-permute-start = (bf16[1024,256]{1,0:T(8,128)(2,1)}, bf16[1024,256]{1,0:T(8,128)(2,1)}, u32[]{:S(2)}, u32[]{:S(2)}) collective-permute-start(bf16[1024,256]{1,0:T(8,128)(2,1)} %get-tuple-element.78), channel_id=1, source_target_pairs={{0,8},{8,16},{16,24},{24,28},{28,20},{20,12},{12,4},{4,0},{1,9},{9... | collective-permute-start | bytes 1572872 | tf_op jit(solution)/shard_map/ppermute | solution.py:305
  8.9 15.2 %collective-permute-start.1 = (bf16[1024,256]{1,0:T(8,128)(2,1)}, bf16[1024,256]{1,0:T(8,128)(2,1)}, u32[]{:S(2)}, u32[]{:S(2)}) collective-permute-start(bf16[1024,256]{1,0:T(8,128)(2,1)} %get-tuple-element.79), channel_id=1, source_target_pairs={{8,0},{16,8},{24,16},{28,24},{20,28},{12,20},{4,12},{0,4},{9,1},{1... | collective-permute-start | bytes 1572872 | tf_op jit(solution)/shard_map/ppermute | solution.py:310
  13.6 19.7 %collective-permute-start.2 = (bf16[1024,256]{1,0:T(8,128)(2,1)}, bf16[1024,256]{1,0:T(8,128)(2,1)S(1)}, u32[]{:S(2)}, u32[]{:S(2)}) collective-permute-start(bf16[1024,256]{1,0:T(8,128)(2,1)} %get-tuple-element.81), channel_id=1, source_target_pairs={{0,8},{8,16},{16,24},{24,28},{28,20},{20,12},{12,4},{4,0},{1,9},{9... | collective-permute-start | bytes 1572872 | tf_op jit(solution)/shard_map/ppermute | solution.py:305
  15.6 19.5 %collective-permute-start.3 = (bf16[1024,256]{1,0:T(8,128)(2,1)}, bf16[1024,256]{1,0:T(8,128)(2,1)S(1)}, u32[]{:S(2)}, u32[]{:S(2)}) collective-permute-start(bf16[1024,256]{1,0:T(8,128)(2,1)} %get-tuple-element.82), channel_id=1, source_target_pairs={{8,0},{16,8},{24,16},{28,24},{20,28},{12,20},{4,12},{0,4},{9,1},{1... | collective-permute-start | bytes 1572872 | tf_op jit(solution)/shard_map/ppermute | solution.py:310
  31.2 14.9 %collective-permute-start.4 = (bf16[1024,256]{1,0:T(8,128)(2,1)S(1)}, bf16[1024,256]{1,0:T(8,128)(2,1)S(1)}, u32[]{:S(2)}, u32[]{:S(2)}) collective-permute-start(bf16[1024,256]{1,0:T(8,128)(2,1)S(1)} %get-tuple-element.84), channel_id=1, source_target_pairs={{0,8},{8,16},{16,24},{24,28},{28,20},{20,12},{12,4},{4,0},{1,9},{9... | collective-permute-start | bytes 1572872 | tf_op jit(solution)/shard_map/ppermute | solution.py:305
  32.8 14.9 %collective-permute-start.5 = (bf16[1024,256]{1,0:T(8,128)(2,1)S(1)}, bf16[1024,256]{1,0:T(8,128)(2,1)S(1)}, u32[]{:S(2)}, u32[]{:S(2)}) collective-permute-start(bf16[1024,256]{1,0:T(8,128)(2,1)S(1)} %get-tuple-element.85), channel_id=1, source_target_pairs={{8,0},{16,8},{24,16},{28,24},{20,28},{12,20},{4,12},{0,4},{9,1},{1... | collective-permute-start | bytes 1572872 | tf_op jit(solution)/shard_map/ppermute | solution.py:310
  38.0 19.4 %collective-permute-start.6 = (bf16[1024,256]{1,0:T(8,128)(2,1)S(1)}, bf16[1024,256]{1,0:T(8,128)(2,1)S(1)}, u32[]{:S(2)}, u32[]{:S(2)}) collective-permute-start(bf16[1024,256]{1,0:T(8,128)(2,1)S(1)} %get-tuple-element.87), channel_id=1, source_target_pairs={{0,8},{8,16},{16,24},{24,28},{28,20},{20,12},{12,4},{4,0},{1,9},{9... | collective-permute-start | bytes 1572872 | tf_op jit(solution)/shard_map/ppermute | solution.py:305
  39.6 19.3 %collective-permute-start.7 = (bf16[1024,256]{1,0:T(8,128)(2,1)S(1)}, bf16[1024,256]{1,0:T(8,128)(2,1)S(1)}, u32[]{:S(2)}, u32[]{:S(2)}) collective-permute-start(bf16[1024,256]{1,0:T(8,128)(2,1)S(1)} %get-tuple-element.88), channel_id=1, source_target_pairs={{8,0},{16,8},{24,16},{28,24},{20,28},{12,20},{4,12},{0,4},{9,1},{1... | collective-permute-start | bytes 1572872 | tf_op jit(solution)/shard_map/ppermute | solution.py:310
  50.5 15.5 %collective-permute-start.8 = (bf16[1024,256]{1,0:T(8,128)(2,1)S(1)}, bf16[1024,256]{1,0:T(8,128)(2,1)S(1)}, u32[]{:S(2)}, u32[]{:S(2)}) collective-permute-start(bf16[1024,256]{1,0:T(8,128)(2,1)S(1)} %get-tuple-element.90), channel_id=1, source_target_pairs={{0,8},{8,16},{16,24},{24,28},{28,20},{20,12},{12,4},{4,0},{1,9},{9... | collective-permute-start | bytes 1572872 | tf_op jit(solution)/shard_map/ppermute | solution.py:305
  52.1 18.0 %collective-permute-start.9 = (bf16[1024,256]{1,0:T(8,128)(2,1)S(1)}, bf16[1024,256]{1,0:T(8,128)(2,1)S(1)}, u32[]{:S(2)}, u32[]{:S(2)}) collective-permute-start(bf16[1024,256]{1,0:T(8,128)(2,1)S(1)} %get-tuple-element.91), channel_id=1, source_target_pairs={{8,0},{16,8},{24,16},{28,24},{20,28},{12,20},{4,12},{0,4},{9,1},{1... | collective-permute-start | bytes 1572872 | tf_op jit(solution)/shard_map/ppermute | solution.py:310
  61.7 19.7 %collective-permute-start.13 = (bf16[1024,256]{1,0:T(8,128)(2,1)S(1)}, bf16[1024,256]{1,0:T(8,128)(2,1)S(1)}, u32[]{:S(2)}, u32[]{:S(2)}) collective-permute-start(bf16[1024,256]{1,0:T(8,128)(2,1)S(1)} %get-tuple-element.94), channel_id=1, source_target_pairs={{8,0},{16,8},{24,16},{28,24},{20,28},{12,20},{4,12},{0,4},{9,1},{1... | collective-permute-start | bytes 1572872 | tf_op jit(solution)/shard_map/ppermute | solution.py:310
  73.0 14.3 %collective-permute-start.12 = (bf16[1024,256]{1,0:T(8,128)(2,1)S(1)}, bf16[1024,256]{1,0:T(8,128)(2,1)S(1)}, u32[]{:S(2)}, u32[]{:S(2)}) collective-permute-start(bf16[1024,256]{1,0:T(8,128)(2,1)S(1)} %get-tuple-element.96), channel_id=1, source_target_pairs={{0,8},{8,16},{16,24},{24,28},{28,20},{20,12},{12,4},{4,0},{1,9},{9... | collective-permute-start | bytes 1572872 | tf_op jit(solution)/shard_map/ppermute | solution.py:305
  74.6 18.3 %collective-permute-start.10 = (bf16[1024,256]{1,0:T(8,128)(2,1)S(1)}, bf16[1024,256]{1,0:T(8,128)(2,1)S(1)}, u32[]{:S(2)}, u32[]{:S(2)}) collective-permute-start(bf16[1024,256]{1,0:T(8,128)(2,1)S(1)} %get-tuple-element.93), channel_id=1, source_target_pairs={{0,8},{8,16},{16,24},{24,28},{28,20},{20,12},{12,4},{4,0},{1,9},{9... | collective-permute-start | bytes 1572872 | tf_op jit(solution)/shard_map/ppermute | solution.py:305
  76.1 18.6 %collective-permute-start.11 = (bf16[1024,256]{1,0:T(8,128)(2,1)S(1)}, bf16[1024,256]{1,0:T(8,128)(2,1)S(1)}, u32[]{:S(2)}, u32[]{:S(2)}) collective-permute-start(bf16[1024,256]{1,0:T(8,128)(2,1)S(1)} %get-tuple-element.97), channel_id=1, source_target_pairs={{8,0},{16,8},{24,16},{28,24},{20,28},{12,20},{4,12},{0,4},{9,1},{1... | collective-permute-start | bytes 1572872 | tf_op jit(solution)/shard_map/ppermute | solution.py:310
  87.2 33.3 %copy-start.59 = (s32[2]{0:T(128)S(1)}, s32[2]{0:T(128)}, u32[]{:S(2)}) copy-start(s32[2]{0:T(128)} %constant.135.clone) | copy-start | bytes 28
  87.9 77.6 %copy-start.3 = (bf16[1024,256]{1,0:T(8,128)(2,1)}, bf16[1024,256]{1,0:T(8,128)(2,1)S(1)}, u32[]{:S(2)}) copy-start(bf16[1024,256]{1,0:T(8,128)(2,1)S(1)} %fusion.18.refs_0_.refs_4_) | copy-start | bytes 1572868
  87.9 7.5 %collective-permute-start.17 = (bf16[1024,256]{1,0:T(8,128)(2,1)S(1)}, bf16[1024,256]{1,0:T(8,128)(2,1)S(1)}, u32[]{:S(2)}, u32[]{:S(2)}) collective-permute-start(bf16[1024,256]{1,0:T(8,128)(2,1)S(1)} %fusion.18.refs_0_.refs_4_), channel_id=1, source_target_pairs={{0,1},{1,0},{2,3},{3,2},{4,5},{5,4},{6,7},{7,6},{8,9},{9,8},{10,11... | collective-permute-start | bytes 1572872 | tf_op jit(solution)/shard_map/ppermute | solution.py:319
  88.0 14.3 %collective-permute-start.16 = (bf16[1024,256]{1,0:T(8,128)(2,1)S(1)}, bf16[1024,256]{1,0:T(8,128)(2,1)S(1)}, u32[]{:S(2)}, u32[]{:S(2)}) collective-permute-start(bf16[1024,256]{1,0:T(8,128)(2,1)S(1)} %fusion.18.refs_0_.refs_4_), channel_id=1, source_target_pairs={{0,2},{1,3},{2,0},{3,1},{4,6},{5,7},{6,4},{7,5},{8,10},{9,11},{10,... | collective-permute-start | bytes 1572872 | tf_op jit(solution)/shard_map/ppermute | solution.py:319
  89.6 14.0 %collective-permute-start.15 = (bf16[1024,256]{1,0:T(8,128)(2,1)S(1)}, bf16[1024,256]{1,0:T(8,128)(2,1)S(1)}, u32[]{:S(2)}, u32[]{:S(2)}) collective-permute-start(bf16[1024,256]{1,0:T(8,128)(2,1)S(1)} %fusion.18.refs_0_.refs_4_), channel_id=1, source_target_pairs={{8,0},{16,8},{24,16},{28,24},{20,28},{12,20},{4,12},{0,4},{9,1},{1... | collective-permute-start | bytes 1572872 | tf_op jit(solution)/shard_map/ppermute | solution.py:310
  92.8 11.5 %collective-permute-start.14 = (bf16[1024,256]{1,0:T(8,128)(2,1)S(1)}, bf16[1024,256]{1,0:T(8,128)(2,1)S(1)}, u32[]{:S(2)}, u32[]{:S(2)}) collective-permute-start(bf16[1024,256]{1,0:T(8,128)(2,1)S(1)} %fusion.18.refs_0_.refs_4_), channel_id=1, source_target_pairs={{0,8},{8,16},{16,24},{24,28},{28,20},{20,12},{12,4},{4,0},{1,9},{9... | collective-permute-start | bytes 1572872 | tf_op jit(solution)/shard_map/ppermute | solution.py:305
  95.4 107.6 %copy-start.1 = (bf16[1024,256]{1,0:T(8,128)(2,1)}, bf16[1024,256]{1,0:T(8,128)(2,1)S(1)}, u32[]{:S(2)}) copy-start(bf16[1024,256]{1,0:T(8,128)(2,1)S(1)} %fusion.15.refs_0_.refs_4_.refs_1_) | copy-start | bytes 1572868
  95.4 9.0 %collective-permute-start.18 = (bf16[1024,256]{1,0:T(8,128)(2,1)S(1)}, bf16[1024,256]{1,0:T(8,128)(2,1)S(1)}, u32[]{:S(2)}, u32[]{:S(2)}) collective-permute-start(bf16[1024,256]{1,0:T(8,128)(2,1)S(1)} %fusion.15.refs_0_.refs_4_.refs_1_), channel_id=1, source_target_pairs={{0,1},{1,0},{2,3},{3,2},{4,5},{5,4},{6,7},{7,6},{8,9},{9,8},{10,11... | collective-permute-start | bytes 1572872 | tf_op jit(solution)/shard_map/ppermute | solution.py:319
  95.5 22.9 %copy-start.55 = (bf16[1024,256]{1,0:T(8,128)(2,1)}, bf16[1024,256]{1,0:T(8,128)(2,1)S(1)}, u32[]{:S(2)}) copy-start(bf16[1024,256]{1,0:T(8,128)(2,1)S(1)} %collective-permute-done.17.refs_2_) | copy-start | bytes 1572868
  103.5 55.6 %copy-start.26 = (bf16[1024,256]{1,0:T(8,128)(2,1)}, bf16[1024,256]{1,0:T(8,128)(2,1)S(1)}, u32[]{:S(2)}) copy-start(bf16[1024,256]{1,0:T(8,128)(2,1)S(1)} %collective-permute-done.15.refs_1_) | copy-start | bytes 1572868
  104.4 28.3 %copy-start.28 = (bf16[1024,256]{1,0:T(8,128)(2,1)}, bf16[1024,256]{1,0:T(8,128)(2,1)S(1)}, u32[]{:S(2)}) copy-start(bf16[1024,256]{1,0:T(8,128)(2,1)S(1)} %collective-permute-done.14.refs_7_) | copy-start | bytes 1572868
  104.4 12.4 %collective-permute-start.19 = (bf16[1024,256]{1,0:T(8,128)(2,1)S(1)}, bf16[1024,256]{1,0:T(8,128)(2,1)S(1)}, u32[]{:S(2)}, u32[]{:S(2)}) collective-permute-start(bf16[1024,256]{1,0:T(8,128)(2,1)S(1)} %collective-permute-done.14.refs_7_), channel_id=1, source_target_pairs={{0,8},{8,16},{16,24},{24,28},{28,20},{20,12},{12,4},{4,0},{1,9},{9... | collective-permute-start | bytes 1572872 | tf_op jit(solution)/shard_map/ppermute | solution.py:305
  105.7 12.4 %collective-permute-start.20 = (bf16[1024,256]{1,0:T(8,128)(2,1)S(1)}, bf16[1024,256]{1,0:T(8,128)(2,1)S(1)}, u32[]{:S(2)}, u32[]{:S(2)}) collective-permute-start(bf16[1024,256]{1,0:T(8,128)(2,1)S(1)} %collective-permute-done.15.refs_1_), channel_id=1, source_target_pairs={{8,0},{16,8},{24,16},{28,24},{20,28},{12,20},{4,12},{0,4},{9,1},{1... | collective-permute-start | bytes 1572872 | tf_op jit(solution)/shard_map/ppermute | solution.py:310
  106.5 11.9 %collective-permute-start.21 = (bf16[1024,256]{1,0:T(8,128)(2,1)S(1)}, bf16[1024,256]{1,0:T(8,128)(2,1)}, u32[]{:S(2)}, u32[]{:S(2)}) collective-permute-start(bf16[1024,256]{1,0:T(8,128)(2,1)S(1)} %fusion.15.refs_0_.refs_4_.refs_1_), channel_id=1, source_target_pairs={{0,2},{1,3},{2,0},{3,1},{4,6},{5,7},{6,4},{7,5},{8,10},{9,11},{10,... | collective-permute-start | bytes 1572872 | tf_op jit(solution)/shard_map/ppermute | solution.py:319
  107.6 10.7 %collective-permute-start.22 = (bf16[1024,256]{1,0:T(8,128)(2,1)S(1)}, bf16[1024,256]{1,0:T(8,128)(2,1)S(1)}, u32[]{:S(2)}, u32[]{:S(2)}) collective-permute-start(bf16[1024,256]{1,0:T(8,128)(2,1)S(1)} %collective-permute-done.16.refs_4_), channel_id=1, source_target_pairs={{0,1},{1,0},{2,3},{3,2},{4,5},{5,4},{6,7},{7,6},{8,9},{9,8},{10,11... | collective-permute-start | bytes 1572872 | tf_op jit(solution)/shard_map/ppermute | solution.py:319
  118.4 11.5 %collective-permute-start.23 = (bf16[1024,256]{1,0:T(8,128)(2,1)S(1)}, bf16[1024,256]{1,0:T(8,128)(2,1)}, u32[]{:S(2)}, u32[]{:S(2)}) collective-permute-start(bf16[1024,256]{1,0:T(8,128)(2,1)S(1)} %collective-permute-done.19.refs_6_), channel_id=1, source_target_pairs={{0,8},{8,16},{16,24},{24,28},{28,20},{20,12},{12,4},{4,0},{1,9},{9... | collective-permute-start | bytes 1572872 | tf_op jit(solution)/shard_map/ppermute | solution.py:305
  120.0 11.0 %collective-permute-start.24 = (bf16[1024,256]{1,0:T(8,128)(2,1)S(1)}, bf16[1024,256]{1,0:T(8,128)(2,1)}, u32[]{:S(2)}, u32[]{:S(2)}) collective-permute-start(bf16[1024,256]{1,0:T(8,128)(2,1)S(1)} %collective-permute-done.20.refs_2_), channel_id=1, source_target_pairs={{8,0},{16,8},{24,16},{28,24},{20,28},{12,20},{4,12},{0,4},{9,1},{1... | collective-permute-start | bytes 1572872 | tf_op jit(solution)/shard_map/ppermute | solution.py:310
  120.5 12.3 %collective-permute-start.25 = (bf16[1024,256]{1,0:T(8,128)(2,1)}, bf16[1024,256]{1,0:T(8,128)(2,1)}, u32[]{:S(2)}, u32[]{:S(2)}) collective-permute-start(bf16[1024,256]{1,0:T(8,128)(2,1)} %collective-permute-done.21.refs_5_), channel_id=1, source_target_pairs={{0,1},{1,0},{2,3},{3,2},{4,5},{5,4},{6,7},{7,6},{8,9},{9,8},{10,11... | collective-permute-start | bytes 1572872 | tf_op jit(solution)/shard_map/ppermute | solution.py:319
  132.7 21.2 %collective-permute-start.30 = (bf16[2,1024,256]{2,1,0:T(8,128)(2,1)S(1)}, bf16[2,1024,256]{2,1,0:T(8,128)(2,1)S(1)}, u32[]{:S(2)}, u32[]{:S(2)}) collective-permute-start(bf16[2,1024,256]{2,1,0:T(8,128)(2,1)S(1)} %shard_map.148.refs_4_.refs_6_), channel_id=1, source_target_pairs={{0,2},{1,3},{2,0},{3,1},{4,6},{5,7},{6,4},{7,5},{8,10},{9,11},{10,... | collective-permute-start | bytes 3145736 | tf_op jit(solution)/shard_map/ppermute | solution.py:319
  132.8 11.5 %collective-permute-start.26 = (bf16[1024,256]{1,0:T(8,128)(2,1)S(1)}, bf16[1024,256]{1,0:T(8,128)(2,1)S(1)}, u32[]{:S(2)}, u32[]{:S(2)}) collective-permute-start(bf16[1024,256]{1,0:T(8,128)(2,1)S(1)} %fusion.15.refs_0_.refs_4_.refs_1_), channel_id=1, source_target_pairs={{8,0},{16,8},{24,16},{28,24},{20,28},{12,20},{4,12},{0,4},{9,1},{1... | collective-permute-start | bytes 1572872 | tf_op jit(solution)/shard_map/ppermute | solution.py:310
  133.5 12.0 %collective-permute-start.27 = (bf16[1024,256]{1,0:T(8,128)(2,1)}, bf16[1024,256]{1,0:T(8,128)(2,1)S(1)}, u32[]{:S(2)}, u32[]{:S(2)}) collective-permute-start(bf16[1024,256]{1,0:T(8,128)(2,1)} %collective-permute-done.23.refs_5_), channel_id=1, source_target_pairs={{0,8},{8,16},{16,24},{24,28},{28,20},{20,12},{12,4},{4,0},{1,9},{9... | collective-permute-start | bytes 1572872 | tf_op jit(solution)/shard_map/ppermute | solution.py:305
  145.4 9.4 %collective-permute-start.28 = (bf16[1024,256]{1,0:T(8,128)(2,1)S(1)}, bf16[1024,256]{1,0:T(8,128)(2,1)S(1)}, u32[]{:S(2)}, u32[]{:S(2)}) collective-permute-start(bf16[1024,256]{1,0:T(8,128)(2,1)S(1)} %collective-permute-done.26.refs_1_), channel_id=1, source_target_pairs={{8,0},{16,8},{24,16},{28,24},{20,28},{12,20},{4,12},{0,4},{9,1},{1... | collective-permute-start | bytes 1572872 | tf_op jit(solution)/shard_map/ppermute | solution.py:310
  145.8 9.2 %collective-permute-start.29 = (bf16[1024,256]{1,0:T(8,128)(2,1)S(1)}, bf16[1024,256]{1,0:T(8,128)(2,1)S(1)}, u32[]{:S(2)}, u32[]{:S(2)}) collective-permute-start(bf16[1024,256]{1,0:T(8,128)(2,1)S(1)} %fusion.15.refs_0_.refs_4_.refs_1_), channel_id=1, source_target_pairs={{0,8},{8,16},{16,24},{24,28},{28,20},{20,12},{12,4},{4,0},{1,9},{9... | collective-permute-start | bytes 1572872 | tf_op jit(solution)/shard_map/ppermute | solution.py:305
  154.9 46.7 %copy-start.10 = (bf16[1024,256]{1,0:T(8,128)(2,1)}, bf16[1024,256]{1,0:T(8,128)(2,1)S(1)}, u32[]{:S(2)}) copy-start(bf16[1024,256]{1,0:T(8,128)(2,1)S(1)} %collective-permute-done.28.refs_2_) | copy-start | bytes 1572868
  155.0 46.6 %copy-start.13 = (bf16[1024,256]{1,0:T(8,128)(2,1)}, bf16[1024,256]{1,0:T(8,128)(2,1)S(1)}, u32[]{:S(2)}) copy-start(bf16[1024,256]{1,0:T(8,128)(2,1)S(1)} %collective-permute-done.29.refs_7_) | copy-start | bytes 1572868
  155.0 14.2 %collective-permute-start.33 = (bf16[1024,256]{1,0:T(8,128)(2,1)S(1)}, bf16[1024,256]{1,0:T(8,128)(2,1)S(1)}, u32[]{:S(2)}, u32[]{:S(2)}) collective-permute-start(bf16[1024,256]{1,0:T(8,128)(2,1)S(1)} %slice_bitcast_fusion.5), channel_id=1, source_target_pairs={{0,1},{1,0},{2,3},{3,2},{4,5},{5,4},{6,7},{7,6},{8,9},{9,8},{10,11... | collective-permute-start | bytes 1572872 | tf_op jit(solution)/shard_map/ppermute | solution.py:319
  161.9 9.8 %collective-permute-start.35 = (bf16[1024,256]{1,0:T(8,128)(2,1)S(1)}, bf16[1024,256]{1,0:T(8,128)(2,1)S(1)}, u32[]{:S(2)}, u32[]{:S(2)}) collective-permute-start(bf16[1024,256]{1,0:T(8,128)(2,1)S(1)} %slice_bitcast_fusion.3), channel_id=1, source_target_pairs={{0,1},{1,0},{2,3},{3,2},{4,5},{5,4},{6,7},{7,6},{8,9},{9,8},{10,11... | collective-permute-start | bytes 1572872 | tf_op jit(solution)/shard_map/ppermute | solution.py:319
  162.2 10.3 %collective-permute-start.34 = (bf16[1024,256]{1,0:T(8,128)(2,1)S(1)}, bf16[1024,256]{1,0:T(8,128)(2,1)S(1)}, u32[]{:S(2)}, u32[]{:S(2)}) collective-permute-start(bf16[1024,256]{1,0:T(8,128)(2,1)S(1)} %slice_bitcast_fusion.4), channel_id=1, source_target_pairs={{0,1},{1,0},{2,3},{3,2},{4,5},{5,4},{6,7},{7,6},{8,9},{9,8},{10,11... | collective-permute-start | bytes 1572872 | tf_op jit(solution)/shard_map/ppermute | solution.py:319
  162.4 14.9 %collective-permute-start.31 = (bf16[1024,256]{1,0:T(8,128)(2,1)S(1)}, bf16[1024,256]{1,0:T(8,128)(2,1)S(1)}, u32[]{:S(2)}, u32[]{:S(2)}) collective-permute-start(bf16[1024,256]{1,0:T(8,128)(2,1)S(1)} %collective-permute-done.28.refs_2_), channel_id=1, source_target_pairs={{8,0},{16,8},{24,16},{28,24},{20,28},{12,20},{4,12},{0,4},{9,1},{1... | collective-permute-start | bytes 1572872 | tf_op jit(solution)/shard_map/ppermute | solution.py:310
  165.5 15.2 %collective-permute-start.32 = (bf16[1024,256]{1,0:T(8,128)(2,1)S(1)}, bf16[1024,256]{1,0:T(8,128)(2,1)}, u32[]{:S(2)}, u32[]{:S(2)}) collective-permute-start(bf16[1024,256]{1,0:T(8,128)(2,1)S(1)} %collective-permute-done.29.refs_7_), channel_id=1, source_target_pairs={{0,8},{8,16},{16,24},{24,28},{28,20},{20,12},{12,4},{4,0},{1,9},{9... | collective-permute-start | bytes 1572872 | tf_op jit(solution)/shard_map/ppermute | solution.py:305
  170.0 25.5 %collective-permute-start.38 = (bf16[2,1024,256]{2,1,0:T(8,128)(2,1)}, bf16[2,1024,256]{2,1,0:T(8,128)(2,1)}, u32[]{:S(2)}, u32[]{:S(2)}) collective-permute-start(bf16[2,1024,256]{2,1,0:T(8,128)(2,1)} %shard_map.153.refs_5_.refs_7_), channel_id=1, source_target_pairs={{0,2},{1,3},{2,0},{3,1},{4,6},{5,7},{6,4},{7,5},{8,10},{9,11},{10,... | collective-permute-start | bytes 3145736 | tf_op jit(solution)/shard_map/ppermute | solution.py:319
  180.7 13.5 %collective-permute-start.36 = (bf16[1024,256]{1,0:T(8,128)(2,1)}, bf16[1024,256]{1,0:T(8,128)(2,1)S(1)}, u32[]{:S(2)}, u32[]{:S(2)}) collective-permute-start(bf16[1024,256]{1,0:T(8,128)(2,1)} %collective-permute-done.32.refs_6_), channel_id=1, source_target_pairs={{0,8},{8,16},{16,24},{24,28},{28,20},{20,12},{12,4},{4,0},{1,9},{9... | collective-permute-start | bytes 1572872 | tf_op jit(solution)/shard_map/ppermute | solution.py:305
  180.7 14.5 %collective-permute-start.37 = (bf16[1024,256]{1,0:T(8,128)(2,1)S(1)}, bf16[1024,256]{1,0:T(8,128)(2,1)}, u32[]{:S(2)}, u32[]{:S(2)}) collective-permute-start(bf16[1024,256]{1,0:T(8,128)(2,1)S(1)} %collective-permute-done.31.refs_3_), channel_id=1, source_target_pairs={{8,0},{16,8},{24,16},{28,24},{20,28},{12,20},{4,12},{0,4},{9,1},{1... | collective-permute-start | bytes 1572872 | tf_op jit(solution)/shard_map/ppermute | solution.py:310
  197.4 11.2 %collective-permute-start.40 = (bf16[1024,256]{1,0:T(8,128)(2,1)}, bf16[1024,256]{1,0:T(8,128)(2,1)}, u32[]{:S(2)}, u32[]{:S(2)}) collective-permute-start(bf16[1024,256]{1,0:T(8,128)(2,1)} %slice_bitcast_fusion.2), channel_id=1, source_target_pairs={{0,1},{1,0},{2,3},{3,2},{4,5},{5,4},{6,7},{7,6},{8,9},{9,8},{10,11... | collective-permute-start | bytes 1572872 | tf_op jit(solution)/shard_map/ppermute | solution.py:319
  197.4 14.7 %collective-permute-start.39 = (bf16[1,1024,256]{2,1,0:T(8,128)(2,1)}, bf16[1,1024,256]{2,1,0:T(8,128)(2,1)}, u32[]{:S(2)}, u32[]{:S(2)}) collective-permute-start(bf16[1,1024,256]{2,1,0:T(8,128)(2,1)} %shard_map.152.refs_2_), channel_id=1, source_target_pairs={{0,2},{1,3},{2,0},{3,1},{4,6},{5,7},{6,4},{7,5},{8,10},{9,11},{10,... | collective-permute-start | bytes 1572872 | tf_op jit(solution)/shard_map/ppermute | solution.py:319
  202.0 44.7 %copy-start.4 = (bf16[2,1024,256]{2,1,0:T(8,128)(2,1)}, bf16[2,1024,256]{2,1,0:T(8,128)(2,1)S(1)}, u32[]{:S(2)}) copy-start(bf16[2,1024,256]{2,1,0:T(8,128)(2,1)S(1)} %shard_map.154.refs_0_.refs_8_.refs_2_) | copy-start | bytes 3145732
  206.8 40.0 %copy-start.5 = (bf16[2,1024,256]{2,1,0:T(8,128)(2,1)}, bf16[2,1024,256]{2,1,0:T(8,128)(2,1)S(1)}, u32[]{:S(2)}) copy-start(bf16[2,1024,256]{2,1,0:T(8,128)(2,1)S(1)} %shard_map.155.refs_1_.refs_9_.refs_3_) | copy-start | bytes 3145732
  212.1 13.8 %collective-permute-start.41 = (bf16[1,1024,256]{2,1,0:T(8,128)(2,1)}, bf16[1,1024,256]{2,1,0:T(8,128)(2,1)S(1)}, u32[]{:S(2)}, u32[]{:S(2)}) collective-permute-start(bf16[1,1024,256]{2,1,0:T(8,128)(2,1)} %shard_map.151.refs_0_), channel_id=1, source_target_pairs={{0,2},{1,3},{2,0},{3,1},{4,6},{5,7},{6,4},{7,5},{8,10},{9,11},{10,... | collective-permute-start | bytes 1572872 | tf_op jit(solution)/shard_map/ppermute | solution.py:319
  213.4 12.4 %collective-permute-start.44 = (bf16[1024,256]{1,0:T(8,128)(2,1)}, bf16[1024,256]{1,0:T(8,128)(2,1)}, u32[]{:S(2)}, u32[]{:S(2)}) collective-permute-start(bf16[1024,256]{1,0:T(8,128)(2,1)} %slice_bitcast_fusion.1), channel_id=1, source_target_pairs={{0,1},{1,0},{2,3},{3,2},{4,5},{5,4},{6,7},{7,6},{8,9},{9,8},{10,11... | collective-permute-start | bytes 1572872 | tf_op jit(solution)/shard_map/ppermute | solution.py:319
  213.4 12.4 %collective-permute-start.45 = (bf16[1024,256]{1,0:T(8,128)(2,1)}, bf16[1024,256]{1,0:T(8,128)(2,1)}, u32[]{:S(2)}, u32[]{:S(2)}) collective-permute-start(bf16[1024,256]{1,0:T(8,128)(2,1)} %slice_bitcast_fusion), channel_id=1, source_target_pairs={{0,1},{1,0},{2,3},{3,2},{4,5},{5,4},{6,7},{7,6},{8,9},{9,8},{10,11... | collective-permute-start | bytes 1572872 | tf_op jit(solution)/shard_map/ppermute | solution.py:319
  213.9 11.9 %collective-permute-start.43 = (bf16[1024,256]{1,0:T(8,128)(2,1)}, bf16[1024,256]{1,0:T(8,128)(2,1)}, u32[]{:S(2)}, u32[]{:S(2)}) collective-permute-start(bf16[1024,256]{1,0:T(8,128)(2,1)} %bitcast.9), channel_id=1, source_target_pairs={{0,1},{1,0},{2,3},{3,2},{4,5},{5,4},{6,7},{7,6},{8,9},{9,8},{10,11... | collective-permute-start | bytes 1572872 | tf_op jit(solution)/shard_map/ppermute | solution.py:319
  213.9 14.8 %collective-permute-start.42 = (bf16[1024,256]{1,0:T(8,128)(2,1)}, bf16[1024,256]{1,0:T(8,128)(2,1)}, u32[]{:S(2)}, u32[]{:S(2)}) collective-permute-start(bf16[1024,256]{1,0:T(8,128)(2,1)} %bitcast.9), channel_id=1, source_target_pairs={{0,4},{4,0},{8,12},{12,8},{16,20},{20,16},{24,28},{28,24},{1,5},{5... | collective-permute-start | bytes 1572872 | tf_op jit(solution)/shard_map/ppermute | solution.py:315
  228.7 15.4 %collective-permute-start.46 = (bf16[1024,256]{1,0:T(8,128)(2,1)S(1)}, bf16[1024,256]{1,0:T(8,128)(2,1)S(1)}, u32[]{:S(2)}, u32[]{:S(2)}) collective-permute-start(bf16[1024,256]{1,0:T(8,128)(2,1)S(1)} %bitcast.31), channel_id=1, source_target_pairs={{0,4},{4,0},{8,12},{12,8},{16,20},{20,16},{24,28},{28,24},{1,5},{5... | collective-permute-start | bytes 1572872 | tf_op jit(solution)/shard_map/ppermute | solution.py:315
  230.4 13.7 %collective-permute-start.47 = (bf16[1024,256]{1,0:T(8,128)(2,1)}, bf16[1024,256]{1,0:T(8,128)(2,1)S(1)}, u32[]{:S(2)}, u32[]{:S(2)}) collective-permute-start(bf16[1024,256]{1,0:T(8,128)(2,1)} %collective-permute-done.42), channel_id=1, source_target_pairs={{0,1},{1,0},{2,3},{3,2},{4,5},{5,4},{6,7},{7,6},{8,9},{9,8},{10,11... | collective-permute-start | bytes 1572872 | tf_op jit(solution)/shard_map/ppermute | solution.py:319
  230.4 13.7 %collective-permute-start.49 = (bf16[2,512,256]{2,1,0:T(8,128)(2,1)S(1)}, bf16[2,512,256]{2,1,0:T(8,128)(2,1)S(1)}, u32[]{:S(2)}, u32[]{:S(2)}) collective-permute-start(bf16[2,512,256]{2,1,0:T(8,128)(2,1)S(1)} %shard_map.158.refs_8_), channel_id=1, source_target_pairs={{0,1},{1,0},{2,3},{3,2},{4,5},{5,4},{6,7},{7,6},{8,9},{9,8},{10,11... | collective-permute-start | bytes 1572872 | tf_op jit(solution)/shard_map/ppermute | solution.py:319
  230.9 13.9 %collective-permute-start.48 = (bf16[2,512,256]{2,1,0:T(8,128)(2,1)S(1)}, bf16[2,512,256]{2,1,0:T(8,128)(2,1)}, u32[]{:S(2)}, u32[]{:S(2)}) collective-permute-start(bf16[2,512,256]{2,1,0:T(8,128)(2,1)S(1)} %shard_map.158.refs_8_), channel_id=1, source_target_pairs={{0,2},{1,3},{2,0},{3,1},{4,6},{5,7},{6,4},{7,5},{8,10},{9,11},{10,... | collective-permute-start | bytes 1572872 | tf_op jit(solution)/shard_map/ppermute | solution.py:319
  245.0 13.0 %collective-permute-start.51 = (bf16[2,512,256]{2,1,0:T(8,128)(2,1)}, bf16[2,512,256]{2,1,0:T(8,128)(2,1)}, u32[]{:S(2)}, u32[]{:S(2)}) collective-permute-start(bf16[2,512,256]{2,1,0:T(8,128)(2,1)} %collective-permute-done.48.refs_10_), channel_id=1, source_target_pairs={{0,1},{1,0},{2,3},{3,2},{4,5},{5,4},{6,7},{7,6},{8,9},{9,8},{10,11... | collective-permute-start | bytes 1572872 | tf_op jit(solution)/shard_map/ppermute | solution.py:319
  247.8 16.2 %collective-permute-start.52 = (bf16[2,512,256]{2,1,0:T(8,128)(2,1)S(1)}, bf16[2,512,256]{2,1,0:T(8,128)(2,1)S(1)}, u32[]{:S(2)}, u32[]{:S(2)}) collective-permute-start(bf16[2,512,256]{2,1,0:T(8,128)(2,1)S(1)} %shard_map.157.refs_4_), channel_id=1, source_target_pairs={{0,1},{1,0},{2,3},{3,2},{4,5},{5,4},{6,7},{7,6},{8,9},{9,8},{10,11... | collective-permute-start | bytes 1572872 | tf_op jit(solution)/shard_map/ppermute | solution.py:319
  249.0 15.1 %collective-permute-start.50 = (bf16[2,512,256]{2,1,0:T(8,128)(2,1)S(1)}, bf16[2,512,256]{2,1,0:T(8,128)(2,1)S(1)}, u32[]{:S(2)}, u32[]{:S(2)}) collective-permute-start(bf16[2,512,256]{2,1,0:T(8,128)(2,1)S(1)} %shard_map.157.refs_4_), channel_id=1, source_target_pairs={{0,2},{1,3},{2,0},{3,1},{4,6},{5,7},{6,4},{7,5},{8,10},{9,11},{10,... | collective-permute-start | bytes 1572872 | tf_op jit(solution)/shard_map/ppermute | solution.py:319
  264.1 8.9 %collective-permute-start.53 = (bf16[2,512,256]{2,1,0:T(8,128)(2,1)S(1)}, bf16[2,512,256]{2,1,0:T(8,128)(2,1)S(1)}, u32[]{:S(2)}, u32[]{:S(2)}) collective-permute-start(bf16[2,512,256]{2,1,0:T(8,128)(2,1)S(1)} %collective-permute-done.50.refs_4_), channel_id=1, source_target_pairs={{0,1},{1,0},{2,3},{3,2},{4,5},{5,4},{6,7},{7,6},{8,9},{9,8},{10,11... | collective-permute-start | bytes 1572872 | tf_op jit(solution)/shard_map/ppermute | solution.py:319
  (50 other events, 248.3 us)

commit v3 on v2

v3 whole, which is shorter than its diff:
```python
import functools

import jax
import jax.numpy as jnp
from jax import lax
from jax.experimental import pallas as pl
from jax.experimental.pallas import tpu as pltpu
from jax.sharding import PartitionSpec as P

ema_decay = 0.95
halves = 2
wire_gain = 2.0**20
all_vmem = 60 * 2**20


def to_wire(value):
    scaled = value * wire_gain
    square = scaled * scaled
    return (scaled * jnp.abs(scaled) * square).astype(jnp.bfloat16)


def from_wire(sent):
    power = sent.astype(jnp.float32)
    root = lax.rsqrt(lax.rsqrt(jnp.abs(power))) * (1.0 / wire_gain)
    return jnp.where(power < 0, -root, root)


def pinned(arrays):
    return [pltpu.with_memory_space_constraint(a, pltpu.HBM) for a in arrays]


def after(values, *done):
    return lax.optimization_barrier((values, done))[0]


def sum_body(counts, parts, slabs, tokens, first, second, *rest):
    arrived, outs = rest[: sum(counts)], rest[sum(counts) :]
    for k, grads in enumerate((first, second)):
        total = lax.dot_general(
            tokens[...],
            grads[...],
            (((0,), (0,)), ((), ())),
            preferred_element_type=jnp.float32,
        )
        across = outs[k].shape[1]
        if total.shape[1] != across:
            total = total[:, parts[k] * across : (parts[k] + 1) * across]
        for ref in arrived[sum(counts[:k]) : sum(counts[: k + 1])]:
            total = total + from_wire(ref[...])
        outs[k][...] = to_wire(total) if outs[k].dtype == jnp.bfloat16 else total


def sum_round(slabs, tokens, grads, half, picks, arrived, kind=jnp.bfloat16):
    depth, rows = tokens.shape
    high = rows // 2 if rows % 512 == 0 else rows
    wide = half if half % 128 == 0 else half * halves
    per_slab = half * halves // wide
    parts = [part for _, part in picks]

    def grad_block(ahead, part):
        return pl.BlockSpec(
            (depth, wide), lambda i, s: (0, s[ahead] * per_slab + part % per_slab)
        )

    token_block = pl.BlockSpec((depth, high), lambda i, s: (0, i))
    block = pl.BlockSpec((high, half), lambda i, s: (i, 0))
    counts = tuple(len(a) for a in arrived)
    flat = [a for group in arrived for a in group]
    return pl.pallas_call(
        functools.partial(sum_body, counts, parts),
        out_shape=[jax.ShapeDtypeStruct((rows, half), kind)] * 2,
        grid_spec=pltpu.PrefetchScalarGridSpec(
            num_scalar_prefetch=1,
            grid=(rows // high,),
            in_specs=[token_block] + [grad_block(*pick) for pick in picks] + [block] * len(flat),
            out_specs=[block] * 2,
        ),
        compiler_params=pltpu.CompilerParams(vmem_limit_bytes=16 * 2**20),
        cost_estimate=pl.CostEstimate(
            flops=4 * half * depth * rows,
            bytes_accessed=0,
            transcendentals=0,
        ),
    )(slabs, tokens, *pinned([grads, grads]), *flat)


def block_spec(block, shape, where):
    array, index = block
    if index is None:
        return pl.BlockSpec(shape, where)
    return pl.BlockSpec((None, *shape), lambda *args: (index, *where(*args)))


def alone(block):
    array, index = block
    return array if index is None else array[index]


def pick_body(cases, groups, spots, *refs):
    sources, outs, sems = refs[:cases], list(refs[cases:-1]), refs[-1]
    targets = []
    for count, stacked in groups:
        if stacked:
            stack = outs.pop(0)
            targets += [stack.at[k] for k in range(count)]
        else:
            targets += [outs.pop(0) for _ in range(count)]
    for k, target in enumerate(targets):
        for c in range(cases):

            @pl.when(spots[k] == c)
            def _():
                pltpu.make_async_copy(sources[c], target, sems.at[k]).start()

    for k, target in enumerate(targets):
        pltpu.make_async_copy(sources[0], target, sems.at[k]).wait()


def pick_blocks(spots, cases, groups):
    total = spots.shape[0]
    shape = cases[0].shape
    shapes = []
    for count, stacked in groups:
        shapes += [(count, *shape)] if stacked else [shape] * count
    return pl.pallas_call(
        functools.partial(pick_body, len(cases), groups),
        out_shape=[jax.ShapeDtypeStruct(s, cases[0].dtype) for s in shapes],
        grid_spec=pltpu.PrefetchScalarGridSpec(
            num_scalar_prefetch=1,
            grid=(1,),
            in_specs=[pl.BlockSpec(memory_space=pl.ANY)] * len(cases),
            out_specs=[
                pl.BlockSpec(s, lambda i, p, s=s: (0,) * len(s)) for s in shapes
            ],
            scratch_shapes=[pltpu.SemaphoreType.DMA((total,))],
        ),
        compiler_params=pltpu.CompilerParams(vmem_limit_bytes=all_vmem),
    )(spots, *cases)


def rows_body(views, pair, high, spots, *refs):
    sources, out, sems = refs[: len(views)], refs[-2], refs[-1]
    start = pl.multiple_of(spots[1] * high, high)

    def rows(k, first):
        if views[k] is None:
            return sources[k].at[pl.ds(first, high)]
        return sources[k].at[views[k], pl.ds(first, high)]

    for r in range(pair):
        for c in range(len(views) // pair):

            @pl.when(spots[0] == c)
            def _():
                copied = rows(c * pair + r, start)
                pltpu.make_async_copy(copied, out.at[r], sems.at[r]).start()

    for r in range(pair):
        pltpu.make_async_copy(rows(r, 0), out.at[r], sems.at[r]).wait()


def pick_rows(spots, cases, pair, high):
    across, kind = cases[0][0].shape[-1], cases[0][0].dtype
    shape = (pair, high, across)
    return pl.pallas_call(
        functools.partial(rows_body, [view for _, view in cases], pair, high),
        out_shape=jax.ShapeDtypeStruct(shape, kind),
        grid_spec=pltpu.PrefetchScalarGridSpec(
            num_scalar_prefetch=1,
            grid=(1,),
            in_specs=[pl.BlockSpec(memory_space=pl.ANY)] * len(cases),
            out_specs=pl.BlockSpec(shape, lambda i, s: (0, 0, 0)),
            scratch_shapes=[pltpu.SemaphoreType.DMA((pair,))],
        ),
        compiler_params=pltpu.CompilerParams(vmem_limit_bytes=all_vmem),
    )(spots, *[array for array, _ in cases])


def left_body(count, pair, first, *refs):
    blocks, theirs = refs[: count * pair], refs[count * pair : count * pair + count]
    earlier, out = refs[count * pair + count :]
    total = 0.0
    for j in range(count):
        for r in range(pair):
            total = total + lax.dot_general(
                blocks[j * pair + r][...],
                theirs[j][r],
                (((1,), (1,)), ((), ())),
                preferred_element_type=jnp.float32,
            )
    kept = ema_decay * earlier[...] if first else earlier[...]
    out[...] = kept + (1.0 - ema_decay) * total


def left_sum(blocks, theirs, earlier, first):
    rows, across = blocks[0][0].shape[-2:]
    width = theirs[0].shape[1]
    high = rows // 2 if rows % 512 == 0 else rows
    pair = len(blocks) // len(theirs)
    out = pl.BlockSpec((high, width), lambda i: (i, 0))
    return pl.pallas_call(
        functools.partial(left_body, len(theirs), pair, first),
        out_shape=jax.ShapeDtypeStruct((rows, width), jnp.float32),
        grid=(rows // high,),
        in_specs=[block_spec(b, (high, across), lambda i: (i, 0)) for b in blocks]
        + [pl.BlockSpec(theirs[0].shape, lambda i: (0, 0, 0))] * len(theirs)
        + [out],
        out_specs=out,
        compiler_params=pltpu.CompilerParams(vmem_limit_bytes=all_vmem),
        cost_estimate=pl.CostEstimate(
            flops=2 * len(blocks) * across * rows * width,
            bytes_accessed=0,
            transcendentals=0,
        ),
    )(*[b for b, _ in blocks], *theirs, earlier)


def turn_body(count, *refs):
    for k in range(count):
        refs[count + k][...] = refs[k][...].T


def turn_blocks(blocks):
    rows, across = blocks[0].shape
    high = min(rows, 256)
    return pl.pallas_call(
        functools.partial(turn_body, len(blocks)),
        out_shape=[pltpu.HBM((across, rows), blocks[0].dtype)] * len(blocks),
        grid=(rows // high,),
        in_specs=[pl.BlockSpec((high, across), lambda i: (i, 0))] * len(blocks),
        out_specs=[pl.BlockSpec((across, high), lambda i: (0, i))] * len(blocks),
        compiler_params=pltpu.CompilerParams(vmem_limit_bytes=all_vmem),
    )(*blocks)


def right_body(count, pair, *refs):
    slabs, blocks = refs[: count * halves], refs[count * halves : -2]
    out, total = refs[-2:]
    step = pl.program_id(0)

    @pl.when(step == 0)
    def _():
        total[...] = jnp.zeros_like(total)

    high = slabs[0].shape[0]
    for r in range(pair):
        for g in range(halves):
            part = 0.0
            for j in range(count):
                part = part + jnp.dot(
                    slabs[j * halves + g][...],
                    blocks[j * pair + r][...],
                    preferred_element_type=jnp.float32,
                )
            total[r, g * high : (g + 1) * high] += part

    @pl.when(step == pl.num_programs(0) - 1)
    def _():
        for r in range(pair):
            out[r] = total[r].T


def right_sum(slabs, blocks, pair):
    half, rows = slabs[0].shape
    count = len(blocks) // pair
    deep = rows // 2 if rows % 512 == 0 else rows
    return pl.pallas_call(
        functools.partial(right_body, count, pair),
        out_shape=jax.ShapeDtypeStruct((pair, half, half * halves), jnp.float32),
        grid=(rows // deep,),
        in_specs=[pl.BlockSpec((half, deep), lambda i: (0, i))] * len(slabs)
        + [block_spec(b, (deep, half), lambda i: (i, 0)) for b in blocks],
        out_specs=pl.BlockSpec((pair, half, half * halves), lambda i: (0, 0, 0)),
        scratch_shapes=[pltpu.VMEM((pair, half * halves, half), jnp.float32)],
        compiler_params=pltpu.CompilerParams(vmem_limit_bytes=all_vmem),
        cost_estimate=pl.CostEstimate(
            flops=2 * len(blocks) * half * rows * half * halves,
            bytes_accessed=0,
            transcendentals=0,
        ),
    )(*pinned(slabs), *[b for b, _ in blocks])


def shards(tokens_in, out_grads, left_old, right_old):
    nodes = lax.axis_size("node")
    ring = lax.axis_size("dp")
    pair = ring // nodes
    depth = ring // pair
    dp_index = lax.axis_index("dp")
    node = lax.axis_index("node")
    z, y = dp_index // pair, dp_index % pair
    width = left_old.shape[1]
    half = width // halves
    steps = ring // 2
    top_bit = nodes // 2

    def place(z, y):
        return jnp.where(y == 0, z, ring - 1 - z)

    order = [k * pair for k in range(depth)] + [k * pair + 1 for k in reversed(range(depth))]
    position = place(z, y)
    places = (position + jnp.arange(ring, dtype=jnp.int32)) % ring
    slabs = jnp.where(places < depth, places * pair, (ring - 1 - places) * pair + 1)

    def rise(block):
        return lax.ppermute(
            block, "dp", [(order[k], order[(k + 1) % ring]) for k in range(ring)]
        )

    def fall(block):
        return lax.ppermute(
            block, "dp", [(order[(k + 1) % ring], order[k]) for k in range(ring)]
        )

    def swap(block):
        return lax.ppermute(block, "dp", [(d, d ^ 1) for d in range(ring)])

    def exchange(bit):
        pairs = [(n, n ^ bit) for n in range(nodes)]
        return lambda block: lax.ppermute(block, "node", pairs)

    up, down = [None] * halves, [None] * halves
    previous = ()

    def send(h, up_step, down_step):
        nonlocal previous
        arrived = [[a[g]] if a[g] is not None else [] for a, g in ((up, h), (down, 1 - h))]
        picks = [(up_step, h), (ring - down_step, 1 - h)]
        turn = after(slabs, previous)
        previous = sum_round(turn, tokens_in, out_grads, half, picks, arrived)
        up[h], down[1 - h] = rise(previous[0]), fall(previous[1])

    send(0, steps, steps)
    for step in range(steps - 1, 0, -1):
        send(1, step, step)
        send(0, step, step)
    turn = after(slabs, previous)
    last = sum_round(
        turn, tokens_in, out_grads, half, [(0, 0), (0, 1)], [[], []], jnp.float32
    )
    def finish(h, *done):
        first = after(last[h], *done)
        return (first + from_wire(up[h]) + from_wire(down[h])).astype(jnp.bfloat16)

    own = [finish(0)]
    slab = [{0: (own[0], None)}]
    slab[0][1] = (exchange(1)(own[0]), None)
    own.append(finish(1, slab[0][1][0]))
    slab.append({0: (own[1], None)})

    ups, downs = [[block] for block in own], [[block] for block in own]
    sent = [{} for _ in range(halves)]
    cols = [{} for _ in range(halves)]
    mine = [{} for _ in range(halves)]
    ended = ()
    near = []

    def choose(h, wanted, *done):
        spots, groups = [], []
        for r, js in wanted:
            bands = node ^ jnp.array(js, jnp.int32)
            spots.append((place(bands, y ^ r) + ring - position) % ring)
            groups.append((len(js), len(js) > 1 and js[0] > 1))
        middle = (ups, downs)[h][h][steps:] or [own[h]]
        cases = downs[h][:steps] + middle + ups[h][steps - 1 : 0 : -1]
        picked = pick_blocks(after(jnp.concatenate(spots), *done), cases, groups)
        first = picked[0]
        for (r, js), (_, stacked) in zip(wanted, groups):
            if stacked:
                stack, picked = picked[0], picked[1:]
            for k, j in enumerate(js):
                if stacked:
                    sent[h][j, r] = (stack, k)
                else:
                    sent[h][j, r], picked = (picked[0], None), picked[1:]
                if j == 0:
                    cols[h][0, r] = sent[h][0, r]
                if j == 1:
                    near.append((sent[h], (1, r), cols[h], (1, r), 1))
        return first

    def take_near(most):
        ready = [k for k, job in enumerate(near) if job[1] in job[0]][:most]
        taken = [near[k] for k in ready]
        near[:] = [job for k, job in enumerate(near) if k not in ready]
        jobs = []
        for source, key, store, place_in, bit in taken:
            array, view = source[key]
            jobs.append((exchange(bit), array, keep(store, place_in, view)))
        return jobs

    def slot(*jobs):
        nonlocal ended
        jobs = list(jobs) + take_near(3)
        ended = tuple(job[0](after(job[1], ended)) for job in jobs)
        for job, result in zip(jobs, ended):
            job[2](result)

    def keep(store, key, view=None):
        return lambda result: store.__setitem__(key, (result, view))

    def spread(store):
        have, bit = [0, top_bit], nodes // 4
        while bit:
            for j in sorted(have):
                if j | bit not in store:
                    near.append((store, j, store, j | bit, bit))
                have.append(j | bit)
            bit //= 2

    passing = [{} for _ in range(halves)]

    def pass_on(h, j, r):
        near.append((passing[h], (j, r), cols[h], (j, r), 1))

    def trade(h, r, js):
        def store(result):
            for k, j in enumerate(js):
                view = (result, k) if len(js) > 1 else (result, None)
                (passing if j & 1 else cols)[h][j, r] = view
                if j & 1:
                    pass_on(h, j, r)

        array = sent[h][js[0], r][0]
        return (exchange(js[0] & ~1), array, store)

    everyone = range(nodes)
    far = list(range(2, nodes))
    queue = [(r, [j, j + 1]) for r in range(pair) for j in far[::2]]
    for h in range(halves):
        spread(slab[h])
    rounds = ring - 1
    gate, loose, holding = (), (), None
    for k in range(1, rounds + 1):
        h_up, h_down = int(k > steps), int(k >= steps)
        top, bottom = ups[h_up][-1], downs[h_down][-1]
        if k <= halves:
            far_own = after(own[k - 1], [g for g in loose[-1:]])
            far_own = exchange(top_bit)(far_own)
            slab[k - 1][top_bit] = (far_own, None)
            loose = loose + (far_own,)
        if k == steps:
            first_wanted, rest = queue[:1], queue[1:]
            choose(0, first_wanted)
        if k >= steps and (k - steps) % 2 == 0 and queue:
            operator, operand, store = trade(0, *queue.pop(0))
            holding = (operator(after(operand, loose)), store)
            loose = ()
        if k == 3 or k > steps + 1:
            for operator, operand, store in take_near(4):
                result = operator(after(operand, gate, top, bottom))
                store(result)
                loose = loose + (result,)
        top, bottom = after((top, bottom), gate)
        if k > steps and (k - steps) % 2:
            gate = (holding[0],) if holding else ()
            if holding:
                holding[1](holding[0])
                holding = None
            if k == steps + 1:
                gate += (choose(0, rest + [(r, [0, 1]) for r in range(pair)]),)
        else:
            gate = ()
        ups[h_up].append(rise(top))
        downs[h_down].append(fall(bottom))
    ended = (ups[1][-1], downs[1][-1], gate, loose)
    if holding:
        holding[1](holding[0])
        ended = ended + (holding[0],)
    while queue:
        slot(trade(0, *queue.pop(0)))
    swaps = []

    def swap_job(j):
        store = passing if j & 1 else cols
        if j & 1:
            pass_on(1, j, 1)
        array, view = store[1][j, 0]
        return (swap, array, keep(store[1], (j, 1), view))

    first = choose(1, [(0, far[-1:])])
    turned_slab = None
    for j in reversed(far):
        slot(trade(1, 0, [j]), *swaps)
        if turned_slab is None:
            single = [(0, [i]) for i in far[:-1]]
            wanted = single + [(r, [0, 1]) for r in range(pair)] + [(1, far)]
            first = choose(1, wanted, first)
            whole_slab = [alone(slab[g][j]) for j in everyone for g in range(halves)]
            turned_slab = turn_blocks(after(whole_slab, first))
        swaps = [swap_job(j)]

    def own_rows(h):
        cases = [cols[h][j, r] for j in range(nodes) for r in range(pair)]
        piece = pick_rows(jnp.stack([z ^ node, y]), cases, pair, width)
        mine[h][0] = (piece, None)
        spread(mine[h])
        return (exchange(top_bit), piece, keep(mine[h], top_bit))

    def left_part(parts, earlier, first=False):
        blocks = [sent[h][j, r] for h, js in parts for j in js for r in range(pair)]
        theirs = [mine[h][j][0] for h, js in parts for j in js]
        return left_sum(blocks, theirs, earlier, first)

    def complete(h):
        return all((j, r) in cols[h] for j in range(nodes) for r in range(pair))

    def right_part(h):
        return right_sum(
            turned_slab, [cols[h][j, r] for j in everyone for r in range(pair)], pair
        )

    while not complete(0):
        slot()
    right_new = [right_part(0)]
    job = own_rows(0)
    slot(job, *swaps)
    ended = ended + (right_new[0],)
    while not complete(1):
        slot()
    job = own_rows(1)
    slot(job)
    right_new.append(right_part(1))
    ended = ended + (right_new[1],)
    while not all(j in mine[0] for j in everyone):
        slot()
    lows, highs = list(everyone)[:top_bit], list(everyone)[top_bit:]
    total = left_part([(0, lows)], left_old, True)
    while not all(j in mine[1] for j in lows):
        slot()
    total = left_part([(0, highs), (1, lows)], total)
    ended = ended + (total,)
    while near:
        slot()
    left_out = left_part([(1, highs)], total)

    right_new = jnp.stack(right_new, 1)
    right_new = jnp.where(y == 0, right_new, right_new[::-1]).reshape(right_old.shape)
    right_out = ema_decay * right_old + (1.0 - ema_decay) * right_new
    return (left_out, right_out)


def solution(mesh):
    placed = (P("dp", "node"), P("dp", None), P("node", "dp"), P("node", "dp"))
    return jax.shard_map(
        shards,
        mesh=mesh,
        in_specs=placed,
        out_specs=(P("node", "dp"), P("node", "dp")),
        check_vma=False,
    )
```

time: 280 us -> 268 us (0.957)
  local copies, waits for them, and re-layouts: 34.7 us -> 7.07 us
  Pallas kernels: 72.4 us -> 82.5 us
  waiting for transfers between devices: 116 us -> 122 us
    unnamed x121 -> x60, local copies, waits for them, and re-layouts: 30.8 us -> 6.9 us
    ppermute x14, starting transfers between devices: 20.9 us -> 27.8 us  [rise(): lax.ppermute(block, 'dp', [(order[k], order[(k + 1) % ring]) for k in ran...]
    pallas_call x21 -> x16, Pallas kernels: 58.8 us -> 65.3 us  [the longest x8 30.8 us: sum_round(): pl.pallas_call(functools.partial(sum_body, counts, parts), out_shape=[jax...]
    ppermute x14, starting transfers between devices: 10.9 us -> 5.84 us  [fall(): lax.ppermute(block, 'dp', [(order[(k + 1) % ring], order[k]) for k in ran...]
    ppermute x14, waiting for transfers between devices: 31.1 us -> 34.9 us  [fall(): lax.ppermute(block, 'dp', [(order[(k + 1) % ring], order[k]) for k in ran...]
    squeeze x6 -> x0, local copies, waits for them, and re-layouts: 3.76 us -> none  [alone(): return array if index is None else array[index]]
    pallas_call x2, Pallas kernels: 1.29 us -> 5.02 us  [pick_rows(): pl.pallas_call(functools.partial(rows_body, [view for _, view in cases],...]
    ppermute x24, waiting for transfers between devices: 20.6 us -> 23.8 us  [exchange(): return lambda block: lax.ppermute(block, 'node', pairs)]
  transfers between devices with their start and end apart: 54 -> 54, of which waited for: 32 -> 31; matrix products, arithmetic and copies ran while one was open for 4% -> 3% of each run, Pallas kernels for 23% -> 27%
where the time goes in v3:
time: 268 us; the launch traced here: 267 us
  waiting for transfers between devices  122 us (46%)
  Pallas kernels  82.5 us (31%)
  starting transfers between devices  47.3 us (18%)
  other arithmetic  7.32 us (3%)
  local copies, waits for them, and re-layouts  7.07 us (3%)
    ppermute x14, waiting for transfers between devices, rise(): lax.ppermute(block, 'dp', [(order[k], order[(k + 1) % ring]) for k in ran...  61.7 us
    ppermute x14, waiting for transfers between devices, fall(): lax.ppermute(block, 'dp', [(order[(k + 1) % ring], order[k]) for k in ran...  34.9 us
    pallas_call x8, Pallas kernels, sum_round(): pl.pallas_call(functools.partial(sum_body, counts, parts), out_shape=[jax...  30.8 us
    ppermute x14, starting transfers between devices, rise(): lax.ppermute(block, 'dp', [(order[k], order[(k + 1) % ring]) for k in ran...  27.8 us
    ppermute x24, waiting for transfers between devices, exchange(): return lambda block: lax.ppermute(block, 'node', pairs)  23.8 us
    pallas_call x3, Pallas kernels, left_sum(): pl.pallas_call(functools.partial(left_body, len(theirs), pair, first), ou...  15.5 us
    pallas_call x4, Pallas kernels, pick_blocks(): pl.pallas_call(functools.partial(pick_body, len(cases), groups), out_shap...  13.9 us
    pallas_call x2, Pallas kernels, right_sum(): pl.pallas_call(functools.partial(right_body, count, pair), out_shape=jax....  12.2 us
  transfers between devices with their start and end apart: 54, of which 31 were waited for; matrix products, arithmetic and copies ran while one was open for 3% of the time, Pallas kernels for 27%

profile of v3, /device:TPU:0, one launch (start us, length us, event | category | flops | bytes accessed | tf_op | source)
XLA Modules:
  0.0 267.0 jit_solution(13153668812583495606)
XLA Ops:
  0.7 1.6 copy-done
  2.3 3.5 %shard_map.140 = (bf16[1024,256]{1,0:T(8,128)(2,1)S(1)}, bf16[1024,256]{1,0:T(8,128)(2,1)S(1)}) custom-call(s32[8]{0:T(128)S(1)} %compare_select_fusion.10.slabs, bf16[1024,1024]{1,0:T(8,128)(2,1)S(1)} %copy-done, bf16[1024,4096]{1,0:T(8,128)(2,1)} %second.15, bf16[1024,4096]{1,0:T(8,128)(2,1)} %second.15), custom_call_target="tpu_custom_call" | custom-call | flops 1073741824 | tf_op jit(solution)/shard_map/pallas_call | solution.py:69
  5.8 3.1 %collective-permute-start = (bf16[1024,256]{1,0:T(8,128)(2,1)S(1)}, bf16[1024,256]{1,0:T(8,128)(2,1)S(1)}, u32[]{:S(2)}, u32[]{:S(2)}) collective-permute-start(bf16[1024,256]{1,0:T(8,128)(2,1)S(1)} %get-tuple-element.88), channel_id=1, source_target_pairs={{0,8},{8,16},{16,24},{24,28},{28,20},{20,12},{12,4},{4,0},{1,9},{9... | collective-permute-start | bytes 1572872 | tf_op jit(solution)/shard_map/ppermute | solution.py:306
  8.9 3.5 %shard_map.141 = (bf16[1024,256]{1,0:T(8,128)(2,1)S(1)}, bf16[1024,256]{1,0:T(8,128)(2,1)S(1)}) custom-call(s32[8]{0:T(128)S(1)} %compare_select_fusion.10.slabs, bf16[1024,1024]{1,0:T(8,128)(2,1)S(1)} %copy-done, bf16[1024,4096]{1,0:T(8,128)(2,1)} %second.15, bf16[1024,4096]{1,0:T(8,128)(2,1)} %second.15), custom_call_target="tpu_custom_call" | custom-call | flops 1073741824 | tf_op jit(solution)/shard_map/pallas_call | solution.py:69
  12.4 2.1 collective-permute-start.2
  14.5 7.1 %collective-permute-done.rest_0_ = bf16[1024,256]{1,0:T(8,128)(2,1)S(1)} collective-permute-done((bf16[1024,256]{1,0:T(8,128)(2,1)S(1)}, bf16[1024,256]{1,0:T(8,128)(2,1)S(1)}, u32[]{:S(2)}, u32[]{:S(2)}) %collective-permute-start) | collective-permute-done | bytes 524320 | tf_op jit(solution)/shard_map/ppermute | solution.py:306
  21.6 2.1 collective-permute-done.1.rest_1_
  23.7 4.1 %shard_map.142 = (bf16[1024,256]{1,0:T(8,128)(2,1)S(1)}, bf16[1024,256]{1,0:T(8,128)(2,1)S(1)}) custom-call(s32[8]{0:T(128)S(1)} %compare_select_fusion.10.slabs, bf16[1024,1024]{1,0:T(8,128)(2,1)S(1)} %copy-done, bf16[1024,4096]{1,0:T(8,128)(2,1)} %second.15, bf16[1024,4096]{1,0:T(8,128)(2,1)} %second.15, ...), custom_call_target="tpu_custom_call" | custom-call | flops 1073741824 | tf_op jit(solution)/shard_map/pallas_call | solution.py:69
  27.8 1.6 collective-permute-start.4
  29.9 2.9 %collective-permute-done.2.rest_0_ = bf16[1024,256]{1,0:T(8,128)(2,1)S(1)} collective-permute-done((bf16[1024,256]{1,0:T(8,128)(2,1)S(1)}, bf16[1024,256]{1,0:T(8,128)(2,1)S(1)}, u32[]{:S(2)}, u32[]{:S(2)}) %collective-permute-start.2) | collective-permute-done | bytes 524320 | tf_op jit(solution)/shard_map/ppermute | solution.py:306
  32.8 2.1 collective-permute-done.3.rest_1_
  35.0 4.1 %shard_map.143 = (bf16[1024,256]{1,0:T(8,128)(2,1)S(1)}, bf16[1024,256]{1,0:T(8,128)(2,1)S(1)}) custom-call(s32[8]{0:T(128)S(1)} %compare_select_fusion.10.slabs, bf16[1024,1024]{1,0:T(8,128)(2,1)S(1)} %copy-done, bf16[1024,4096]{1,0:T(8,128)(2,1)} %second.15, bf16[1024,4096]{1,0:T(8,128)(2,1)} %second.15, ...), custom_call_target="tpu_custom_call" | custom-call | flops 1073741824 | tf_op jit(solution)/shard_map/pallas_call | solution.py:69
  39.0 1.6 collective-permute-start.6
  41.1 2.9 %collective-permute-done.4.rest_0_ = bf16[1024,256]{1,0:T(8,128)(2,1)S(1)} collective-permute-done((bf16[1024,256]{1,0:T(8,128)(2,1)S(1)}, bf16[1024,256]{1,0:T(8,128)(2,1)S(1)}, u32[]{:S(2)}, u32[]{:S(2)}) %collective-permute-start.4) | collective-permute-done | bytes 524320 | tf_op jit(solution)/shard_map/ppermute | solution.py:306
  44.0 2.1 collective-permute-done.5.rest_1_
  46.2 4.1 %shard_map.144 = (bf16[1024,256]{1,0:T(8,128)(2,1)S(1)}, bf16[1024,256]{1,0:T(8,128)(2,1)S(1)}) custom-call(s32[8]{0:T(128)S(1)} %compare_select_fusion.10.slabs, bf16[1024,1024]{1,0:T(8,128)(2,1)S(1)} %copy-done, bf16[1024,4096]{1,0:T(8,128)(2,1)} %second.15, bf16[1024,4096]{1,0:T(8,128)(2,1)} %second.15, ...), custom_call_target="tpu_custom_call" | custom-call | flops 1073741824 | tf_op jit(solution)/shard_map/pallas_call | solution.py:69
  50.3 1.6 collective-permute-start.8
  52.4 2.9 %collective-permute-done.6.rest_0_ = bf16[1024,256]{1,0:T(8,128)(2,1)S(1)} collective-permute-done((bf16[1024,256]{1,0:T(8,128)(2,1)S(1)}, bf16[1024,256]{1,0:T(8,128)(2,1)S(1)}, u32[]{:S(2)}, u32[]{:S(2)}) %collective-permute-start.6) | collective-permute-done | bytes 524320 | tf_op jit(solution)/shard_map/ppermute | solution.py:306
  55.3 2.1 collective-permute-done.7.rest_1_
  57.4 4.1 %shard_map.145 = (bf16[1024,256]{1,0:T(8,128)(2,1)S(1)}, bf16[1024,256]{1,0:T(8,128)(2,1)S(1)}) custom-call(s32[8]{0:T(128)S(1)} %compare_select_fusion.10.slabs, bf16[1024,1024]{1,0:T(8,128)(2,1)S(1)} %copy-done, bf16[1024,4096]{1,0:T(8,128)(2,1)} %second.15, bf16[1024,4096]{1,0:T(8,128)(2,1)} %second.15, ...), custom_call_target="tpu_custom_call" | custom-call | flops 1073741824 | tf_op jit(solution)/shard_map/pallas_call | solution.py:69
  61.6 4.1 %collective-permute-done.8.rest_0_ = bf16[1024,256]{1,0:T(8,128)(2,1)S(1)} collective-permute-done((bf16[1024,256]{1,0:T(8,128)(2,1)S(1)}, bf16[1024,256]{1,0:T(8,128)(2,1)S(1)}, u32[]{:S(2)}, u32[]{:S(2)}) %collective-permute-start.8) | collective-permute-done | bytes 524320 | tf_op jit(solution)/shard_map/ppermute | solution.py:306
  65.7 3.0 %collective-permute-done.9.rest_1_ = bf16[1024,256]{1,0:T(8,128)(2,1)S(1)} collective-permute-done((bf16[1024,256]{1,0:T(8,128)(2,1)S(1)}, bf16[1024,256]{1,0:T(8,128)(2,1)S(1)}, u32[]{:S(2)}, u32[]{:S(2)}) %collective-permute-start.9) | collective-permute-done | bytes 524320 | tf_op jit(solution)/shard_map/ppermute | solution.py:311
  68.7 4.1 %shard_map.146 = (bf16[1024,256]{1,0:T(8,128)(2,1)S(1)}, bf16[1024,256]{1,0:T(8,128)(2,1)S(1)}) custom-call(s32[8]{0:T(128)S(1)} %compare_select_fusion.10.slabs, bf16[1024,1024]{1,0:T(8,128)(2,1)S(1)} %copy-done, bf16[1024,4096]{1,0:T(8,128)(2,1)} %second.15, bf16[1024,4096]{1,0:T(8,128)(2,1)} %second.15, ...), custom_call_target="tpu_custom_call" | custom-call | flops 1073741824 | tf_op jit(solution)/shard_map/pallas_call | solution.py:69
  72.7 1.6 collective-permute-start.10
  74.4 3.4 %shard_map.147 = (f32[1024,256]{1,0:T(8,128)S(1)}, f32[1024,256]{1,0:T(8,128)S(1)}) custom-call(s32[8]{0:T(128)S(1)} %compare_select_fusion.10.slabs, bf16[1024,1024]{1,0:T(8,128)(2,1)S(1)} %copy-done, bf16[1024,4096]{1,0:T(8,128)(2,1)} %second.15, bf16[1024,4096]{1,0:T(8,128)(2,1)} %second.15), custom_call_target="tpu_custom_call" | custom-call | flops 1073741824 | tf_op jit(solution)/shard_map/pallas_call | solution.py:69
  78.4 5.7 %collective-permute-done.10 = bf16[1024,256]{1,0:T(8,128)(2,1)S(1)} collective-permute-done((bf16[1024,256]{1,0:T(8,128)(2,1)S(1)}, bf16[1024,256]{1,0:T(8,128)(2,1)S(1)}, u32[]{:S(2)}, u32[]{:S(2)}) %collective-permute-start.10) | collective-permute-done | bytes 524320 | tf_op jit(solution)/shard_map/ppermute | solution.py:306
  84.8 1.6 collective-permute-start.15
  86.9 1.6 collective-permute-start.13
  88.9 10.8 %collective-permute-done.15.refs_7_ = bf16[1024,256]{1,0:T(8,128)(2,1)S(1)} collective-permute-done((bf16[1024,256]{1,0:T(8,128)(2,1)S(1)}, bf16[1024,256]{1,0:T(8,128)(2,1)S(1)}, u32[]{:S(2)}, u32[]{:S(2)}) %collective-permute-start.15) | collective-permute-done | bytes 524320 | tf_op jit(solution)/shard_map/ppermute | solution.py:306
  99.8 1.5 collective-permute-start.24
  101.3 1.6 collective-permute-start.17
  103.3 7.7 %collective-permute-done.13 = bf16[1024,256]{1,0:T(8,128)(2,1)S(1)} collective-permute-done((bf16[1024,256]{1,0:T(8,128)(2,1)S(1)}, bf16[1024,256]{1,0:T(8,128)(2,1)S(1)}, u32[]{:S(2)}, u32[]{:S(2)}) %collective-permute-start.13) | collective-permute-done | bytes 524320 | tf_op jit(solution)/shard_map/ppermute | solution.py:306
  112.4 1.6 collective-permute-start.25
  114.0 4.2 %collective-permute-done.17.refs_6_ = bf16[1024,256]{1,0:T(8,128)(2,1)} collective-permute-done((bf16[1024,256]{1,0:T(8,128)(2,1)S(1)}, bf16[1024,256]{1,0:T(8,128)(2,1)}, u32[]{:S(2)}, u32[]{:S(2)}) %collective-permute-start.17) | collective-permute-done | bytes 524320 | tf_op jit(solution)/shard_map/ppermute | solution.py:306
  118.7 1.6 collective-permute-start.19
  122.9 5.8 %collective-permute-done.19.refs_5_ = bf16[1024,256]{1,0:T(8,128)(2,1)S(1)} collective-permute-done((bf16[1024,256]{1,0:T(8,128)(2,1)}, bf16[1024,256]{1,0:T(8,128)(2,1)S(1)}, u32[]{:S(2)}, u32[]{:S(2)}) %collective-permute-start.19) | collective-permute-done | bytes 524320 | tf_op jit(solution)/shard_map/ppermute | solution.py:306
  129.6 4.3 %collective-permute-done.23.refs_3_ = bf16[1024,256]{1,0:T(8,128)(2,1)S(1)} collective-permute-done((bf16[1024,256]{1,0:T(8,128)(2,1)}, bf16[1024,256]{1,0:T(8,128)(2,1)S(1)}, u32[]{:S(2)}, u32[]{:S(2)}) %collective-permute-start.23) | collective-permute-done | bytes 524320 | tf_op jit(solution)/shard_map/ppermute | solution.py:311
  134.7 2.9 %shard_map.148.refs_0_.refs_2_ = bf16[2,1024,256]{2,1,0:T(8,128)(2,1)} custom-call(s32[2]{0:T(128)} %get-tuple-element.174.spots, bf16[1024,256]{1,0:T(8,128)(2,1)} %copy-done.1, bf16[1024,256]{1,0:T(8,128)(2,1)} %copy-done.21, bf16[1024,256]{1,0:T(8,128)(2,1)} %collective-permute-done.18.refs_2_, bf16[1024,256]{1,0:T(8,128)(2,1)} %copy-done.23, ...), custom_call_target="tpu_custom_call" | custom-call | tf_op jit(solution)/shard_map/pallas_call | solution.py:125
  137.6 1.6 collective-permute-start.29
  139.2 2.6 collective-permute-start.30
  142.3 2.6 collective-permute-start.22
  145.6 6.3 %collective-permute-done.30.refs_4_ = bf16[1024,256]{1,0:T(8,128)(2,1)S(1)} collective-permute-done((bf16[1024,256]{1,0:T(8,128)(2,1)}, bf16[1024,256]{1,0:T(8,128)(2,1)S(1)}, u32[]{:S(2)}, u32[]{:S(2)}) %collective-permute-start.30) | collective-permute-done | bytes 524320 | tf_op jit(solution)/shard_map/ppermute | solution.py:306
  152.7 4.3 %shard_map.149 = (bf16[2,1024,256]{2,1,0:T(8,128)(2,1)}, bf16[1024,256]{1,0:T(8,128)(2,1)}, bf16[1024,256]{1,0:T(8,128)(2,1)}, bf16[1024,256]{1,0:T(8,128)(2,1)}, bf16[1024,256]{1,0:T(8,128)(2,1)}) custom-call(s32[6]{0:T(128)} %pad_add_fusion.1.spots, bf16[1024,256]{1,0:T(8,128)(2,1)} %copy-done.1, bf16[1024,256]{1,0:T(8,128)(2,1)} %copy-done.21, ...), custom_call_target="tpu_custom_call" | custom-call | tf_op jit(solution)/shard_map/pallas_call | solution.py:125
  157.0 1.7 collective-permute-start.35
  160.8 2.7 %collective-permute-start.32 = (bf16[1024,256]{1,0:T(8,128)(2,1)}, bf16[1024,256]{1,0:T(8,128)(2,1)S(1)}, u32[]{:S(2)}, u32[]{:S(2)}) collective-permute-start(bf16[1024,256]{1,0:T(8,128)(2,1)} %collective-permute-done.22.refs_7_), channel_id=1, source_target_pairs={{0,8},{8,16},{16,24},{24,28},{28,20},{20,12},{12,4},{4,0},{1,9},{9... | collective-permute-start | bytes 1572872 | tf_op jit(solution)/shard_map/ppermute | solution.py:306
  164.0 6.8 %collective-permute-done.31.refs_3_ = bf16[1024,256]{1,0:T(8,128)(2,1)S(1)} collective-permute-done((bf16[1024,256]{1,0:T(8,128)(2,1)}, bf16[1024,256]{1,0:T(8,128)(2,1)S(1)}, u32[]{:S(2)}, u32[]{:S(2)}) %collective-permute-start.31) | collective-permute-done | bytes 524320 | tf_op jit(solution)/shard_map/ppermute | solution.py:311
  171.8 1.8 collective-permute-start.34
  173.6 2.6 collective-permute-done.35.refs_5_.refs_13_
  176.2 9.8 %collective-permute-done.33.refs_4_ = bf16[1024,256]{1,0:T(8,128)(2,1)S(1)} collective-permute-done((bf16[1024,256]{1,0:T(8,128)(2,1)S(1)}, bf16[1024,256]{1,0:T(8,128)(2,1)S(1)}, u32[]{:S(2)}, u32[]{:S(2)}) %collective-permute-start.33) | collective-permute-done | bytes 524320 | tf_op jit(solution)/shard_map/ppermute | solution.py:311
  187.0 2.2 shard_map.150.refs_2_
  190.5 4.6 %shard_map.151 = (bf16[1024,256]{1,0:T(8,128)(2,1)}, bf16[1024,256]{1,0:T(8,128)(2,1)}, bf16[1024,256]{1,0:T(8,128)(2,1)}, bf16[1024,256]{1,0:T(8,128)(2,1)}, bf...) custom-call(s32[7]{0:T(128)} %pad_add_fusion.spots, bf16[1024,256]{1,0:T(8,128)(2,1)} %copy-done.2, ...), custom_call_target="tpu_custom_call" | custom-call | tf_op jit(solution)/shard_map/pallas_call | solution.py:125
  195.0 8.6 %collective-permute-done.39 = bf16[1024,256]{1,0:T(8,128)(2,1)} collective-permute-done((bf16[1024,256]{1,0:T(8,128)(2,1)}, bf16[1024,256]{1,0:T(8,128)(2,1)}, u32[]{:S(2)}, u32[]{:S(2)}) %collective-permute-start.39) | collective-permute-done | bytes 524320 | tf_op jit(solution)/shard_map/ppermute | solution.py:320
  206.5 2.5 shard_map.153.refs_4_
  209.0 9.2 %collective-permute-done.43.refs_4_.refs_12_ = bf16[1024,256]{1,0:T(8,128)(2,1)S(1)} collective-permute-done((bf16[1024,256]{1,0:T(8,128)(2,1)}, bf16[1024,256]{1,0:T(8,128)(2,1)S(1)}, u32[]{:S(2)}, u32[]{:S(2)}) %collective-permute-start.43) | collective-permute-done | bytes 524320 | tf_op jit(solution)/shard_map/ppermute | solution.py:320
  221.6 5.0 %shard_map.154 = (bf16[256,1024]{1,0:T(8,128)(2,1)}, bf16[256,1024]{1,0:T(8,128)(2,1)}, bf16[256,1024]{1,0:T(8,128)(2,1)}, bf16[256,1024]{1,0:T(8,128)(2,1)}, bf...) custom-call(bf16[1024,256]{1,0:T(8,128)(2,1)} %copy-done.1, ...), custom_call_target="tpu_custom_call" | custom-call | tf_op jit(solution)/shard_map/pallas_call | solution.py:226
  226.7 6.1 %shard_map.155 = f32[2,256,512]{2,1,0:T(8,128)} custom-call(bf16[256,1024]{1,0:T(8,128)(2,1)} %get-tuple-element.163.refs_0_, bf16[256,1024]{1,0:T(8,128)(2,1)} %get-tuple-element.164.refs_1_, bf16[256,1024]{1,0:T(8,128)(2,1)} %get-tuple-element.165.refs_2_, bf16[256,1024]{1,0:T(8,128)(2,1)} %get-tuple-element.166.refs_3_, ...), custom_call_target="tpu_custom_call" | custom-call | flops 2147483648 | tf_op jit(solution)/shard_map/pallas_call | solution.py:267
  232.9 2.2 collective-permute-done.48.refs_8_
  235.2 2.5 shard_map.152.refs_10_
  238.9 4.6 %shard_map.157.refs_12_ = f32[1024,512]{1,0:T(8,128)} custom-call(bf16[1024,256]{1,0:T(8,128)(2,1)} %get-tuple-element.152.refs_0_.refs_8_, bf16[1024,256]{1,0:T(8,128)(2,1)} %get-tuple-element.153.refs_1_.refs_9_, bf16[1024,256]{1,0:T(8,128)(2,1)} %get-tuple-element.140.refs_2_, bf16[1024,256]{1,0:T(8,128)(2,1)} %get-tuple-element.142.refs_3_, ...), custom_call_target="tpu_custom_call" | custom-call | flops 1073741824 | tf_op jit(solution)/shard_map/pallas_call | solution.py:201
  243.5 6.2 %shard_map.156 = f32[2,256,512]{2,1,0:T(8,128)} custom-call(bf16[256,1024]{1,0:T(8,128)(2,1)} %get-tuple-element.163.refs_0_, bf16[256,1024]{1,0:T(8,128)(2,1)} %get-tuple-element.164.refs_1_, bf16[256,1024]{1,0:T(8,128)(2,1)} %get-tuple-element.165.refs_2_, bf16[256,1024]{1,0:T(8,128)(2,1)} %get-tuple-element.166.refs_3_, ...), custom_call_target="tpu_custom_call" | custom-call | flops 2147483648 | tf_op jit(solution)/shard_map/pallas_call | solution.py:267
  251.1 6.4 %shard_map.158.refs_6_ = f32[1024,512]{1,0:T(8,128)} custom-call(bf16[2,1024,256]{2,1,0:T(8,128)(2,1)} %shard_map.148.refs_0_.refs_2_, bf16[2,1024,256]{2,1,0:T(8,128)(2,1)} %get-tuple-element.127.refs_1_.refs_3_, bf16[2,1024,256]{2,1,0:T(8,128)(2,1)} %shard_map.148.refs_0_.refs_2_, bf16[2,1024,256]{2,1,0:T(8,128)(2,1)} %get-tuple-element.127.refs_1_.refs_3_, ...), custom_call_target="tpu_custom_call" | custom-call | flops 2147483648 | tf_op jit(solution)/shard_map/pallas_call | solution.py:201
  258.5 1.4 copy-done.7
  259.9 1.8 bitcast_add_fusion
  262.5 4.5 %shard_map.159 = f32[1024,512]{1,0:T(8,128)} custom-call(bf16[1024,256]{1,0:T(8,128)(2,1)} %get-tuple-element.148.refs_0_, bf16[2,1024,256]{2,1,0:T(8,128)(2,1)} %get-tuple-element.134.refs_1_.refs_3_, bf16[1024,256]{1,0:T(8,128)(2,1)} %shard_map.150.refs_2_, bf16[2,1024,256]{2,1,0:T(8,128)(2,1)} %get-tuple-element.134.refs_1_.refs_3_, ...), custom_call_target="tpu_custom_call" | custom-call | flops 1073741824 | tf_op jit(solution)/shard_map/pallas_call | solution.py:201
  (136 shorter events, 28.8 us)
Async XLA Ops:
  5.8 15.8 %collective-permute-start = (bf16[1024,256]{1,0:T(8,128)(2,1)S(1)}, bf16[1024,256]{1,0:T(8,128)(2,1)S(1)}, u32[]{:S(2)}, u32[]{:S(2)}) collective-permute-start(bf16[1024,256]{1,0:T(8,128)(2,1)S(1)} %get-tuple-element.88), channel_id=1, source_target_pairs={{0,8},{8,16},{16,24},{24,28},{28,20},{20,12},{12,4},{4,0},{1,9},{9... | collective-permute-start | bytes 1572872 | tf_op jit(solution)/shard_map/ppermute | solution.py:306
  8.9 14.8 %collective-permute-start.1 = (bf16[1024,256]{1,0:T(8,128)(2,1)S(1)}, bf16[1024,256]{1,0:T(8,128)(2,1)S(1)}, u32[]{:S(2)}, u32[]{:S(2)}) collective-permute-start(bf16[1024,256]{1,0:T(8,128)(2,1)S(1)} %get-tuple-element.89), channel_id=1, source_target_pairs={{8,0},{16,8},{24,16},{28,24},{20,28},{12,20},{4,12},{0,4},{9,1},{1... | collective-permute-start | bytes 1572872 | tf_op jit(solution)/shard_map/ppermute | solution.py:311
  12.4 20.4 %collective-permute-start.2 = (bf16[1024,256]{1,0:T(8,128)(2,1)S(1)}, bf16[1024,256]{1,0:T(8,128)(2,1)S(1)}, u32[]{:S(2)}, u32[]{:S(2)}) collective-permute-start(bf16[1024,256]{1,0:T(8,128)(2,1)S(1)} %get-tuple-element.91), channel_id=1, source_target_pairs={{0,8},{8,16},{16,24},{24,28},{28,20},{20,12},{12,4},{4,0},{1,9},{9... | collective-permute-start | bytes 1572872 | tf_op jit(solution)/shard_map/ppermute | solution.py:306
  14.5 20.5 %collective-permute-start.3 = (bf16[1024,256]{1,0:T(8,128)(2,1)S(1)}, bf16[1024,256]{1,0:T(8,128)(2,1)S(1)}, u32[]{:S(2)}, u32[]{:S(2)}) collective-permute-start(bf16[1024,256]{1,0:T(8,128)(2,1)S(1)} %get-tuple-element.92), channel_id=1, source_target_pairs={{8,0},{16,8},{24,16},{28,24},{20,28},{12,20},{4,12},{0,4},{9,1},{1... | collective-permute-start | bytes 1572872 | tf_op jit(solution)/shard_map/ppermute | solution.py:311
  27.8 16.2 %collective-permute-start.4 = (bf16[1024,256]{1,0:T(8,128)(2,1)S(1)}, bf16[1024,256]{1,0:T(8,128)(2,1)S(1)}, u32[]{:S(2)}, u32[]{:S(2)}) collective-permute-start(bf16[1024,256]{1,0:T(8,128)(2,1)S(1)} %get-tuple-element.94), channel_id=1, source_target_pairs={{0,8},{8,16},{16,24},{24,28},{28,20},{20,12},{12,4},{4,0},{1,9},{9... | collective-permute-start | bytes 1572872 | tf_op jit(solution)/shard_map/ppermute | solution.py:306
  29.4 16.8 %collective-permute-start.5 = (bf16[1024,256]{1,0:T(8,128)(2,1)S(1)}, bf16[1024,256]{1,0:T(8,128)(2,1)S(1)}, u32[]{:S(2)}, u32[]{:S(2)}) collective-permute-start(bf16[1024,256]{1,0:T(8,128)(2,1)S(1)} %get-tuple-element.95), channel_id=1, source_target_pairs={{8,0},{16,8},{24,16},{28,24},{20,28},{12,20},{4,12},{0,4},{9,1},{1... | collective-permute-start | bytes 1572872 | tf_op jit(solution)/shard_map/ppermute | solution.py:311
  39.0 16.2 %collective-permute-start.6 = (bf16[1024,256]{1,0:T(8,128)(2,1)S(1)}, bf16[1024,256]{1,0:T(8,128)(2,1)S(1)}, u32[]{:S(2)}, u32[]{:S(2)}) collective-permute-start(bf16[1024,256]{1,0:T(8,128)(2,1)S(1)} %get-tuple-element.97), channel_id=1, source_target_pairs={{0,8},{8,16},{16,24},{24,28},{28,20},{20,12},{12,4},{4,0},{1,9},{9... | collective-permute-start | bytes 1572872 | tf_op jit(solution)/shard_map/ppermute | solution.py:306
  40.7 16.8 %collective-permute-start.7 = (bf16[1024,256]{1,0:T(8,128)(2,1)S(1)}, bf16[1024,256]{1,0:T(8,128)(2,1)S(1)}, u32[]{:S(2)}, u32[]{:S(2)}) collective-permute-start(bf16[1024,256]{1,0:T(8,128)(2,1)S(1)} %get-tuple-element.98), channel_id=1, source_target_pairs={{8,0},{16,8},{24,16},{28,24},{20,28},{12,20},{4,12},{0,4},{9,1},{1... | collective-permute-start | bytes 1572872 | tf_op jit(solution)/shard_map/ppermute | solution.py:311
  50.3 15.4 %collective-permute-start.8 = (bf16[1024,256]{1,0:T(8,128)(2,1)S(1)}, bf16[1024,256]{1,0:T(8,128)(2,1)S(1)}, u32[]{:S(2)}, u32[]{:S(2)}) collective-permute-start(bf16[1024,256]{1,0:T(8,128)(2,1)S(1)} %get-tuple-element.100), channel_id=1, source_target_pairs={{0,8},{8,16},{16,24},{24,28},{28,20},{20,12},{12,4},{4,0},{1,9},{9... | collective-permute-start | bytes 1572872 | tf_op jit(solution)/shard_map/ppermute | solution.py:306
  51.9 16.8 %collective-permute-start.9 = (bf16[1024,256]{1,0:T(8,128)(2,1)S(1)}, bf16[1024,256]{1,0:T(8,128)(2,1)S(1)}, u32[]{:S(2)}, u32[]{:S(2)}) collective-permute-start(bf16[1024,256]{1,0:T(8,128)(2,1)S(1)} %get-tuple-element.101), channel_id=1, source_target_pairs={{8,0},{16,8},{24,16},{28,24},{20,28},{12,20},{4,12},{0,4},{9,1},{1... | collective-permute-start | bytes 1572872 | tf_op jit(solution)/shard_map/ppermute | solution.py:311
  61.5 16.9 %collective-permute-start.11 = (bf16[1024,256]{1,0:T(8,128)(2,1)S(1)}, bf16[1024,256]{1,0:T(8,128)(2,1)S(1)}, u32[]{:S(2)}, u32[]{:S(2)}) collective-permute-start(bf16[1024,256]{1,0:T(8,128)(2,1)S(1)} %get-tuple-element.104), channel_id=1, source_target_pairs={{8,0},{16,8},{24,16},{28,24},{20,28},{12,20},{4,12},{0,4},{9,1},{1... | collective-permute-start | bytes 1572872 | tf_op jit(solution)/shard_map/ppermute | solution.py:311
  72.7 11.4 %collective-permute-start.10 = (bf16[1024,256]{1,0:T(8,128)(2,1)S(1)}, bf16[1024,256]{1,0:T(8,128)(2,1)S(1)}, u32[]{:S(2)}, u32[]{:S(2)}) collective-permute-start(bf16[1024,256]{1,0:T(8,128)(2,1)S(1)} %get-tuple-element.106), channel_id=1, source_target_pairs={{0,8},{8,16},{16,24},{24,28},{28,20},{20,12},{12,4},{4,0},{1,9},{9... | collective-permute-start | bytes 1572872 | tf_op jit(solution)/shard_map/ppermute | solution.py:306
  77.8 44.5 %copy-start.29 = (s32[2]{0:T(128)S(1)}, s32[2]{0:T(128)}, u32[]{:S(2)}) copy-start(s32[2]{0:T(128)} %constant.135.clone) | copy-start | bytes 28
  84.8 49.1 %copy-start.1 = (bf16[1024,256]{1,0:T(8,128)(2,1)}, bf16[1024,256]{1,0:T(8,128)(2,1)S(1)}, u32[]{:S(2)}) copy-start(bf16[1024,256]{1,0:T(8,128)(2,1)S(1)} %fusion.15.refs_0_.refs_4_) | copy-start | bytes 1572868
  84.8 14.9 %collective-permute-start.15 = (bf16[1024,256]{1,0:T(8,128)(2,1)S(1)}, bf16[1024,256]{1,0:T(8,128)(2,1)S(1)}, u32[]{:S(2)}, u32[]{:S(2)}) collective-permute-start(bf16[1024,256]{1,0:T(8,128)(2,1)S(1)} %fusion.15.refs_0_.refs_4_), channel_id=1, source_target_pairs={{0,8},{8,16},{16,24},{24,28},{28,20},{20,12},{12,4},{4,0},{1,9},{9... | collective-permute-start | bytes 1572872 | tf_op jit(solution)/shard_map/ppermute | solution.py:306
  86.5 14.8 %collective-permute-start.16 = (bf16[1024,256]{1,0:T(8,128)(2,1)S(1)}, bf16[1024,256]{1,0:T(8,128)(2,1)S(1)}, u32[]{:S(2)}, u32[]{:S(2)}) collective-permute-start(bf16[1024,256]{1,0:T(8,128)(2,1)S(1)} %fusion.15.refs_0_.refs_4_), channel_id=1, source_target_pairs={{8,0},{16,8},{24,16},{28,24},{20,28},{12,20},{4,12},{0,4},{9,1},{1... | collective-permute-start | bytes 1572872 | tf_op jit(solution)/shard_map/ppermute | solution.py:311
  86.9 15.9 %collective-permute-start.12 = (bf16[1024,256]{1,0:T(8,128)(2,1)S(1)}, bf16[1024,256]{1,0:T(8,128)(2,1)S(1)}, u32[]{:S(2)}, u32[]{:S(2)}) collective-permute-start(bf16[1024,256]{1,0:T(8,128)(2,1)S(1)} %fusion.15.refs_0_.refs_4_), channel_id=1, source_target_pairs={{0,1},{1,0},{2,3},{3,2},{4,5},{5,4},{6,7},{7,6},{8,9},{9,8},{10,11... | collective-permute-start | bytes 1572872 | tf_op jit(solution)/shard_map/ppermute | solution.py:320
  86.9 24.1 %collective-permute-start.13 = (bf16[1024,256]{1,0:T(8,128)(2,1)S(1)}, bf16[1024,256]{1,0:T(8,128)(2,1)S(1)}, u32[]{:S(2)}, u32[]{:S(2)}) collective-permute-start(bf16[1024,256]{1,0:T(8,128)(2,1)S(1)} %get-tuple-element.103), channel_id=1, source_target_pairs={{0,8},{8,16},{16,24},{24,28},{28,20},{20,12},{12,4},{4,0},{1,9},{9... | collective-permute-start | bytes 1572872 | tf_op jit(solution)/shard_map/ppermute | solution.py:306
  88.5 23.2 %collective-permute-start.14 = (bf16[1024,256]{1,0:T(8,128)(2,1)S(1)}, bf16[1024,256]{1,0:T(8,128)(2,1)S(1)}, u32[]{:S(2)}, u32[]{:S(2)}) collective-permute-start(bf16[1024,256]{1,0:T(8,128)(2,1)S(1)} %get-tuple-element.107), channel_id=1, source_target_pairs={{8,0},{16,8},{24,16},{28,24},{20,28},{12,20},{4,12},{0,4},{9,1},{1... | collective-permute-start | bytes 1572872 | tf_op jit(solution)/shard_map/ppermute | solution.py:311
  99.8 34.1 %copy-start.20 = (bf16[1024,256]{1,0:T(8,128)(2,1)}, bf16[1024,256]{1,0:T(8,128)(2,1)S(1)}, u32[]{:S(2)}) copy-start(bf16[1024,256]{1,0:T(8,128)(2,1)S(1)} %collective-permute-done.15.refs_7_) | copy-start | bytes 1572868
  99.8 12.7 %collective-permute-start.24 = (bf16[1024,256]{1,0:T(8,128)(2,1)S(1)}, bf16[1024,256]{1,0:T(8,128)(2,1)}, u32[]{:S(2)}, u32[]{:S(2)}) collective-permute-start(bf16[1024,256]{1,0:T(8,128)(2,1)S(1)} %fusion.15.refs_0_.refs_4_), channel_id=1, source_target_pairs={{0,2},{1,3},{2,0},{3,1},{4,6},{5,7},{6,4},{7,5},{8,10},{9,11},{10,... | collective-permute-start | bytes 1572872 | tf_op jit(solution)/shard_map/ppermute | solution.py:320
  101.3 32.6 %copy-start.21 = (bf16[1024,256]{1,0:T(8,128)(2,1)}, bf16[1024,256]{1,0:T(8,128)(2,1)S(1)}, u32[]{:S(2)}) copy-start(bf16[1024,256]{1,0:T(8,128)(2,1)S(1)} %collective-permute-done.16.refs_1_) | copy-start | bytes 1572868
  101.3 17.0 %collective-permute-start.17 = (bf16[1024,256]{1,0:T(8,128)(2,1)S(1)}, bf16[1024,256]{1,0:T(8,128)(2,1)}, u32[]{:S(2)}, u32[]{:S(2)}) collective-permute-start(bf16[1024,256]{1,0:T(8,128)(2,1)S(1)} %collective-permute-done.15.refs_7_), channel_id=1, source_target_pairs={{0,8},{8,16},{16,24},{24,28},{28,20},{20,12},{12,4},{4,0},{1,9},{9... | collective-permute-start | bytes 1572872 | tf_op jit(solution)/shard_map/ppermute | solution.py:306
  102.8 19.0 %copy-start.28 = (bf16[1024,256]{1,0:T(8,128)(2,1)}, bf16[1024,256]{1,0:T(8,128)(2,1)S(1)}, u32[]{:S(2)}) copy-start(bf16[1024,256]{1,0:T(8,128)(2,1)S(1)} %collective-permute-done.12.refs_2_) | copy-start | bytes 1572868
  102.8 15.9 %collective-permute-start.18 = (bf16[1024,256]{1,0:T(8,128)(2,1)S(1)}, bf16[1024,256]{1,0:T(8,128)(2,1)}, u32[]{:S(2)}, u32[]{:S(2)}) collective-permute-start(bf16[1024,256]{1,0:T(8,128)(2,1)S(1)} %collective-permute-done.16.refs_1_), channel_id=1, source_target_pairs={{8,0},{16,8},{24,16},{28,24},{20,28},{12,20},{4,12},{0,4},{9,1},{1... | collective-permute-start | bytes 1572872 | tf_op jit(solution)/shard_map/ppermute | solution.py:311
  112.4 29.9 %copy-start.2 = (bf16[1024,256]{1,0:T(8,128)(2,1)}, bf16[1024,256]{1,0:T(8,128)(2,1)S(1)}, u32[]{:S(2)}) copy-start(bf16[1024,256]{1,0:T(8,128)(2,1)S(1)} %fusion.18.refs_0_.refs_1_) | copy-start | bytes 1572868
  112.4 9.4 %collective-permute-start.25 = (bf16[1024,256]{1,0:T(8,128)(2,1)S(1)}, bf16[1024,256]{1,0:T(8,128)(2,1)}, u32[]{:S(2)}, u32[]{:S(2)}) collective-permute-start(bf16[1024,256]{1,0:T(8,128)(2,1)S(1)} %fusion.18.refs_0_.refs_1_), channel_id=1, source_target_pairs={{0,2},{1,3},{2,0},{3,1},{4,6},{5,7},{6,4},{7,5},{8,10},{9,11},{10,... | collective-permute-start | bytes 1572872 | tf_op jit(solution)/shard_map/ppermute | solution.py:320
  118.7 10.1 %collective-permute-start.19 = (bf16[1024,256]{1,0:T(8,128)(2,1)}, bf16[1024,256]{1,0:T(8,128)(2,1)S(1)}, u32[]{:S(2)}, u32[]{:S(2)}) collective-permute-start(bf16[1024,256]{1,0:T(8,128)(2,1)} %collective-permute-done.17.refs_6_), channel_id=1, source_target_pairs={{0,8},{8,16},{16,24},{24,28},{28,20},{20,12},{12,4},{4,0},{1,9},{9... | collective-permute-start | bytes 1572872 | tf_op jit(solution)/shard_map/ppermute | solution.py:306
  120.3 13.6 %collective-permute-start.23 = (bf16[1024,256]{1,0:T(8,128)(2,1)}, bf16[1024,256]{1,0:T(8,128)(2,1)S(1)}, u32[]{:S(2)}, u32[]{:S(2)}) collective-permute-start(bf16[1024,256]{1,0:T(8,128)(2,1)} %collective-permute-done.18.refs_2_), channel_id=1, source_target_pairs={{8,0},{16,8},{24,16},{28,24},{20,28},{12,20},{4,12},{0,4},{9,1},{1... | collective-permute-start | bytes 1572872 | tf_op jit(solution)/shard_map/ppermute | solution.py:311
  120.7 16.9 %collective-permute-start.26 = (bf16[1024,256]{1,0:T(8,128)(2,1)}, bf16[1024,256]{1,0:T(8,128)(2,1)}, u32[]{:S(2)}, u32[]{:S(2)}) collective-permute-start(bf16[1024,256]{1,0:T(8,128)(2,1)} %collective-permute-done.24.refs_4_), channel_id=1, source_target_pairs={{0,1},{1,0},{2,3},{3,2},{4,5},{5,4},{6,7},{7,6},{8,9},{9,8},{10,11... | collective-permute-start | bytes 1572872 | tf_op jit(solution)/shard_map/ppermute | solution.py:320
  121.8 15.8 %collective-permute-start.28 = (bf16[1024,256]{1,0:T(8,128)(2,1)}, bf16[1024,256]{1,0:T(8,128)(2,1)}, u32[]{:S(2)}, u32[]{:S(2)}) collective-permute-start(bf16[1024,256]{1,0:T(8,128)(2,1)} %collective-permute-done.25.refs_5_), channel_id=1, source_target_pairs={{0,1},{1,0},{2,3},{3,2},{4,5},{5,4},{6,7},{7,6},{8,9},{9,8},{10,11... | collective-permute-start | bytes 1572872 | tf_op jit(solution)/shard_map/ppermute | solution.py:320
  121.8 15.8 %collective-permute-start.27 = (bf16[1024,256]{1,0:T(8,128)(2,1)S(1)}, bf16[1024,256]{1,0:T(8,128)(2,1)}, u32[]{:S(2)}, u32[]{:S(2)}) collective-permute-start(bf16[1024,256]{1,0:T(8,128)(2,1)S(1)} %fusion.18.refs_0_.refs_1_), channel_id=1, source_target_pairs={{0,1},{1,0},{2,3},{3,2},{4,5},{5,4},{6,7},{7,6},{8,9},{9,8},{10,11... | collective-permute-start | bytes 1572872 | tf_op jit(solution)/shard_map/ppermute | solution.py:320
  128.8 13.6 %collective-permute-start.20 = (bf16[1024,256]{1,0:T(8,128)(2,1)S(1)}, bf16[1024,256]{1,0:T(8,128)(2,1)S(1)}, u32[]{:S(2)}, u32[]{:S(2)}) collective-permute-start(bf16[1024,256]{1,0:T(8,128)(2,1)S(1)} %fusion.18.refs_0_.refs_1_), channel_id=1, source_target_pairs={{8,0},{16,8},{24,16},{28,24},{20,28},{12,20},{4,12},{0,4},{9,1},{1... | collective-permute-start | bytes 1572872 | tf_op jit(solution)/shard_map/ppermute | solution.py:311
  137.6 22.2 %collective-permute-start.29 = (bf16[2,1024,256]{2,1,0:T(8,128)(2,1)}, bf16[2,1024,256]{2,1,0:T(8,128)(2,1)S(1)}, u32[]{:S(2)}, u32[]{:S(2)}) collective-permute-start(bf16[2,1024,256]{2,1,0:T(8,128)(2,1)} %shard_map.148.refs_0_.refs_2_), channel_id=1, source_target_pairs={{0,2},{1,3},{2,0},{3,1},{4,6},{5,7},{6,4},{7,5},{8,10},{9,11},{10,... | collective-permute-start | bytes 3145736 | tf_op jit(solution)/shard_map/ppermute | solution.py:320
  139.2 12.7 %collective-permute-start.30 = (bf16[1024,256]{1,0:T(8,128)(2,1)}, bf16[1024,256]{1,0:T(8,128)(2,1)S(1)}, u32[]{:S(2)}, u32[]{:S(2)}) collective-permute-start(bf16[1024,256]{1,0:T(8,128)(2,1)} %copy-done.22), channel_id=1, source_target_pairs={{0,8},{8,16},{16,24},{24,28},{28,20},{20,12},{12,4},{4,0},{1,9},{9... | collective-permute-start | bytes 1572872 | tf_op jit(solution)/shard_map/ppermute | solution.py:306
  142.3 16.3 %collective-permute-start.21 = (bf16[1024,256]{1,0:T(8,128)(2,1)S(1)}, bf16[1024,256]{1,0:T(8,128)(2,1)}, u32[]{:S(2)}, u32[]{:S(2)}) collective-permute-start(bf16[1024,256]{1,0:T(8,128)(2,1)S(1)} %collective-permute-done.20.refs_1_), channel_id=1, source_target_pairs={{8,0},{16,8},{24,16},{28,24},{20,28},{12,20},{4,12},{0,4},{9,1},{1... | collective-permute-start | bytes 1572872 | tf_op jit(solution)/shard_map/ppermute | solution.py:311
  142.3 17.5 %collective-permute-start.22 = (bf16[1024,256]{1,0:T(8,128)(2,1)S(1)}, bf16[1024,256]{1,0:T(8,128)(2,1)}, u32[]{:S(2)}, u32[]{:S(2)}) collective-permute-start(bf16[1024,256]{1,0:T(8,128)(2,1)S(1)} %fusion.18.refs_0_.refs_1_), channel_id=1, source_target_pairs={{0,8},{8,16},{16,24},{24,28},{28,20},{20,12},{12,4},{4,0},{1,9},{9... | collective-permute-start | bytes 1572872 | tf_op jit(solution)/shard_map/ppermute | solution.py:306
  157.0 19.2 %collective-permute-start.35 = (bf16[2,1024,256]{2,1,0:T(8,128)(2,1)}, bf16[2,1024,256]{2,1,0:T(8,128)(2,1)S(1)}, u32[]{:S(2)}, u32[]{:S(2)}) collective-permute-start(bf16[2,1024,256]{2,1,0:T(8,128)(2,1)} %get-tuple-element.127.refs_1_.refs_3_), channel_id=1, source_target_pairs={{0,2},{1,3},{2,0},{3,1},{4,6},{5,7},{6,4},{7,5},{8,10},{9,11},{10,... | collective-permute-start | bytes 3145736 | tf_op jit(solution)/shard_map/ppermute | solution.py:320
  159.9 29.4 %copy-start.3 = (bf16[2,1024,256]{2,1,0:T(8,128)(2,1)}, bf16[2,1024,256]{2,1,0:T(8,128)(2,1)S(1)}, u32[]{:S(2)}) copy-start(bf16[2,1024,256]{2,1,0:T(8,128)(2,1)S(1)} %collective-permute-done.29.refs_4_.refs_12_) | copy-start | bytes 3145732
  159.9 11.0 %collective-permute-start.31 = (bf16[1024,256]{1,0:T(8,128)(2,1)}, bf16[1024,256]{1,0:T(8,128)(2,1)S(1)}, u32[]{:S(2)}, u32[]{:S(2)}) collective-permute-start(bf16[1024,256]{1,0:T(8,128)(2,1)} %collective-permute-done.21.refs_2_), channel_id=1, source_target_pairs={{8,0},{16,8},{24,16},{28,24},{20,28},{12,20},{4,12},{0,4},{9,1},{1... | collective-permute-start | bytes 1572872 | tf_op jit(solution)/shard_map/ppermute | solution.py:311
  160.8 10.1 %collective-permute-start.32 = (bf16[1024,256]{1,0:T(8,128)(2,1)}, bf16[1024,256]{1,0:T(8,128)(2,1)S(1)}, u32[]{:S(2)}, u32[]{:S(2)}) collective-permute-start(bf16[1024,256]{1,0:T(8,128)(2,1)} %collective-permute-done.22.refs_7_), channel_id=1, source_target_pairs={{0,8},{8,16},{16,24},{24,28},{28,20},{20,12},{12,4},{4,0},{1,9},{9... | collective-permute-start | bytes 1572872 | tf_op jit(solution)/shard_map/ppermute | solution.py:306
  163.5 8.3 %collective-permute-start.37 = (bf16[1024,256]{1,0:T(8,128)(2,1)}, bf16[1024,256]{1,0:T(8,128)(2,1)}, u32[]{:S(2)}, u32[]{:S(2)}) collective-permute-start(bf16[1024,256]{1,0:T(8,128)(2,1)} %get-tuple-element.140.refs_2_), channel_id=1, source_target_pairs={{0,1},{1,0},{2,3},{3,2},{4,5},{5,4},{6,7},{7,6},{8,9},{9,8},{10,11... | collective-permute-start | bytes 1572872 | tf_op jit(solution)/shard_map/ppermute | solution.py:320
  163.5 22.5 %collective-permute-start.36 = (bf16[2,1024,256]{2,1,0:T(8,128)(2,1)S(1)}, bf16[2,1024,256]{2,1,0:T(8,128)(2,1)S(1)}, u32[]{:S(2)}, u32[]{:S(2)}) collective-permute-start(bf16[2,1024,256]{2,1,0:T(8,128)(2,1)S(1)} %collective-permute-done.29.refs_4_.refs_12_), channel_id=1, source_target_pairs={{0,1},{1,0},{2,3},{3,2},{4,5},{5,4},{6,7},{7,6},{8,9},{9,8},{10,11... | collective-permute-start | bytes 3145736 | tf_op jit(solution)/shard_map/ppermute | solution.py:320
  170.8 15.2 %copy-start.9 = (bf16[1024,256]{1,0:T(8,128)(2,1)}, bf16[1024,256]{1,0:T(8,128)(2,1)S(1)}, u32[]{:S(2)}) copy-start(bf16[1024,256]{1,0:T(8,128)(2,1)S(1)} %collective-permute-done.31.refs_3_) | copy-start | bytes 1572868
  170.8 2.7 %collective-permute-start.38 = (bf16[1024,256]{1,0:T(8,128)(2,1)}, bf16[1024,256]{1,0:T(8,128)(2,1)S(1)}, u32[]{:S(2)}, u32[]{:S(2)}) collective-permute-start(bf16[1024,256]{1,0:T(8,128)(2,1)} %get-tuple-element.142.refs_3_), channel_id=1, source_target_pairs={{0,1},{1,0},{2,3},{3,2},{4,5},{5,4},{6,7},{7,6},{8,9},{9,8},{10,11... | collective-permute-start | bytes 1572872 | tf_op jit(solution)/shard_map/ppermute | solution.py:320
  170.9 15.2 %collective-permute-start.33 = (bf16[1024,256]{1,0:T(8,128)(2,1)S(1)}, bf16[1024,256]{1,0:T(8,128)(2,1)S(1)}, u32[]{:S(2)}, u32[]{:S(2)}) collective-permute-start(bf16[1024,256]{1,0:T(8,128)(2,1)S(1)} %collective-permute-done.31.refs_3_), channel_id=1, source_target_pairs={{8,0},{16,8},{24,16},{28,24},{20,28},{12,20},{4,12},{0,4},{9,1},{1... | collective-permute-start | bytes 1572872 | tf_op jit(solution)/shard_map/ppermute | solution.py:311
  171.8 14.2 %collective-permute-start.34 = (bf16[1024,256]{1,0:T(8,128)(2,1)S(1)}, bf16[1024,256]{1,0:T(8,128)(2,1)S(1)}, u32[]{:S(2)}, u32[]{:S(2)}) collective-permute-start(bf16[1024,256]{1,0:T(8,128)(2,1)S(1)} %collective-permute-done.32.refs_6_), channel_id=1, source_target_pairs={{0,8},{8,16},{16,24},{24,28},{28,20},{20,12},{12,4},{4,0},{1,9},{9... | collective-permute-start | bytes 1572872 | tf_op jit(solution)/shard_map/ppermute | solution.py:306
  187.0 16.6 %collective-permute-start.40 = (bf16[2,1024,256]{2,1,0:T(8,128)(2,1)S(1)}, bf16[2,1024,256]{2,1,0:T(8,128)(2,1)}, u32[]{:S(2)}, u32[]{:S(2)}) collective-permute-start(bf16[2,1024,256]{2,1,0:T(8,128)(2,1)S(1)} %collective-permute-done.35.refs_5_.refs_13_), channel_id=1, source_target_pairs={{0,1},{1,0},{2,3},{3,2},{4,5},{5,4},{6,7},{7,6},{8,9},{9,8},{10,11... | collective-permute-start | bytes 3145736 | tf_op jit(solution)/shard_map/ppermute | solution.py:320
  189.3 14.4 %collective-permute-start.39 = (bf16[1024,256]{1,0:T(8,128)(2,1)}, bf16[1024,256]{1,0:T(8,128)(2,1)}, u32[]{:S(2)}, u32[]{:S(2)}) collective-permute-start(bf16[1024,256]{1,0:T(8,128)(2,1)} %shard_map.150.refs_2_), channel_id=1, source_target_pairs={{0,2},{1,3},{2,0},{3,1},{4,6},{5,7},{6,4},{7,5},{8,10},{9,11},{10,... | collective-permute-start | bytes 1572872 | tf_op jit(solution)/shard_map/ppermute | solution.py:320
  203.6 5.3 %collective-permute-start.41 = (bf16[1024,256]{1,0:T(8,128)(2,1)}, bf16[1024,256]{1,0:T(8,128)(2,1)S(1)}, u32[]{:S(2)}, u32[]{:S(2)}) collective-permute-start(bf16[1024,256]{1,0:T(8,128)(2,1)} %get-tuple-element.145.refs_6_), channel_id=1, source_target_pairs={{0,1},{1,0},{2,3},{3,2},{4,5},{5,4},{6,7},{7,6},{8,9},{9,8},{10,11... | collective-permute-start | bytes 1572872 | tf_op jit(solution)/shard_map/ppermute | solution.py:320
  203.6 5.3 %collective-permute-start.42 = (bf16[1024,256]{1,0:T(8,128)(2,1)}, bf16[1024,256]{1,0:T(8,128)(2,1)S(1)}, u32[]{:S(2)}, u32[]{:S(2)}) collective-permute-start(bf16[1024,256]{1,0:T(8,128)(2,1)} %get-tuple-element.147.refs_7_), channel_id=1, source_target_pairs={{0,1},{1,0},{2,3},{3,2},{4,5},{5,4},{6,7},{7,6},{8,9},{9,8},{10,11... | collective-permute-start | bytes 1572872 | tf_op jit(solution)/shard_map/ppermute | solution.py:320
  204.2 14.0 %collective-permute-start.43 = (bf16[1024,256]{1,0:T(8,128)(2,1)}, bf16[1024,256]{1,0:T(8,128)(2,1)S(1)}, u32[]{:S(2)}, u32[]{:S(2)}) collective-permute-start(bf16[1024,256]{1,0:T(8,128)(2,1)} %get-tuple-element.148.refs_0_), channel_id=1, source_target_pairs={{0,2},{1,3},{2,0},{3,1},{4,6},{5,7},{6,4},{7,5},{8,10},{9,11},{10,... | collective-permute-start | bytes 1572872 | tf_op jit(solution)/shard_map/ppermute | solution.py:320
  204.7 13.5 %collective-permute-start.45 = (bf16[1024,256]{1,0:T(8,128)(2,1)}, bf16[1024,256]{1,0:T(8,128)(2,1)S(1)}, u32[]{:S(2)}, u32[]{:S(2)}) collective-permute-start(bf16[1024,256]{1,0:T(8,128)(2,1)} %collective-permute-done.39), channel_id=1, source_target_pairs={{0,1},{1,0},{2,3},{3,2},{4,5},{5,4},{6,7},{7,6},{8,9},{9,8},{10,11... | collective-permute-start | bytes 1572872 | tf_op jit(solution)/shard_map/ppermute | solution.py:320
  204.7 14.7 %collective-permute-start.44 = (bf16[1024,256]{1,0:T(8,128)(2,1)}, bf16[1024,256]{1,0:T(8,128)(2,1)}, u32[]{:S(2)}, u32[]{:S(2)}) collective-permute-start(bf16[1024,256]{1,0:T(8,128)(2,1)} %collective-permute-done.39), channel_id=1, source_target_pairs={{0,4},{4,0},{8,12},{12,8},{16,20},{20,16},{24,28},{28,24},{1,5},{5... | collective-permute-start | bytes 1572872 | tf_op jit(solution)/shard_map/ppermute | solution.py:316
  209.0 17.6 %copy-start.12 = (bf16[1024,256]{1,0:T(8,128)(2,1)}, bf16[1024,256]{1,0:T(8,128)(2,1)S(1)}, u32[]{:S(2)}) copy-start(bf16[1024,256]{1,0:T(8,128)(2,1)S(1)} %collective-permute-done.41.refs_2_.refs_10_) | copy-start | bytes 1572868
  209.0 17.6 %copy-start.13 = (bf16[1024,256]{1,0:T(8,128)(2,1)}, bf16[1024,256]{1,0:T(8,128)(2,1)S(1)}, u32[]{:S(2)}) copy-start(bf16[1024,256]{1,0:T(8,128)(2,1)S(1)} %collective-permute-done.42.refs_3_.refs_11_) | copy-start | bytes 1572868
  219.3 13.6 %collective-permute-start.46 = (bf16[1024,256]{1,0:T(8,128)(2,1)S(1)}, bf16[1024,256]{1,0:T(8,128)(2,1)S(1)}, u32[]{:S(2)}, u32[]{:S(2)}) collective-permute-start(bf16[1024,256]{1,0:T(8,128)(2,1)S(1)} %collective-permute-done.43.refs_4_.refs_12_), channel_id=1, source_target_pairs={{0,4},{4,0},{8,12},{12,8},{16,20},{20,16},{24,28},{28,24},{1,5},{5... | collective-permute-start | bytes 1572872 | tf_op jit(solution)/shard_map/ppermute | solution.py:316
  220.5 12.4 %collective-permute-start.47 = (bf16[1024,256]{1,0:T(8,128)(2,1)}, bf16[1024,256]{1,0:T(8,128)(2,1)S(1)}, u32[]{:S(2)}, u32[]{:S(2)}) collective-permute-start(bf16[1024,256]{1,0:T(8,128)(2,1)} %collective-permute-done.44), channel_id=1, source_target_pairs={{0,1},{1,0},{2,3},{3,2},{4,5},{5,4},{6,7},{7,6},{8,9},{9,8},{10,11... | collective-permute-start | bytes 1572872 | tf_op jit(solution)/shard_map/ppermute | solution.py:320
  220.5 12.4 %collective-permute-start.49 = (bf16[2,512,256]{2,1,0:T(8,128)(2,1)}, bf16[2,512,256]{2,1,0:T(8,128)(2,1)S(1)}, u32[]{:S(2)}, u32[]{:S(2)}) collective-permute-start(bf16[2,512,256]{2,1,0:T(8,128)(2,1)} %shard_map.153.refs_4_), channel_id=1, source_target_pairs={{0,1},{1,0},{2,3},{3,2},{4,5},{5,4},{6,7},{7,6},{8,9},{9,8},{10,11... | collective-permute-start | bytes 1572872 | tf_op jit(solution)/shard_map/ppermute | solution.py:320
  221.0 14.1 %collective-permute-start.48 = (bf16[2,512,256]{2,1,0:T(8,128)(2,1)}, bf16[2,512,256]{2,1,0:T(8,128)(2,1)}, u32[]{:S(2)}, u32[]{:S(2)}) collective-permute-start(bf16[2,512,256]{2,1,0:T(8,128)(2,1)} %shard_map.153.refs_4_), channel_id=1, source_target_pairs={{0,2},{1,3},{2,0},{3,1},{4,6},{5,7},{6,4},{7,5},{8,10},{9,11},{10,... | collective-permute-start | bytes 1572872 | tf_op jit(solution)/shard_map/ppermute | solution.py:320
  237.7 13.4 %collective-permute-start.52 = (bf16[2,512,256]{2,1,0:T(8,128)(2,1)}, bf16[2,512,256]{2,1,0:T(8,128)(2,1)}, u32[]{:S(2)}, u32[]{:S(2)}) collective-permute-start(bf16[2,512,256]{2,1,0:T(8,128)(2,1)} %shard_map.152.refs_10_), channel_id=1, source_target_pairs={{0,1},{1,0},{2,3},{3,2},{4,5},{5,4},{6,7},{7,6},{8,9},{9,8},{10,11... | collective-permute-start | bytes 1572872 | tf_op jit(solution)/shard_map/ppermute | solution.py:320
  237.8 13.3 %collective-permute-start.51 = (bf16[2,512,256]{2,1,0:T(8,128)(2,1)}, bf16[2,512,256]{2,1,0:T(8,128)(2,1)}, u32[]{:S(2)}, u32[]{:S(2)}) collective-permute-start(bf16[2,512,256]{2,1,0:T(8,128)(2,1)} %collective-permute-done.48.refs_8_), channel_id=1, source_target_pairs={{0,1},{1,0},{2,3},{3,2},{4,5},{5,4},{6,7},{7,6},{8,9},{9,8},{10,11... | collective-permute-start | bytes 1572872 | tf_op jit(solution)/shard_map/ppermute | solution.py:320
  238.3 19.2 %collective-permute-start.50 = (bf16[2,512,256]{2,1,0:T(8,128)(2,1)}, bf16[2,512,256]{2,1,0:T(8,128)(2,1)S(1)}, u32[]{:S(2)}, u32[]{:S(2)}) collective-permute-start(bf16[2,512,256]{2,1,0:T(8,128)(2,1)} %shard_map.152.refs_10_), channel_id=1, source_target_pairs={{0,2},{1,3},{2,0},{3,1},{4,6},{5,7},{6,4},{7,5},{8,10},{9,11},{10,... | collective-permute-start | bytes 1572872 | tf_op jit(solution)/shard_map/ppermute | solution.py:320
  257.5 4.2 %collective-permute-start.53 = (bf16[2,512,256]{2,1,0:T(8,128)(2,1)S(1)}, bf16[2,512,256]{2,1,0:T(8,128)(2,1)S(1)}, u32[]{:S(2)}, u32[]{:S(2)}) collective-permute-start(bf16[2,512,256]{2,1,0:T(8,128)(2,1)S(1)} %collective-permute-done.50.refs_4_), channel_id=1, source_target_pairs={{0,1},{1,0},{2,3},{3,2},{4,5},{5,4},{6,7},{7,6},{8,9},{9,8},{10,11... | collective-permute-start | bytes 1572872 | tf_op jit(solution)/shard_map/ppermute | solution.py:320
  (20 other events, 103.4 us)

commit v4 on v3

--- a/solution.py
+++ b/solution.py
@@ -9,20 +9,20 @@
 
 ema_decay = 0.95
 halves = 2
-wire_gain = 2.0**20
+wire_gain = 2.0**31
 all_vmem = 60 * 2**20
 
 
 def to_wire(value):
     scaled = value * wire_gain
-    square = scaled * scaled
-    return (scaled * jnp.abs(scaled) * square).astype(jnp.bfloat16)
+    return (scaled * scaled * scaled).astype(jnp.bfloat16)
 
 
 def from_wire(sent):
-    power = sent.astype(jnp.float32)
-    root = lax.rsqrt(lax.rsqrt(jnp.abs(power))) * (1.0 / wire_gain)
-    return jnp.where(power < 0, -root, root)
+    cube = sent.astype(jnp.float32)
+    size = jnp.maximum(jnp.abs(cube), 2.0**-126)
+    root = jnp.exp2(jnp.log2(size) * (1.0 / 3.0)) * (1.0 / wire_gain)
+    return jnp.where(cube < 0, -root, root)
 
 
 def pinned(arrays):
@@ -488,6 +488,7 @@
             first = choose(1, wanted, first)
             whole_slab = [alone(slab[g][j]) for j in everyone for g in range(halves)]
             turned_slab = turn_blocks(after(whole_slab, first))
+            ended = ended + (turned_slab[0],)
         swaps = [swap_job(j)]
 
     def own_rows(h):
@@ -514,19 +515,18 @@
         slot()
     right_new = [right_part(0)]
     job = own_rows(0)
+    ended = ended + (right_new[0],)
     slot(job, *swaps)
-    ended = ended + (right_new[0],)
-    while not complete(1):
+    lows, highs = list(everyone)[:top_bit], list(everyone)[top_bit:]
+    while not complete(1) or not all(j in mine[0] for j in lows):
         slot()
+    total = left_part([(0, lows)], left_old, True)
     job = own_rows(1)
+    ended = ended + (total,)
     slot(job)
     right_new.append(right_part(1))
     ended = ended + (right_new[1],)
-    while not all(j in mine[0] for j in everyone):
-        slot()
-    lows, highs = list(everyone)[:top_bit], list(everyone)[top_bit:]
-    total = left_part([(0, lows)], left_old, True)
-    while not all(j in mine[1] for j in lows):
+    while not all(j in mine[0] for j in everyone) or not all(j in mine[1] for j in lows):
         slot()
     total = left_part([(0, highs), (1, lows)], total)
     ended = ended + (total,)

time: 268 us -> 263 us (0.981)
  waiting for transfers between devices: 122 us -> 118 us
  starting transfers between devices: 47.3 us -> 44.5 us
    ppermute x24, waiting for transfers between devices: 23.8 us -> 11.7 us  [exchange(): return lambda block: lax.ppermute(block, 'node', pairs)]
    ppermute x2, waiting for transfers between devices: 1.3 us -> 8.98 us  [swap(): return lax.ppermute(block, 'dp', [(d, d ^ 1) for d in range(ring)])]
    unnamed x60 -> x64, local copies, waits for them, and re-layouts: 6.9 us -> 8.08 us
  transfers between devices with their start and end apart: 54 -> 54, of which waited for: 31 -> 32; matrix products, arithmetic and copies ran while one was open for 3% -> 3% of each run, Pallas kernels for 27% -> 27%
where the time goes in v4:
time: 263 us; the launch traced here: 262 us
  waiting for transfers between devices  118 us (45%)
  Pallas kernels  82.3 us (31%)
  starting transfers between devices  44.5 us (17%)
  local copies, waits for them, and re-layouts  8.25 us (3%)
  other arithmetic  7.75 us (3%)
    ppermute x14, waiting for transfers between devices, rise(): lax.ppermute(block, 'dp', [(order[k], order[(k + 1) % ring]) for k in ran...  61 us
    ppermute x14, waiting for transfers between devices, fall(): lax.ppermute(block, 'dp', [(order[(k + 1) % ring], order[k]) for k in ran...  36.2 us
    pallas_call x8, Pallas kernels, sum_round(): pl.pallas_call(functools.partial(sum_body, counts, parts), out_shape=[jax...  30.5 us
    ppermute x14, starting transfers between devices, rise(): lax.ppermute(block, 'dp', [(order[k], order[(k + 1) % ring]) for k in ran...  26.9 us
    pallas_call x3, Pallas kernels, left_sum(): pl.pallas_call(functools.partial(left_body, len(theirs), pair, first), ou...  15.5 us
    pallas_call x4, Pallas kernels, pick_blocks(): pl.pallas_call(functools.partial(pick_body, len(cases), groups), out_shap...  13.9 us
    pallas_call x2, Pallas kernels, right_sum(): pl.pallas_call(functools.partial(right_body, count, pair), out_shape=jax....  12.2 us
    ppermute x24, starting transfers between devices, exchange(): return lambda block: lax.ppermute(block, 'node', pairs)  11.8 us
  transfers between devices with their start and end apart: 54, of which 32 were waited for; matrix products, arithmetic and copies ran while one was open for 3% of the time, Pallas kernels for 27%

profile of v4, /device:TPU:0, one launch (start us, length us, event | category | flops | bytes accessed | tf_op | source)
XLA Modules:
  0.0 261.8 jit_solution(7283214840098957581)
XLA Ops:
  0.7 1.6 copy-done
  2.3 3.4 %shard_map.140 = (bf16[1024,256]{1,0:T(8,128)(2,1)S(1)}, bf16[1024,256]{1,0:T(8,128)(2,1)S(1)}) custom-call(s32[8]{0:T(128)S(1)} %compare_select_fusion.10.slabs, bf16[1024,1024]{1,0:T(8,128)(2,1)S(1)} %copy-done, bf16[1024,4096]{1,0:T(8,128)(2,1)} %second.15, bf16[1024,4096]{1,0:T(8,128)(2,1)} %second.15), custom_call_target="tpu_custom_call" | custom-call | flops 1073741824 | tf_op jit(solution)/shard_map/pallas_call | solution.py:69
  5.7 3.1 %collective-permute-start = (bf16[1024,256]{1,0:T(8,128)(2,1)S(1)}, bf16[1024,256]{1,0:T(8,128)(2,1)S(1)}, u32[]{:S(2)}, u32[]{:S(2)}) collective-permute-start(bf16[1024,256]{1,0:T(8,128)(2,1)S(1)} %get-tuple-element.88), channel_id=1, source_target_pairs={{0,8},{8,16},{16,24},{24,28},{28,20},{20,12},{12,4},{4,0},{1,9},{9... | collective-permute-start | bytes 1572872 | tf_op jit(solution)/shard_map/ppermute | solution.py:306
  8.8 3.4 %shard_map.141 = (bf16[1024,256]{1,0:T(8,128)(2,1)S(1)}, bf16[1024,256]{1,0:T(8,128)(2,1)S(1)}) custom-call(s32[8]{0:T(128)S(1)} %compare_select_fusion.10.slabs, bf16[1024,1024]{1,0:T(8,128)(2,1)S(1)} %copy-done, bf16[1024,4096]{1,0:T(8,128)(2,1)} %second.15, bf16[1024,4096]{1,0:T(8,128)(2,1)} %second.15), custom_call_target="tpu_custom_call" | custom-call | flops 1073741824 | tf_op jit(solution)/shard_map/pallas_call | solution.py:69
  12.2 2.1 collective-permute-start.2
  14.3 7.2 %collective-permute-done.rest_0_ = bf16[1024,256]{1,0:T(8,128)(2,1)S(1)} collective-permute-done((bf16[1024,256]{1,0:T(8,128)(2,1)S(1)}, bf16[1024,256]{1,0:T(8,128)(2,1)S(1)}, u32[]{:S(2)}, u32[]{:S(2)}) %collective-permute-start) | collective-permute-done | bytes 524320 | tf_op jit(solution)/shard_map/ppermute | solution.py:306
  21.5 2.1 collective-permute-done.1.rest_1_
  23.6 4.0 %shard_map.142 = (bf16[1024,256]{1,0:T(8,128)(2,1)S(1)}, bf16[1024,256]{1,0:T(8,128)(2,1)S(1)}) custom-call(s32[8]{0:T(128)S(1)} %compare_select_fusion.10.slabs, bf16[1024,1024]{1,0:T(8,128)(2,1)S(1)} %copy-done, bf16[1024,4096]{1,0:T(8,128)(2,1)} %second.15, bf16[1024,4096]{1,0:T(8,128)(2,1)} %second.15, ...), custom_call_target="tpu_custom_call" | custom-call | flops 1073741824 | tf_op jit(solution)/shard_map/pallas_call | solution.py:69
  27.7 1.6 collective-permute-start.4
  29.8 3.0 %collective-permute-done.2.rest_0_ = bf16[1024,256]{1,0:T(8,128)(2,1)S(1)} collective-permute-done((bf16[1024,256]{1,0:T(8,128)(2,1)S(1)}, bf16[1024,256]{1,0:T(8,128)(2,1)S(1)}, u32[]{:S(2)}, u32[]{:S(2)}) %collective-permute-start.2) | collective-permute-done | bytes 524320 | tf_op jit(solution)/shard_map/ppermute | solution.py:306
  32.7 2.1 collective-permute-done.3.rest_1_
  34.9 4.0 %shard_map.143 = (bf16[1024,256]{1,0:T(8,128)(2,1)S(1)}, bf16[1024,256]{1,0:T(8,128)(2,1)S(1)}) custom-call(s32[8]{0:T(128)S(1)} %compare_select_fusion.10.slabs, bf16[1024,1024]{1,0:T(8,128)(2,1)S(1)} %copy-done, bf16[1024,4096]{1,0:T(8,128)(2,1)} %second.15, bf16[1024,4096]{1,0:T(8,128)(2,1)} %second.15, ...), custom_call_target="tpu_custom_call" | custom-call | flops 1073741824 | tf_op jit(solution)/shard_map/pallas_call | solution.py:69
  38.9 1.6 collective-permute-start.6
  41.0 3.0 %collective-permute-done.4.rest_0_ = bf16[1024,256]{1,0:T(8,128)(2,1)S(1)} collective-permute-done((bf16[1024,256]{1,0:T(8,128)(2,1)S(1)}, bf16[1024,256]{1,0:T(8,128)(2,1)S(1)}, u32[]{:S(2)}, u32[]{:S(2)}) %collective-permute-start.4) | collective-permute-done | bytes 524320 | tf_op jit(solution)/shard_map/ppermute | solution.py:306
  43.9 2.1 collective-permute-done.5.rest_1_
  46.1 4.0 %shard_map.144 = (bf16[1024,256]{1,0:T(8,128)(2,1)S(1)}, bf16[1024,256]{1,0:T(8,128)(2,1)S(1)}) custom-call(s32[8]{0:T(128)S(1)} %compare_select_fusion.10.slabs, bf16[1024,1024]{1,0:T(8,128)(2,1)S(1)} %copy-done, bf16[1024,4096]{1,0:T(8,128)(2,1)} %second.15, bf16[1024,4096]{1,0:T(8,128)(2,1)} %second.15, ...), custom_call_target="tpu_custom_call" | custom-call | flops 1073741824 | tf_op jit(solution)/shard_map/pallas_call | solution.py:69
  50.1 1.6 collective-permute-start.8
  52.2 3.0 %collective-permute-done.6.rest_0_ = bf16[1024,256]{1,0:T(8,128)(2,1)S(1)} collective-permute-done((bf16[1024,256]{1,0:T(8,128)(2,1)S(1)}, bf16[1024,256]{1,0:T(8,128)(2,1)S(1)}, u32[]{:S(2)}, u32[]{:S(2)}) %collective-permute-start.6) | collective-permute-done | bytes 524320 | tf_op jit(solution)/shard_map/ppermute | solution.py:306
  55.2 2.1 collective-permute-done.7.rest_1_
  57.3 4.0 %shard_map.145 = (bf16[1024,256]{1,0:T(8,128)(2,1)S(1)}, bf16[1024,256]{1,0:T(8,128)(2,1)S(1)}) custom-call(s32[8]{0:T(128)S(1)} %compare_select_fusion.10.slabs, bf16[1024,1024]{1,0:T(8,128)(2,1)S(1)} %copy-done, bf16[1024,4096]{1,0:T(8,128)(2,1)} %second.15, bf16[1024,4096]{1,0:T(8,128)(2,1)} %second.15, ...), custom_call_target="tpu_custom_call" | custom-call | flops 1073741824 | tf_op jit(solution)/shard_map/pallas_call | solution.py:69
  61.4 4.1 %collective-permute-done.8.rest_0_ = bf16[1024,256]{1,0:T(8,128)(2,1)S(1)} collective-permute-done((bf16[1024,256]{1,0:T(8,128)(2,1)S(1)}, bf16[1024,256]{1,0:T(8,128)(2,1)S(1)}, u32[]{:S(2)}, u32[]{:S(2)}) %collective-permute-start.8) | collective-permute-done | bytes 524320 | tf_op jit(solution)/shard_map/ppermute | solution.py:306
  65.6 3.0 %collective-permute-done.9.rest_1_ = bf16[1024,256]{1,0:T(8,128)(2,1)S(1)} collective-permute-done((bf16[1024,256]{1,0:T(8,128)(2,1)S(1)}, bf16[1024,256]{1,0:T(8,128)(2,1)S(1)}, u32[]{:S(2)}, u32[]{:S(2)}) %collective-permute-start.9) | collective-permute-done | bytes 524320 | tf_op jit(solution)/shard_map/ppermute | solution.py:311
  68.6 4.0 %shard_map.146 = (bf16[1024,256]{1,0:T(8,128)(2,1)S(1)}, bf16[1024,256]{1,0:T(8,128)(2,1)S(1)}) custom-call(s32[8]{0:T(128)S(1)} %compare_select_fusion.10.slabs, bf16[1024,1024]{1,0:T(8,128)(2,1)S(1)} %copy-done, bf16[1024,4096]{1,0:T(8,128)(2,1)} %second.15, bf16[1024,4096]{1,0:T(8,128)(2,1)} %second.15, ...), custom_call_target="tpu_custom_call" | custom-call | flops 1073741824 | tf_op jit(solution)/shard_map/pallas_call | solution.py:69
  72.6 1.6 collective-permute-start.10
  74.2 3.4 %shard_map.147 = (f32[1024,256]{1,0:T(8,128)S(1)}, f32[1024,256]{1,0:T(8,128)S(1)}) custom-call(s32[8]{0:T(128)S(1)} %compare_select_fusion.10.slabs, bf16[1024,1024]{1,0:T(8,128)(2,1)S(1)} %copy-done, bf16[1024,4096]{1,0:T(8,128)(2,1)} %second.15, bf16[1024,4096]{1,0:T(8,128)(2,1)} %second.15), custom_call_target="tpu_custom_call" | custom-call | flops 1073741824 | tf_op jit(solution)/shard_map/pallas_call | solution.py:69
  78.3 5.4 %collective-permute-done.10 = bf16[1024,256]{1,0:T(8,128)(2,1)S(1)} collective-permute-done((bf16[1024,256]{1,0:T(8,128)(2,1)S(1)}, bf16[1024,256]{1,0:T(8,128)(2,1)S(1)}, u32[]{:S(2)}, u32[]{:S(2)}) %collective-permute-start.10) | collective-permute-done | bytes 524320 | tf_op jit(solution)/shard_map/ppermute | solution.py:306
  84.7 1.6 collective-permute-start.15
  86.8 1.6 collective-permute-start.13
  88.8 10.8 %collective-permute-done.15.refs_7_ = bf16[1024,256]{1,0:T(8,128)(2,1)S(1)} collective-permute-done((bf16[1024,256]{1,0:T(8,128)(2,1)S(1)}, bf16[1024,256]{1,0:T(8,128)(2,1)S(1)}, u32[]{:S(2)}, u32[]{:S(2)}) %collective-permute-start.15) | collective-permute-done | bytes 524320 | tf_op jit(solution)/shard_map/ppermute | solution.py:306
  99.6 1.5 collective-permute-start.24
  101.1 1.6 collective-permute-start.17
  103.2 7.7 %collective-permute-done.13 = bf16[1024,256]{1,0:T(8,128)(2,1)S(1)} collective-permute-done((bf16[1024,256]{1,0:T(8,128)(2,1)S(1)}, bf16[1024,256]{1,0:T(8,128)(2,1)S(1)}, u32[]{:S(2)}, u32[]{:S(2)}) %collective-permute-start.13) | collective-permute-done | bytes 524320 | tf_op jit(solution)/shard_map/ppermute | solution.py:306
  113.1 1.6 collective-permute-start.25
  114.7 3.4 %collective-permute-done.17.refs_6_ = bf16[1024,256]{1,0:T(8,128)(2,1)} collective-permute-done((bf16[1024,256]{1,0:T(8,128)(2,1)S(1)}, bf16[1024,256]{1,0:T(8,128)(2,1)}, u32[]{:S(2)}, u32[]{:S(2)}) %collective-permute-start.17) | collective-permute-done | bytes 524320 | tf_op jit(solution)/shard_map/ppermute | solution.py:306
  119.1 1.6 collective-permute-start.19
  123.5 5.1 %collective-permute-done.19.refs_5_ = bf16[1024,256]{1,0:T(8,128)(2,1)S(1)} collective-permute-done((bf16[1024,256]{1,0:T(8,128)(2,1)}, bf16[1024,256]{1,0:T(8,128)(2,1)S(1)}, u32[]{:S(2)}, u32[]{:S(2)}) %collective-permute-start.19) | collective-permute-done | bytes 524320 | tf_op jit(solution)/shard_map/ppermute | solution.py:306
  129.7 5.0 %collective-permute-done.23.refs_3_ = bf16[1024,256]{1,0:T(8,128)(2,1)S(1)} collective-permute-done((bf16[1024,256]{1,0:T(8,128)(2,1)}, bf16[1024,256]{1,0:T(8,128)(2,1)S(1)}, u32[]{:S(2)}, u32[]{:S(2)}) %collective-permute-start.23) | collective-permute-done | bytes 524320 | tf_op jit(solution)/shard_map/ppermute | solution.py:311
  135.6 2.9 %shard_map.148.refs_0_.refs_2_ = bf16[2,1024,256]{2,1,0:T(8,128)(2,1)} custom-call(s32[2]{0:T(128)} %get-tuple-element.174.spots, bf16[1024,256]{1,0:T(8,128)(2,1)} %copy-done.1, bf16[1024,256]{1,0:T(8,128)(2,1)} %copy-done.21, bf16[1024,256]{1,0:T(8,128)(2,1)} %collective-permute-done.18.refs_2_, bf16[1024,256]{1,0:T(8,128)(2,1)} %copy-done.23, ...), custom_call_target="tpu_custom_call" | custom-call | tf_op jit(solution)/shard_map/pallas_call | solution.py:125
  138.5 1.6 collective-permute-start.29
  140.0 2.5 collective-permute-start.30
  143.2 2.6 collective-permute-start.22
  146.4 5.9 %collective-permute-done.30.refs_4_ = bf16[1024,256]{1,0:T(8,128)(2,1)S(1)} collective-permute-done((bf16[1024,256]{1,0:T(8,128)(2,1)}, bf16[1024,256]{1,0:T(8,128)(2,1)S(1)}, u32[]{:S(2)}, u32[]{:S(2)}) %collective-permute-start.30) | collective-permute-done | bytes 524320 | tf_op jit(solution)/shard_map/ppermute | solution.py:306
  153.2 4.2 %shard_map.149 = (bf16[2,1024,256]{2,1,0:T(8,128)(2,1)}, bf16[1024,256]{1,0:T(8,128)(2,1)}, bf16[1024,256]{1,0:T(8,128)(2,1)}, bf16[1024,256]{1,0:T(8,128)(2,1)}, bf16[1024,256]{1,0:T(8,128)(2,1)}) custom-call(s32[6]{0:T(128)} %pad_add_fusion.1.spots, bf16[1024,256]{1,0:T(8,128)(2,1)} %copy-done.1, bf16[1024,256]{1,0:T(8,128)(2,1)} %copy-done.21, ...), custom_call_target="tpu_custom_call" | custom-call | tf_op jit(solution)/shard_map/pallas_call | solution.py:125
  158.1 2.4 collective-permute-done.22.refs_7_
  160.5 2.6 collective-permute-start.32
  163.6 6.9 %collective-permute-done.31.refs_3_ = bf16[1024,256]{1,0:T(8,128)(2,1)S(1)} collective-permute-done((bf16[1024,256]{1,0:T(8,128)(2,1)}, bf16[1024,256]{1,0:T(8,128)(2,1)S(1)}, u32[]{:S(2)}, u32[]{:S(2)}) %collective-permute-start.31) | collective-permute-done | bytes 524320 | tf_op jit(solution)/shard_map/ppermute | solution.py:311
  172.8 3.3 %collective-permute-done.35.refs_13_.refs_5_ = bf16[2,1024,256]{2,1,0:T(8,128)(2,1)S(1)} collective-permute-done((bf16[2,1024,256]{2,1,0:T(8,128)(2,1)}, bf16[2,1024,256]{2,1,0:T(8,128)(2,1)S(1)}, u32[]{:S(2)}, u32[]{:S(2)}) %collective-permute-start.35) | collective-permute-done | bytes 1048608 | tf_op jit(solution)/shard_map/ppermute | solution.py:320
  176.1 9.2 %collective-permute-done.33.refs_4_ = bf16[1024,256]{1,0:T(8,128)(2,1)S(1)} collective-permute-done((bf16[1024,256]{1,0:T(8,128)(2,1)S(1)}, bf16[1024,256]{1,0:T(8,128)(2,1)S(1)}, u32[]{:S(2)}, u32[]{:S(2)}) %collective-permute-start.33) | collective-permute-done | bytes 524320 | tf_op jit(solution)/shard_map/ppermute | solution.py:311
  186.2 2.2 shard_map.150.refs_2_
  190.4 4.6 %shard_map.151 = (bf16[1024,256]{1,0:T(8,128)(2,1)}, bf16[1024,256]{1,0:T(8,128)(2,1)}, bf16[1024,256]{1,0:T(8,128)(2,1)}, bf16[1024,256]{1,0:T(8,128)(2,1)}, bf...) custom-call(s32[7]{0:T(128)} %pad_add_fusion.spots, bf16[1024,256]{1,0:T(8,128)(2,1)} %copy-done.2, ...), custom_call_target="tpu_custom_call" | custom-call | tf_op jit(solution)/shard_map/pallas_call | solution.py:125
  195.1 5.1 %shard_map.152 = (bf16[256,1024]{1,0:T(8,128)(2,1)}, bf16[256,1024]{1,0:T(8,128)(2,1)}, bf16[256,1024]{1,0:T(8,128)(2,1)}, bf16[256,1024]{1,0:T(8,128)(2,1)}, bf...) custom-call(bf16[1024,256]{1,0:T(8,128)(2,1)} %copy-done.1, ...), custom_call_target="tpu_custom_call" | custom-call | tf_op jit(solution)/shard_map/pallas_call | solution.py:226
  200.2 2.6 %collective-permute-done.39 = bf16[1024,256]{1,0:T(8,128)(2,1)} collective-permute-done((bf16[1024,256]{1,0:T(8,128)(2,1)}, bf16[1024,256]{1,0:T(8,128)(2,1)}, u32[]{:S(2)}, u32[]{:S(2)}) %collective-permute-start.39) | collective-permute-done | bytes 524320 | tf_op jit(solution)/shard_map/ppermute | solution.py:320
  205.2 2.5 shard_map.155.refs_4_
  207.8 6.1 %shard_map.153 = f32[2,256,512]{2,1,0:T(8,128)} custom-call(bf16[256,1024]{1,0:T(8,128)(2,1)} %get-tuple-element.153.refs_0_, bf16[256,1024]{1,0:T(8,128)(2,1)} %get-tuple-element.159.refs_1_, bf16[256,1024]{1,0:T(8,128)(2,1)} %get-tuple-element.160.refs_2_, bf16[256,1024]{1,0:T(8,128)(2,1)} %get-tuple-element.161.refs_3_, ...), custom_call_target="tpu_custom_call" | custom-call | flops 2147483648 | tf_op jit(solution)/shard_map/pallas_call | solution.py:267
  213.9 3.4 %collective-permute-done.43.refs_4_.refs_12_ = bf16[1024,256]{1,0:T(8,128)(2,1)S(1)} collective-permute-done((bf16[1024,256]{1,0:T(8,128)(2,1)S(1)}, bf16[1024,256]{1,0:T(8,128)(2,1)S(1)}, u32[]{:S(2)}, u32[]{:S(2)}) %collective-permute-start.43) | collective-permute-done | bytes 524320 | tf_op jit(solution)/shard_map/ppermute | solution.py:320
  217.3 2.0 collective-permute-done.44
  222.0 4.6 %shard_map.156.refs_12_ = f32[1024,512]{1,0:T(8,128)} custom-call(bf16[1024,256]{1,0:T(8,128)(2,1)} %get-tuple-element.166.refs_8_.refs_0_, bf16[1024,256]{1,0:T(8,128)(2,1)} %get-tuple-element.167.refs_9_.refs_1_, bf16[1024,256]{1,0:T(8,128)(2,1)} %get-tuple-element.140.refs_2_, bf16[1024,256]{1,0:T(8,128)(2,1)} %get-tuple-element.142.refs_3_, ...), custom_call_target="tpu_custom_call" | custom-call | flops 1073741824 | tf_op jit(solution)/shard_map/pallas_call | solution.py:201
  226.6 7.0 %collective-permute-done.46.refs_5_.refs_13_ = bf16[1024,256]{1,0:T(8,128)(2,1)S(1)} collective-permute-done((bf16[1024,256]{1,0:T(8,128)(2,1)S(1)}, bf16[1024,256]{1,0:T(8,128)(2,1)S(1)}, u32[]{:S(2)}, u32[]{:S(2)}) %collective-permute-start.46) | collective-permute-done | bytes 524320 | tf_op jit(solution)/shard_map/ppermute | solution.py:316
  234.4 2.5 shard_map.154.refs_10_
  238.3 6.1 %shard_map.157 = f32[2,256,512]{2,1,0:T(8,128)} custom-call(bf16[256,1024]{1,0:T(8,128)(2,1)} %get-tuple-element.153.refs_0_, bf16[256,1024]{1,0:T(8,128)(2,1)} %get-tuple-element.159.refs_1_, bf16[256,1024]{1,0:T(8,128)(2,1)} %get-tuple-element.160.refs_2_, bf16[256,1024]{1,0:T(8,128)(2,1)} %get-tuple-element.161.refs_3_, ...), custom_call_target="tpu_custom_call" | custom-call | flops 2147483648 | tf_op jit(solution)/shard_map/pallas_call | solution.py:267
  245.9 6.4 %shard_map.158.refs_6_ = f32[1024,512]{1,0:T(8,128)} custom-call(bf16[2,1024,256]{2,1,0:T(8,128)(2,1)} %shard_map.148.refs_0_.refs_2_, bf16[2,1024,256]{2,1,0:T(8,128)(2,1)} %get-tuple-element.127.refs_1_.refs_3_, bf16[2,1024,256]{2,1,0:T(8,128)(2,1)} %shard_map.148.refs_0_.refs_2_, bf16[2,1024,256]{2,1,0:T(8,128)(2,1)} %get-tuple-element.127.refs_1_.refs_3_, ...), custom_call_target="tpu_custom_call" | custom-call | flops 2147483648 | tf_op jit(solution)/shard_map/pallas_call | solution.py:201
  253.3 1.4 copy-done.7
  254.7 1.8 bitcast_add_fusion
  257.3 4.5 %shard_map.159 = f32[1024,512]{1,0:T(8,128)} custom-call(bf16[1024,256]{1,0:T(8,128)(2,1)} %get-tuple-element.157.refs_0_, bf16[2,1024,256]{2,1,0:T(8,128)(2,1)} %get-tuple-element.134.refs_1_.refs_3_, bf16[1024,256]{1,0:T(8,128)(2,1)} %shard_map.150.refs_2_, bf16[2,1024,256]{2,1,0:T(8,128)(2,1)} %get-tuple-element.134.refs_1_.refs_3_, ...), custom_call_target="tpu_custom_call" | custom-call | flops 1073741824 | tf_op jit(solution)/shard_map/pallas_call | solution.py:201
  (140 shorter events, 31.2 us)
Async XLA Ops:
  5.7 15.8 %collective-permute-start = (bf16[1024,256]{1,0:T(8,128)(2,1)S(1)}, bf16[1024,256]{1,0:T(8,128)(2,1)S(1)}, u32[]{:S(2)}, u32[]{:S(2)}) collective-permute-start(bf16[1024,256]{1,0:T(8,128)(2,1)S(1)} %get-tuple-element.88), channel_id=1, source_target_pairs={{0,8},{8,16},{16,24},{24,28},{28,20},{20,12},{12,4},{4,0},{1,9},{9... | collective-permute-start | bytes 1572872 | tf_op jit(solution)/shard_map/ppermute | solution.py:306
  8.8 14.8 %collective-permute-start.1 = (bf16[1024,256]{1,0:T(8,128)(2,1)S(1)}, bf16[1024,256]{1,0:T(8,128)(2,1)S(1)}, u32[]{:S(2)}, u32[]{:S(2)}) collective-permute-start(bf16[1024,256]{1,0:T(8,128)(2,1)S(1)} %get-tuple-element.89), channel_id=1, source_target_pairs={{8,0},{16,8},{24,16},{28,24},{20,28},{12,20},{4,12},{0,4},{9,1},{1... | collective-permute-start | bytes 1572872 | tf_op jit(solution)/shard_map/ppermute | solution.py:311
  12.2 20.5 %collective-permute-start.2 = (bf16[1024,256]{1,0:T(8,128)(2,1)S(1)}, bf16[1024,256]{1,0:T(8,128)(2,1)S(1)}, u32[]{:S(2)}, u32[]{:S(2)}) collective-permute-start(bf16[1024,256]{1,0:T(8,128)(2,1)S(1)} %get-tuple-element.91), channel_id=1, source_target_pairs={{0,8},{8,16},{16,24},{24,28},{28,20},{20,12},{12,4},{4,0},{1,9},{9... | collective-permute-start | bytes 1572872 | tf_op jit(solution)/shard_map/ppermute | solution.py:306
  14.3 20.6 %collective-permute-start.3 = (bf16[1024,256]{1,0:T(8,128)(2,1)S(1)}, bf16[1024,256]{1,0:T(8,128)(2,1)S(1)}, u32[]{:S(2)}, u32[]{:S(2)}) collective-permute-start(bf16[1024,256]{1,0:T(8,128)(2,1)S(1)} %get-tuple-element.92), channel_id=1, source_target_pairs={{8,0},{16,8},{24,16},{28,24},{20,28},{12,20},{4,12},{0,4},{9,1},{1... | collective-permute-start | bytes 1572872 | tf_op jit(solution)/shard_map/ppermute | solution.py:311
  27.7 16.3 %collective-permute-start.4 = (bf16[1024,256]{1,0:T(8,128)(2,1)S(1)}, bf16[1024,256]{1,0:T(8,128)(2,1)S(1)}, u32[]{:S(2)}, u32[]{:S(2)}) collective-permute-start(bf16[1024,256]{1,0:T(8,128)(2,1)S(1)} %get-tuple-element.94), channel_id=1, source_target_pairs={{0,8},{8,16},{16,24},{24,28},{28,20},{20,12},{12,4},{4,0},{1,9},{9... | collective-permute-start | bytes 1572872 | tf_op jit(solution)/shard_map/ppermute | solution.py:306
  29.3 16.8 %collective-permute-start.5 = (bf16[1024,256]{1,0:T(8,128)(2,1)S(1)}, bf16[1024,256]{1,0:T(8,128)(2,1)S(1)}, u32[]{:S(2)}, u32[]{:S(2)}) collective-permute-start(bf16[1024,256]{1,0:T(8,128)(2,1)S(1)} %get-tuple-element.95), channel_id=1, source_target_pairs={{8,0},{16,8},{24,16},{28,24},{20,28},{12,20},{4,12},{0,4},{9,1},{1... | collective-permute-start | bytes 1572872 | tf_op jit(solution)/shard_map/ppermute | solution.py:311
  38.9 16.3 %collective-permute-start.6 = (bf16[1024,256]{1,0:T(8,128)(2,1)S(1)}, bf16[1024,256]{1,0:T(8,128)(2,1)S(1)}, u32[]{:S(2)}, u32[]{:S(2)}) collective-permute-start(bf16[1024,256]{1,0:T(8,128)(2,1)S(1)} %get-tuple-element.97), channel_id=1, source_target_pairs={{0,8},{8,16},{16,24},{24,28},{28,20},{20,12},{12,4},{4,0},{1,9},{9... | collective-permute-start | bytes 1572872 | tf_op jit(solution)/shard_map/ppermute | solution.py:306
  40.5 16.8 %collective-permute-start.7 = (bf16[1024,256]{1,0:T(8,128)(2,1)S(1)}, bf16[1024,256]{1,0:T(8,128)(2,1)S(1)}, u32[]{:S(2)}, u32[]{:S(2)}) collective-permute-start(bf16[1024,256]{1,0:T(8,128)(2,1)S(1)} %get-tuple-element.98), channel_id=1, source_target_pairs={{8,0},{16,8},{24,16},{28,24},{20,28},{12,20},{4,12},{0,4},{9,1},{1... | collective-permute-start | bytes 1572872 | tf_op jit(solution)/shard_map/ppermute | solution.py:311
  50.1 15.4 %collective-permute-start.8 = (bf16[1024,256]{1,0:T(8,128)(2,1)S(1)}, bf16[1024,256]{1,0:T(8,128)(2,1)S(1)}, u32[]{:S(2)}, u32[]{:S(2)}) collective-permute-start(bf16[1024,256]{1,0:T(8,128)(2,1)S(1)} %get-tuple-element.100), channel_id=1, source_target_pairs={{0,8},{8,16},{16,24},{24,28},{28,20},{20,12},{12,4},{4,0},{1,9},{9... | collective-permute-start | bytes 1572872 | tf_op jit(solution)/shard_map/ppermute | solution.py:306
  51.8 16.8 %collective-permute-start.9 = (bf16[1024,256]{1,0:T(8,128)(2,1)S(1)}, bf16[1024,256]{1,0:T(8,128)(2,1)S(1)}, u32[]{:S(2)}, u32[]{:S(2)}) collective-permute-start(bf16[1024,256]{1,0:T(8,128)(2,1)S(1)} %get-tuple-element.101), channel_id=1, source_target_pairs={{8,0},{16,8},{24,16},{28,24},{20,28},{12,20},{4,12},{0,4},{9,1},{1... | collective-permute-start | bytes 1572872 | tf_op jit(solution)/shard_map/ppermute | solution.py:311
  61.4 17.0 %collective-permute-start.11 = (bf16[1024,256]{1,0:T(8,128)(2,1)S(1)}, bf16[1024,256]{1,0:T(8,128)(2,1)S(1)}, u32[]{:S(2)}, u32[]{:S(2)}) collective-permute-start(bf16[1024,256]{1,0:T(8,128)(2,1)S(1)} %get-tuple-element.104), channel_id=1, source_target_pairs={{8,0},{16,8},{24,16},{28,24},{20,28},{12,20},{4,12},{0,4},{9,1},{1... | collective-permute-start | bytes 1572872 | tf_op jit(solution)/shard_map/ppermute | solution.py:311
  72.6 11.1 %collective-permute-start.10 = (bf16[1024,256]{1,0:T(8,128)(2,1)S(1)}, bf16[1024,256]{1,0:T(8,128)(2,1)S(1)}, u32[]{:S(2)}, u32[]{:S(2)}) collective-permute-start(bf16[1024,256]{1,0:T(8,128)(2,1)S(1)} %get-tuple-element.106), channel_id=1, source_target_pairs={{0,8},{8,16},{16,24},{24,28},{28,20},{20,12},{12,4},{4,0},{1,9},{9... | collective-permute-start | bytes 1572872 | tf_op jit(solution)/shard_map/ppermute | solution.py:306
  77.7 45.3 %copy-start.31 = (s32[2]{0:T(128)S(1)}, s32[2]{0:T(128)}, u32[]{:S(2)}) copy-start(s32[2]{0:T(128)} %constant.149.clone) | copy-start | bytes 28
  84.7 50.0 %copy-start.1 = (bf16[1024,256]{1,0:T(8,128)(2,1)}, bf16[1024,256]{1,0:T(8,128)(2,1)S(1)}, u32[]{:S(2)}) copy-start(bf16[1024,256]{1,0:T(8,128)(2,1)S(1)} %fusion.23.refs_0_.refs_4_) | copy-start | bytes 1572868
  84.7 14.9 %collective-permute-start.15 = (bf16[1024,256]{1,0:T(8,128)(2,1)S(1)}, bf16[1024,256]{1,0:T(8,128)(2,1)S(1)}, u32[]{:S(2)}, u32[]{:S(2)}) collective-permute-start(bf16[1024,256]{1,0:T(8,128)(2,1)S(1)} %fusion.23.refs_0_.refs_4_), channel_id=1, source_target_pairs={{0,8},{8,16},{16,24},{24,28},{28,20},{20,12},{12,4},{4,0},{1,9},{9... | collective-permute-start | bytes 1572872 | tf_op jit(solution)/shard_map/ppermute | solution.py:306
  86.3 14.8 %collective-permute-start.16 = (bf16[1024,256]{1,0:T(8,128)(2,1)S(1)}, bf16[1024,256]{1,0:T(8,128)(2,1)S(1)}, u32[]{:S(2)}, u32[]{:S(2)}) collective-permute-start(bf16[1024,256]{1,0:T(8,128)(2,1)S(1)} %fusion.23.refs_0_.refs_4_), channel_id=1, source_target_pairs={{8,0},{16,8},{24,16},{28,24},{20,28},{12,20},{4,12},{0,4},{9,1},{1... | collective-permute-start | bytes 1572872 | tf_op jit(solution)/shard_map/ppermute | solution.py:311
  86.8 15.9 %collective-permute-start.12 = (bf16[1024,256]{1,0:T(8,128)(2,1)S(1)}, bf16[1024,256]{1,0:T(8,128)(2,1)S(1)}, u32[]{:S(2)}, u32[]{:S(2)}) collective-permute-start(bf16[1024,256]{1,0:T(8,128)(2,1)S(1)} %fusion.23.refs_0_.refs_4_), channel_id=1, source_target_pairs={{0,1},{1,0},{2,3},{3,2},{4,5},{5,4},{6,7},{7,6},{8,9},{9,8},{10,11... | collective-permute-start | bytes 1572872 | tf_op jit(solution)/shard_map/ppermute | solution.py:320
  86.8 24.1 %collective-permute-start.13 = (bf16[1024,256]{1,0:T(8,128)(2,1)S(1)}, bf16[1024,256]{1,0:T(8,128)(2,1)S(1)}, u32[]{:S(2)}, u32[]{:S(2)}) collective-permute-start(bf16[1024,256]{1,0:T(8,128)(2,1)S(1)} %get-tuple-element.103), channel_id=1, source_target_pairs={{0,8},{8,16},{16,24},{24,28},{28,20},{20,12},{12,4},{4,0},{1,9},{9... | collective-permute-start | bytes 1572872 | tf_op jit(solution)/shard_map/ppermute | solution.py:306
  88.4 23.8 %collective-permute-start.14 = (bf16[1024,256]{1,0:T(8,128)(2,1)S(1)}, bf16[1024,256]{1,0:T(8,128)(2,1)S(1)}, u32[]{:S(2)}, u32[]{:S(2)}) collective-permute-start(bf16[1024,256]{1,0:T(8,128)(2,1)S(1)} %get-tuple-element.107), channel_id=1, source_target_pairs={{8,0},{16,8},{24,16},{28,24},{20,28},{12,20},{4,12},{0,4},{9,1},{1... | collective-permute-start | bytes 1572872 | tf_op jit(solution)/shard_map/ppermute | solution.py:311
  99.6 35.1 %copy-start.20 = (bf16[1024,256]{1,0:T(8,128)(2,1)}, bf16[1024,256]{1,0:T(8,128)(2,1)S(1)}, u32[]{:S(2)}) copy-start(bf16[1024,256]{1,0:T(8,128)(2,1)S(1)} %collective-permute-done.15.refs_7_) | copy-start | bytes 1572868
  99.6 13.5 %collective-permute-start.24 = (bf16[1024,256]{1,0:T(8,128)(2,1)S(1)}, bf16[1024,256]{1,0:T(8,128)(2,1)}, u32[]{:S(2)}, u32[]{:S(2)}) collective-permute-start(bf16[1024,256]{1,0:T(8,128)(2,1)S(1)} %fusion.23.refs_0_.refs_4_), channel_id=1, source_target_pairs={{0,2},{1,3},{2,0},{3,1},{4,6},{5,7},{6,4},{7,5},{8,10},{9,11},{10,... | collective-permute-start | bytes 1572872 | tf_op jit(solution)/shard_map/ppermute | solution.py:320
  101.1 33.6 %copy-start.21 = (bf16[1024,256]{1,0:T(8,128)(2,1)}, bf16[1024,256]{1,0:T(8,128)(2,1)S(1)}, u32[]{:S(2)}) copy-start(bf16[1024,256]{1,0:T(8,128)(2,1)S(1)} %collective-permute-done.16.refs_1_) | copy-start | bytes 1572868
  101.1 17.0 %collective-permute-start.17 = (bf16[1024,256]{1,0:T(8,128)(2,1)S(1)}, bf16[1024,256]{1,0:T(8,128)(2,1)}, u32[]{:S(2)}, u32[]{:S(2)}) collective-permute-start(bf16[1024,256]{1,0:T(8,128)(2,1)S(1)} %collective-permute-done.15.refs_7_), channel_id=1, source_target_pairs={{0,8},{8,16},{16,24},{24,28},{28,20},{20,12},{12,4},{4,0},{1,9},{9... | collective-permute-start | bytes 1572872 | tf_op jit(solution)/shard_map/ppermute | solution.py:306
  102.7 19.7 %copy-start.30 = (bf16[1024,256]{1,0:T(8,128)(2,1)}, bf16[1024,256]{1,0:T(8,128)(2,1)S(1)}, u32[]{:S(2)}) copy-start(bf16[1024,256]{1,0:T(8,128)(2,1)S(1)} %collective-permute-done.12.refs_2_) | copy-start | bytes 1572868
  102.7 16.4 %collective-permute-start.18 = (bf16[1024,256]{1,0:T(8,128)(2,1)S(1)}, bf16[1024,256]{1,0:T(8,128)(2,1)}, u32[]{:S(2)}, u32[]{:S(2)}) collective-permute-start(bf16[1024,256]{1,0:T(8,128)(2,1)S(1)} %collective-permute-done.16.refs_1_), channel_id=1, source_target_pairs={{8,0},{16,8},{24,16},{28,24},{20,28},{12,20},{4,12},{0,4},{9,1},{1... | collective-permute-start | bytes 1572872 | tf_op jit(solution)/shard_map/ppermute | solution.py:311
  113.1 30.1 %copy-start.2 = (bf16[1024,256]{1,0:T(8,128)(2,1)}, bf16[1024,256]{1,0:T(8,128)(2,1)S(1)}, u32[]{:S(2)}) copy-start(bf16[1024,256]{1,0:T(8,128)(2,1)S(1)} %fusion.26.refs_0_.refs_1_) | copy-start | bytes 1572868
  113.1 9.4 %collective-permute-start.25 = (bf16[1024,256]{1,0:T(8,128)(2,1)S(1)}, bf16[1024,256]{1,0:T(8,128)(2,1)}, u32[]{:S(2)}, u32[]{:S(2)}) collective-permute-start(bf16[1024,256]{1,0:T(8,128)(2,1)S(1)} %fusion.26.refs_0_.refs_1_), channel_id=1, source_target_pairs={{0,2},{1,3},{2,0},{3,1},{4,6},{5,7},{6,4},{7,5},{8,10},{9,11},{10,... | collective-permute-start | bytes 1572872 | tf_op jit(solution)/shard_map/ppermute | solution.py:320
  119.1 9.6 %collective-permute-start.19 = (bf16[1024,256]{1,0:T(8,128)(2,1)}, bf16[1024,256]{1,0:T(8,128)(2,1)S(1)}, u32[]{:S(2)}, u32[]{:S(2)}) collective-permute-start(bf16[1024,256]{1,0:T(8,128)(2,1)} %collective-permute-done.17.refs_6_), channel_id=1, source_target_pairs={{0,8},{8,16},{16,24},{24,28},{28,20},{20,12},{12,4},{4,0},{1,9},{9... | collective-permute-start | bytes 1572872 | tf_op jit(solution)/shard_map/ppermute | solution.py:306
  120.7 14.0 %collective-permute-start.23 = (bf16[1024,256]{1,0:T(8,128)(2,1)}, bf16[1024,256]{1,0:T(8,128)(2,1)S(1)}, u32[]{:S(2)}, u32[]{:S(2)}) collective-permute-start(bf16[1024,256]{1,0:T(8,128)(2,1)} %collective-permute-done.18.refs_2_), channel_id=1, source_target_pairs={{8,0},{16,8},{24,16},{28,24},{20,28},{12,20},{4,12},{0,4},{9,1},{1... | collective-permute-start | bytes 1572872 | tf_op jit(solution)/shard_map/ppermute | solution.py:311
  121.1 17.3 %collective-permute-start.26 = (bf16[1024,256]{1,0:T(8,128)(2,1)}, bf16[1024,256]{1,0:T(8,128)(2,1)}, u32[]{:S(2)}, u32[]{:S(2)}) collective-permute-start(bf16[1024,256]{1,0:T(8,128)(2,1)} %collective-permute-done.24.refs_4_), channel_id=1, source_target_pairs={{0,1},{1,0},{2,3},{3,2},{4,5},{5,4},{6,7},{7,6},{8,9},{9,8},{10,11... | collective-permute-start | bytes 1572872 | tf_op jit(solution)/shard_map/ppermute | solution.py:320
  122.4 16.0 %collective-permute-start.28 = (bf16[1024,256]{1,0:T(8,128)(2,1)}, bf16[1024,256]{1,0:T(8,128)(2,1)}, u32[]{:S(2)}, u32[]{:S(2)}) collective-permute-start(bf16[1024,256]{1,0:T(8,128)(2,1)} %collective-permute-done.25.refs_5_), channel_id=1, source_target_pairs={{0,1},{1,0},{2,3},{3,2},{4,5},{5,4},{6,7},{7,6},{8,9},{9,8},{10,11... | collective-permute-start | bytes 1572872 | tf_op jit(solution)/shard_map/ppermute | solution.py:320
  122.4 16.0 %collective-permute-start.27 = (bf16[1024,256]{1,0:T(8,128)(2,1)S(1)}, bf16[1024,256]{1,0:T(8,128)(2,1)}, u32[]{:S(2)}, u32[]{:S(2)}) collective-permute-start(bf16[1024,256]{1,0:T(8,128)(2,1)S(1)} %fusion.26.refs_0_.refs_1_), channel_id=1, source_target_pairs={{0,1},{1,0},{2,3},{3,2},{4,5},{5,4},{6,7},{7,6},{8,9},{9,8},{10,11... | collective-permute-start | bytes 1572872 | tf_op jit(solution)/shard_map/ppermute | solution.py:320
  128.6 14.6 %collective-permute-start.20 = (bf16[1024,256]{1,0:T(8,128)(2,1)S(1)}, bf16[1024,256]{1,0:T(8,128)(2,1)S(1)}, u32[]{:S(2)}, u32[]{:S(2)}) collective-permute-start(bf16[1024,256]{1,0:T(8,128)(2,1)S(1)} %fusion.26.refs_0_.refs_1_), channel_id=1, source_target_pairs={{8,0},{16,8},{24,16},{28,24},{20,28},{12,20},{4,12},{0,4},{9,1},{1... | collective-permute-start | bytes 1572872 | tf_op jit(solution)/shard_map/ppermute | solution.py:311
  138.5 22.1 %collective-permute-start.29 = (bf16[2,1024,256]{2,1,0:T(8,128)(2,1)}, bf16[2,1024,256]{2,1,0:T(8,128)(2,1)S(1)}, u32[]{:S(2)}, u32[]{:S(2)}) collective-permute-start(bf16[2,1024,256]{2,1,0:T(8,128)(2,1)} %shard_map.148.refs_0_.refs_2_), channel_id=1, source_target_pairs={{0,2},{1,3},{2,0},{3,1},{4,6},{5,7},{6,4},{7,5},{8,10},{9,11},{10,... | collective-permute-start | bytes 3145736 | tf_op jit(solution)/shard_map/ppermute | solution.py:320
  140.0 12.4 %collective-permute-start.30 = (bf16[1024,256]{1,0:T(8,128)(2,1)}, bf16[1024,256]{1,0:T(8,128)(2,1)S(1)}, u32[]{:S(2)}, u32[]{:S(2)}) collective-permute-start(bf16[1024,256]{1,0:T(8,128)(2,1)} %copy-done.22), channel_id=1, source_target_pairs={{0,8},{8,16},{16,24},{24,28},{28,20},{20,12},{12,4},{4,0},{1,9},{9... | collective-permute-start | bytes 1572872 | tf_op jit(solution)/shard_map/ppermute | solution.py:306
  143.2 14.2 %copy-start.8 = (bf16[1024,256]{1,0:T(8,128)(2,1)}, bf16[1024,256]{1,0:T(8,128)(2,1)S(1)}, u32[]{:S(2)}) copy-start(bf16[1024,256]{1,0:T(8,128)(2,1)S(1)} %collective-permute-done.20.refs_1_) | copy-start | bytes 1572868
  143.2 14.9 %collective-permute-start.21 = (bf16[1024,256]{1,0:T(8,128)(2,1)S(1)}, bf16[1024,256]{1,0:T(8,128)(2,1)}, u32[]{:S(2)}, u32[]{:S(2)}) collective-permute-start(bf16[1024,256]{1,0:T(8,128)(2,1)S(1)} %collective-permute-done.20.refs_1_), channel_id=1, source_target_pairs={{8,0},{16,8},{24,16},{28,24},{20,28},{12,20},{4,12},{0,4},{9,1},{1... | collective-permute-start | bytes 1572872 | tf_op jit(solution)/shard_map/ppermute | solution.py:311
  143.2 17.3 %collective-permute-start.22 = (bf16[1024,256]{1,0:T(8,128)(2,1)S(1)}, bf16[1024,256]{1,0:T(8,128)(2,1)}, u32[]{:S(2)}, u32[]{:S(2)}) collective-permute-start(bf16[1024,256]{1,0:T(8,128)(2,1)S(1)} %fusion.26.refs_0_.refs_1_), channel_id=1, source_target_pairs={{0,8},{8,16},{16,24},{24,28},{28,20},{20,12},{12,4},{4,0},{1,9},{9... | collective-permute-start | bytes 1572872 | tf_op jit(solution)/shard_map/ppermute | solution.py:306
  157.4 18.7 %collective-permute-start.35 = (bf16[2,1024,256]{2,1,0:T(8,128)(2,1)}, bf16[2,1024,256]{2,1,0:T(8,128)(2,1)S(1)}, u32[]{:S(2)}, u32[]{:S(2)}) collective-permute-start(bf16[2,1024,256]{2,1,0:T(8,128)(2,1)} %get-tuple-element.127.refs_1_.refs_3_), channel_id=1, source_target_pairs={{0,2},{1,3},{2,0},{3,1},{4,6},{5,7},{6,4},{7,5},{8,10},{9,11},{10,... | collective-permute-start | bytes 3145736 | tf_op jit(solution)/shard_map/ppermute | solution.py:320
  160.5 28.0 %copy-start.3 = (bf16[2,1024,256]{2,1,0:T(8,128)(2,1)}, bf16[2,1024,256]{2,1,0:T(8,128)(2,1)S(1)}, u32[]{:S(2)}) copy-start(bf16[2,1024,256]{2,1,0:T(8,128)(2,1)S(1)} %collective-permute-done.29.refs_12_.refs_4_) | copy-start | bytes 3145732
  160.5 10.0 %collective-permute-start.31 = (bf16[1024,256]{1,0:T(8,128)(2,1)}, bf16[1024,256]{1,0:T(8,128)(2,1)S(1)}, u32[]{:S(2)}, u32[]{:S(2)}) collective-permute-start(bf16[1024,256]{1,0:T(8,128)(2,1)} %collective-permute-done.21.refs_2_), channel_id=1, source_target_pairs={{8,0},{16,8},{24,16},{28,24},{20,28},{12,20},{4,12},{0,4},{9,1},{1... | collective-permute-start | bytes 1572872 | tf_op jit(solution)/shard_map/ppermute | solution.py:311
  160.5 10.0 %collective-permute-start.32 = (bf16[1024,256]{1,0:T(8,128)(2,1)}, bf16[1024,256]{1,0:T(8,128)(2,1)S(1)}, u32[]{:S(2)}, u32[]{:S(2)}) collective-permute-start(bf16[1024,256]{1,0:T(8,128)(2,1)} %collective-permute-done.22.refs_7_), channel_id=1, source_target_pairs={{0,8},{8,16},{16,24},{24,28},{28,20},{20,12},{12,4},{4,0},{1,9},{9... | collective-permute-start | bytes 1572872 | tf_op jit(solution)/shard_map/ppermute | solution.py:306
  163.1 8.5 %collective-permute-start.37 = (bf16[1024,256]{1,0:T(8,128)(2,1)}, bf16[1024,256]{1,0:T(8,128)(2,1)}, u32[]{:S(2)}, u32[]{:S(2)}) collective-permute-start(bf16[1024,256]{1,0:T(8,128)(2,1)} %get-tuple-element.140.refs_2_), channel_id=1, source_target_pairs={{0,1},{1,0},{2,3},{3,2},{4,5},{5,4},{6,7},{7,6},{8,9},{9,8},{10,11... | collective-permute-start | bytes 1572872 | tf_op jit(solution)/shard_map/ppermute | solution.py:320
  163.1 22.1 %collective-permute-start.36 = (bf16[2,1024,256]{2,1,0:T(8,128)(2,1)S(1)}, bf16[2,1024,256]{2,1,0:T(8,128)(2,1)S(1)}, u32[]{:S(2)}, u32[]{:S(2)}) collective-permute-start(bf16[2,1024,256]{2,1,0:T(8,128)(2,1)S(1)} %collective-permute-done.29.refs_12_.refs_4_), channel_id=1, source_target_pairs={{0,1},{1,0},{2,3},{3,2},{4,5},{5,4},{6,7},{7,6},{8,9},{9,8},{10,11... | collective-permute-start | bytes 3145736 | tf_op jit(solution)/shard_map/ppermute | solution.py:320
  170.5 14.8 %copy-start.9 = (bf16[1024,256]{1,0:T(8,128)(2,1)}, bf16[1024,256]{1,0:T(8,128)(2,1)S(1)}, u32[]{:S(2)}) copy-start(bf16[1024,256]{1,0:T(8,128)(2,1)S(1)} %collective-permute-done.31.refs_3_) | copy-start | bytes 1572868
  170.5 2.3 collective-permute-start.38
  170.5 14.8 %copy-start.10 = (bf16[1024,256]{1,0:T(8,128)(2,1)}, bf16[1024,256]{1,0:T(8,128)(2,1)S(1)}, u32[]{:S(2)}) copy-start(bf16[1024,256]{1,0:T(8,128)(2,1)S(1)} %collective-permute-done.32.refs_6_) | copy-start | bytes 1572868
  170.5 14.7 %collective-permute-start.33 = (bf16[1024,256]{1,0:T(8,128)(2,1)S(1)}, bf16[1024,256]{1,0:T(8,128)(2,1)S(1)}, u32[]{:S(2)}, u32[]{:S(2)}) collective-permute-start(bf16[1024,256]{1,0:T(8,128)(2,1)S(1)} %collective-permute-done.31.refs_3_), channel_id=1, source_target_pairs={{8,0},{16,8},{24,16},{28,24},{20,28},{12,20},{4,12},{0,4},{9,1},{1... | collective-permute-start | bytes 1572872 | tf_op jit(solution)/shard_map/ppermute | solution.py:311
  171.6 13.6 %collective-permute-start.34 = (bf16[1024,256]{1,0:T(8,128)(2,1)S(1)}, bf16[1024,256]{1,0:T(8,128)(2,1)S(1)}, u32[]{:S(2)}, u32[]{:S(2)}) collective-permute-start(bf16[1024,256]{1,0:T(8,128)(2,1)S(1)} %collective-permute-done.32.refs_6_), channel_id=1, source_target_pairs={{0,8},{8,16},{16,24},{24,28},{28,20},{20,12},{12,4},{4,0},{1,9},{9... | collective-permute-start | bytes 1572872 | tf_op jit(solution)/shard_map/ppermute | solution.py:306
  186.2 16.6 %collective-permute-start.40 = (bf16[2,1024,256]{2,1,0:T(8,128)(2,1)S(1)}, bf16[2,1024,256]{2,1,0:T(8,128)(2,1)}, u32[]{:S(2)}, u32[]{:S(2)}) collective-permute-start(bf16[2,1024,256]{2,1,0:T(8,128)(2,1)S(1)} %collective-permute-done.35.refs_13_.refs_5_), channel_id=1, source_target_pairs={{0,1},{1,0},{2,3},{3,2},{4,5},{5,4},{6,7},{7,6},{8,9},{9,8},{10,11... | collective-permute-start | bytes 3145736 | tf_op jit(solution)/shard_map/ppermute | solution.py:320
  188.5 14.4 %collective-permute-start.39 = (bf16[1024,256]{1,0:T(8,128)(2,1)}, bf16[1024,256]{1,0:T(8,128)(2,1)}, u32[]{:S(2)}, u32[]{:S(2)}) collective-permute-start(bf16[1024,256]{1,0:T(8,128)(2,1)} %shard_map.150.refs_2_), channel_id=1, source_target_pairs={{0,2},{1,3},{2,0},{3,1},{4,6},{5,7},{6,4},{7,5},{8,10},{9,11},{10,... | collective-permute-start | bytes 1572872 | tf_op jit(solution)/shard_map/ppermute | solution.py:320
  202.9 11.0 %collective-permute-start.41 = (bf16[1024,256]{1,0:T(8,128)(2,1)S(1)}, bf16[1024,256]{1,0:T(8,128)(2,1)S(1)}, u32[]{:S(2)}, u32[]{:S(2)}) collective-permute-start(bf16[1024,256]{1,0:T(8,128)(2,1)S(1)} %copy-done.26), channel_id=1, source_target_pairs={{0,1},{1,0},{2,3},{3,2},{4,5},{5,4},{6,7},{7,6},{8,9},{9,8},{10,11... | collective-permute-start | bytes 1572872 | tf_op jit(solution)/shard_map/ppermute | solution.py:320
  202.9 11.0 %collective-permute-start.42 = (bf16[1024,256]{1,0:T(8,128)(2,1)}, bf16[1024,256]{1,0:T(8,128)(2,1)S(1)}, u32[]{:S(2)}, u32[]{:S(2)}) collective-permute-start(bf16[1024,256]{1,0:T(8,128)(2,1)} %get-tuple-element.156.refs_7_), channel_id=1, source_target_pairs={{0,1},{1,0},{2,3},{3,2},{4,5},{5,4},{6,7},{7,6},{8,9},{9,8},{10,11... | collective-permute-start | bytes 1572872 | tf_op jit(solution)/shard_map/ppermute | solution.py:320
  203.4 13.9 %collective-permute-start.43 = (bf16[1024,256]{1,0:T(8,128)(2,1)S(1)}, bf16[1024,256]{1,0:T(8,128)(2,1)S(1)}, u32[]{:S(2)}, u32[]{:S(2)}) collective-permute-start(bf16[1024,256]{1,0:T(8,128)(2,1)S(1)} %copy-done.25), channel_id=1, source_target_pairs={{0,2},{1,3},{2,0},{3,1},{4,6},{5,7},{6,4},{7,5},{8,10},{9,11},{10,... | collective-permute-start | bytes 1572872 | tf_op jit(solution)/shard_map/ppermute | solution.py:320
  204.6 12.7 %collective-permute-start.45 = (bf16[1024,256]{1,0:T(8,128)(2,1)}, bf16[1024,256]{1,0:T(8,128)(2,1)S(1)}, u32[]{:S(2)}, u32[]{:S(2)}) collective-permute-start(bf16[1024,256]{1,0:T(8,128)(2,1)} %collective-permute-done.39), channel_id=1, source_target_pairs={{0,1},{1,0},{2,3},{3,2},{4,5},{5,4},{6,7},{7,6},{8,9},{9,8},{10,11... | collective-permute-start | bytes 1572872 | tf_op jit(solution)/shard_map/ppermute | solution.py:320
  204.6 14.7 %collective-permute-start.44 = (bf16[1024,256]{1,0:T(8,128)(2,1)}, bf16[1024,256]{1,0:T(8,128)(2,1)}, u32[]{:S(2)}, u32[]{:S(2)}) collective-permute-start(bf16[1024,256]{1,0:T(8,128)(2,1)} %collective-permute-done.39), channel_id=1, source_target_pairs={{0,4},{4,0},{8,12},{12,8},{16,20},{20,16},{24,28},{28,24},{1,5},{5... | collective-permute-start | bytes 1572872 | tf_op jit(solution)/shard_map/ppermute | solution.py:316
  219.3 1.9 collective-permute-start.49
  219.3 14.3 %collective-permute-start.46 = (bf16[1024,256]{1,0:T(8,128)(2,1)S(1)}, bf16[1024,256]{1,0:T(8,128)(2,1)S(1)}, u32[]{:S(2)}, u32[]{:S(2)}) collective-permute-start(bf16[1024,256]{1,0:T(8,128)(2,1)S(1)} %collective-permute-done.43.refs_4_.refs_12_), channel_id=1, source_target_pairs={{0,4},{4,0},{8,12},{12,8},{16,20},{20,16},{24,28},{28,24},{1,5},{5... | collective-permute-start | bytes 1572872 | tf_op jit(solution)/shard_map/ppermute | solution.py:316
  219.5 14.1 %collective-permute-start.47 = (bf16[1024,256]{1,0:T(8,128)(2,1)}, bf16[1024,256]{1,0:T(8,128)(2,1)}, u32[]{:S(2)}, u32[]{:S(2)}) collective-permute-start(bf16[1024,256]{1,0:T(8,128)(2,1)} %collective-permute-done.44), channel_id=1, source_target_pairs={{0,1},{1,0},{2,3},{3,2},{4,5},{5,4},{6,7},{7,6},{8,9},{9,8},{10,11... | collective-permute-start | bytes 1572872 | tf_op jit(solution)/shard_map/ppermute | solution.py:320
  219.8 14.2 %collective-permute-start.48 = (bf16[2,512,256]{2,1,0:T(8,128)(2,1)S(1)}, bf16[2,512,256]{2,1,0:T(8,128)(2,1)}, u32[]{:S(2)}, u32[]{:S(2)}) collective-permute-start(bf16[2,512,256]{2,1,0:T(8,128)(2,1)S(1)} %copy-done.17), channel_id=1, source_target_pairs={{0,2},{1,3},{2,0},{3,1},{4,6},{5,7},{6,4},{7,5},{8,10},{9,11},{10,... | collective-permute-start | bytes 1572872 | tf_op jit(solution)/shard_map/ppermute | solution.py:320
  236.9 8.9 %collective-permute-start.52 = (bf16[2,512,256]{2,1,0:T(8,128)(2,1)}, bf16[2,512,256]{2,1,0:T(8,128)(2,1)}, u32[]{:S(2)}, u32[]{:S(2)}) collective-permute-start(bf16[2,512,256]{2,1,0:T(8,128)(2,1)} %shard_map.154.refs_10_), channel_id=1, source_target_pairs={{0,1},{1,0},{2,3},{3,2},{4,5},{5,4},{6,7},{7,6},{8,9},{9,8},{10,11... | collective-permute-start | bytes 1572872 | tf_op jit(solution)/shard_map/ppermute | solution.py:320
  237.0 8.9 %collective-permute-start.51 = (bf16[2,512,256]{2,1,0:T(8,128)(2,1)}, bf16[2,512,256]{2,1,0:T(8,128)(2,1)}, u32[]{:S(2)}, u32[]{:S(2)}) collective-permute-start(bf16[2,512,256]{2,1,0:T(8,128)(2,1)} %collective-permute-done.48.refs_8_), channel_id=1, source_target_pairs={{0,1},{1,0},{2,3},{3,2},{4,5},{5,4},{6,7},{7,6},{8,9},{9,8},{10,11... | collective-permute-start | bytes 1572872 | tf_op jit(solution)/shard_map/ppermute | solution.py:320
  237.5 14.8 %collective-permute-start.50 = (bf16[2,512,256]{2,1,0:T(8,128)(2,1)}, bf16[2,512,256]{2,1,0:T(8,128)(2,1)S(1)}, u32[]{:S(2)}, u32[]{:S(2)}) collective-permute-start(bf16[2,512,256]{2,1,0:T(8,128)(2,1)} %shard_map.154.refs_10_), channel_id=1, source_target_pairs={{0,2},{1,3},{2,0},{3,1},{4,6},{5,7},{6,4},{7,5},{8,10},{9,11},{10,... | collective-permute-start | bytes 1572872 | tf_op jit(solution)/shard_map/ppermute | solution.py:320
  252.4 4.2 %collective-permute-start.53 = (bf16[2,512,256]{2,1,0:T(8,128)(2,1)S(1)}, bf16[2,512,256]{2,1,0:T(8,128)(2,1)S(1)}, u32[]{:S(2)}, u32[]{:S(2)}) collective-permute-start(bf16[2,512,256]{2,1,0:T(8,128)(2,1)S(1)} %collective-permute-done.50.refs_4_), channel_id=1, source_target_pairs={{0,1},{1,0},{2,3},{3,2},{4,5},{5,4},{6,7},{7,6},{8,9},{9,8},{10,11... | collective-permute-start | bytes 1572872 | tf_op jit(solution)/shard_map/ppermute | solution.py:320
  (22 other events, 122.1 us)
